TPU v7x, 256 devices: a whole 4x4x8 slice. The times are simulated.
256 devices in a mesh: blk: 32 (over x, z), kv: 8 (over y, core).
Axes of the slice: x: 4, y: 4, z: 8, core: 2. Of those that a mesh axis runs over, the one named last changes fastest.
Arguments:
- context: bfloat16 [16384, 4096], P('blk'), may hold values from -6 to 6
- question: bfloat16 [256, 4096], P('blk'), may hold values from -6 to 6
- norm_gain: float32 [4096], replicated, may hold values from 0.1 to 1.9
- w_query: bfloat16 [4096, 4096], P(None, 'kv')
- w_key: bfloat16 [4096, 1024], P(None, 'kv'), as said below
- w_value: bfloat16 [4096, 1024], P(None, 'kv'), may hold values from -0.09375 to 0.09375
- w_out: bfloat16 [4096, 4096], P('kv'), may hold values from -0.375 to 0.375
- block_len: int32 [32], replicated, may hold values from 1 to 512, as said below
- question_len: int32 [1], replicated, may hold values from 64 to 256
Outputs:
- context_out: bfloat16 [16384, 4096], P('blk', 'kv')
- question_out: bfloat16 [256, 4096], P('blk', 'kv')
Inputs may be any that keep to these rules, and one draw needn't show every extreme that they name: `block_len`: every block holds 512 live tokens except the last, which holds 1 to 511. `w_key`: entries are those of a fan-in scaled projection.
All inputs are finite; a program needn't handle non-finite values.
Results may differ from a plain program's by a relative error of at most 0.022.
Values may be sent and summed in bfloat16 or wider, within the bound.
No kernel may reach another device: no remote copies, remote signals or barrier semaphores. Data moves between devices by JAX's collectives and lax.ppermute only.
A program may use at most 128 MiB of HBM per device.

v0:
```python
import jax
import jax.numpy as jnp
from jax import lax
from jax.sharding import PartitionSpec as P

HD = 128


epsilon = 1e-05
rope_base = 500000.0
masked_score = -1e30


def from_root(value, axis, root):
    mine = lax.axis_index(axis) == root
    return lax.psum(jnp.where(mine, value, jnp.zeros_like(value)), axis)


def combined_all(value, axis, combine):
    everything = jax.tree.map(lambda part: lax.all_gather(part, axis), value)
    initial = jax.tree.map(lambda part: part[0], everything)

    def turn(k, so_far):
        return combine(so_far, jax.tree.map(lambda part: part[k], everything))

    return lax.fori_loop(1, lax.axis_size(axis), turn, initial)


def normalize(rows_in, gain_full):
    values = rows_in.astype(jnp.float32)
    factor = lax.rsqrt(jnp.mean(values * values, axis=-1, keepdims=True) + epsilon)
    return (values * factor * gain_full).astype(jnp.bfloat16)


def rotate(heads_in, positions):
    head_width = heads_in.shape[-1]
    half_width = head_width // 2
    inverse_freq = rope_base ** (-2.0 * jnp.arange(half_width, dtype=jnp.float32) / head_width)
    angles = positions.astype(jnp.float32)[:, None] * inverse_freq[None, :]
    cosine = jnp.cos(angles)[:, None, :]
    sine_part = jnp.sin(angles)[:, None, :]
    former = heads_in[..., :half_width]
    latter = heads_in[..., half_width:]
    return jnp.concatenate(
        [former * cosine - latter * sine_part, latter * cosine + former * sine_part], axis=-1
    )


def project(normed, weight, positions):
    product = jnp.dot(normed, weight, preferred_element_type=jnp.float32)
    row_count = product.shape[0]
    heads_in = product.reshape(row_count, -1, HD)
    if positions is not None:
        heads_in = rotate(heads_in, positions)
    return heads_in.reshape(row_count, -1).astype(jnp.bfloat16)


def local_attention(queries, key_rows, value_rows, allowed):
    row_count = queries.shape[0]
    key_count = key_rows.shape[0]
    kv_heads = key_rows.shape[1] // HD
    query_heads = queries.shape[1] // HD
    shaped_query = queries.reshape(row_count, kv_heads, query_heads // kv_heads, HD)
    shaped_key = key_rows.reshape(key_count, kv_heads, HD)
    shaped_value = value_rows.reshape(key_count, kv_heads, HD)
    scores = jnp.einsum(
        "rkgh,skh->kgrs", shaped_query, shaped_key, preferred_element_type=jnp.float32
    ) * HD ** (-0.5)
    masked = jnp.where(allowed, scores, masked_score)
    highest = jnp.max(masked, axis=-1)
    weights = jnp.where(allowed, jnp.exp(masked - highest[..., None]), 0.0)
    totals = jnp.sum(weights, axis=-1)
    mixture = jnp.einsum(
        "kgrs,skh->rkgh",
        weights.astype(jnp.bfloat16),
        shaped_value,
        preferred_element_type=jnp.float32,
    )
    highest_rows = jnp.transpose(highest, (2, 0, 1)).reshape(row_count, query_heads)
    total_rows = jnp.transpose(totals, (2, 0, 1)).reshape(row_count, query_heads)
    return (highest_rows, total_rows, mixture.reshape(row_count, query_heads, HD))


def merge_parts(first_set, second_set):
    highest_a, totals_a, mixture_a = first_set
    highest_b, totals_b, mixture_b = second_set
    highest = jnp.maximum(highest_a, highest_b)
    factor_a = jnp.exp(highest_a - highest)
    factor_b = jnp.exp(highest_b - highest)
    return (
        highest,
        totals_a * factor_a + totals_b * factor_b,
        mixture_a * factor_a[..., None] + mixture_b * factor_b[..., None],
    )


def finish(totals, mixture, row_valid):
    result = mixture / totals[..., None]
    result = jnp.where(row_valid[:, None, None], result, 0.0)
    return result.reshape(result.shape[0], -1).astype(jnp.bfloat16)


def body(context, question, norm_gain, w_query, w_key, w_value, w_out, block_len, question_len):
    block_rows = context.shape[0]
    question_rows = question.shape[0]
    block_count = lax.axis_size("blk")
    blk_index = lax.axis_index("blk")
    block_ids = jnp.arange(block_len.shape[0], dtype=jnp.int32)
    own_length = jnp.sum(jnp.where(block_ids == blk_index, block_len, 0))
    total_ctx = jnp.sum(block_len)
    live_questions = question_len[0]
    token_ids = jnp.arange(block_rows, dtype=jnp.int32)
    ctx_positions = blk_index * block_rows + token_ids
    own_questions = blk_index * question_rows + jnp.arange(question_rows, dtype=jnp.int32)
    all_positions = jnp.concatenate([ctx_positions, total_ctx + own_questions], 0)
    all_normed = jnp.concatenate([normalize(context, norm_gain), normalize(question, norm_gain)], 0)
    all_query = project(all_normed, w_query, all_positions)
    all_key = project(all_normed, w_key, all_positions)
    all_value = project(all_normed, w_value, None)
    anchor_key, anchor_value = (
        from_root(all_key[:block_rows], "blk", 0),
        from_root(all_value[:block_rows], "blk", 0),
    )
    key_rows = jnp.concatenate([anchor_key, all_key[:block_rows]], 0)
    value_rows = jnp.concatenate([anchor_value, all_value[:block_rows]], 0)
    ctx_allowed = jnp.concatenate(
        [
            jnp.broadcast_to(blk_index > 0, (block_rows, block_rows)),
            token_ids[None, :] <= token_ids[:, None],
        ],
        1,
    )
    ctx_parts = local_attention(all_query[:block_rows], key_rows, value_rows, ctx_allowed)
    ctx_attn = finish(ctx_parts[1], ctx_parts[2], token_ids < own_length)
    question_query = all_query[block_rows:]
    question_ids = jnp.arange(question_rows * block_count, dtype=jnp.int32)
    que_allowed = jnp.concatenate(
        [
            jnp.broadcast_to(
                (token_ids < own_length)[None, :], (question_ids.shape[0], block_rows)
            ),
            own_questions[None, :] <= question_ids[:, None],
        ],
        1,
    )
    first_question = blk_index * question_rows
    gathered = lax.all_gather(question_query, "blk", axis=0, tiled=True)
    highest_all, totals_all, mixture_all = local_attention(
        gathered, all_key, all_value, que_allowed
    )
    merged = combined_all((highest_all, totals_all, mixture_all), "blk", merge_parts)
    totals = lax.dynamic_slice_in_dim(merged[1], first_question, question_rows, 0)
    mixture = lax.dynamic_slice_in_dim(merged[2], first_question, question_rows, 0)
    que_attn = finish(totals, mixture, own_questions < live_questions)
    attended = jnp.concatenate([ctx_attn, que_attn], 0)
    term_rows = jnp.dot(attended, w_out, preferred_element_type=jnp.float32)
    projected = lax.psum_scatter(
        term_rows.astype(jnp.bfloat16), "kv", scatter_dimension=1, tiled=True
    )
    return (projected[:block_rows], projected[block_rows:])


def solution(mesh):
    return jax.shard_map(
        body,
        mesh=mesh,
        in_specs=(
            P("blk", None),
            P("blk", None),
            P(),
            P(None, "kv"),
            P(None, "kv"),
            P(None, "kv"),
            P("kv", None),
            P(),
            P(),
        ),
        out_specs=(P("blk", "kv"), P("blk", "kv")),
        check_vma=False,
    )
```

profile of v0, /device:TPU:32, one launch (start us, length us, event | category | flops | bytes accessed | tf_op | source)
XLA Modules:
  0.0 488.0 jit_solution(1444360102800675019)
XLA Ops:
  9.8 3.1 fusion.3
  13.0 3.6 fusion.5
  16.6 3.6 fusion.19
  27.0 6.8 %fusion.16 = f32[520,512]{1,0:T(8,128)} fusion(bf16[4096,512]{1,0:T(8,128)(2,1)} %param.14, bf16[8,4096]{1,0:T(8,128)(2,1)S(1)} %fusion.54, bf16[512,4096]{1,0:T(8,128)(2,1)} %fusion.5), kind=kOutput, calls=%fused_computation.29 | convolution fusion | flops 2189557760 | bytes 9519104 | tf_op jit(solution)/shard_map/dot_general | solution.py:50
  37.3 51.3 %all_gather.12 = bf16[256,512]{1,0:T(8,128)(2,1)S(1)} all-gather(bf16[8,512]{1,0:T(8,128)(2,1)S(1)} %fusion.56), channel_id=1, replica_groups=mesh['blk'=32,'kv'=8] {'blk'}, dimensions={0}, use_global_device_ids=true | all-gather | bytes 270336 | tf_op jit(solution)/shard_map/all_gather | solution.py:147
  93.8 40.9 %all-gather = f32[8192,1,4]{0,2,1:T(4,128)S(1)} all-gather(f32[256,1,4]{0,2,1:T(4,128)S(1)} %bitcast.132), channel_id=2, replica_groups=mesh['blk'=32,'kv'=8] {'blk'}, dimensions={0}, use_global_device_ids=true | all-gather | bytes 135168 | tf_op jit(solution)/shard_map/all_gather | solution.py:20
  135.3 42.3 %all-gather.1 = f32[8192,1,4]{0,2,1:T(4,128)S(1)} all-gather(f32[256,1,4]{0,2,1:T(4,128)S(1)} %bitcast.134), channel_id=3, replica_groups=mesh['blk'=32,'kv'=8] {'blk'}, dimensions={0}, use_global_device_ids=true | all-gather | bytes 135168 | tf_op jit(solution)/shard_map/all_gather | solution.py:20
  177.7 3.2 fusion.6
  185.5 137.0 %all-gather.5.cloned.1.call-done = f32[8192,1,4,128]{0,3,2,1:T(8,128)} async-done(((f32[256,1,4,128]{0,3,2,1:T(8,128)}), f32[8192,1,4,128]{0,3,2,1:T(8,128)}) %all-gather.5.cloned.1.call-update) | async-done | bytes 16777232 | tf_op jit(solution)/shard_map/all_gather | solution.py:20
  323.8 19.2 %copy.48 = f32[8192,1,4,128]{3,2,0,1:T(4,128)} copy(f32[8192,1,4,128]{0,3,2,1:T(8,128)} %all-gather.5.cloned.1.call-done) | data formatting | bytes 33554432 | tf_op jit(solution)/shard_map/while | solution.py:26
  343.0 90.2 %while.19 = (s32[]{:T(128)}, f32[256,4]{0,1:T(4,128)S(1)}, f32[256,4]{0,1:T(4,128)S(1)}, f32[256,4,128]{2,1,0:T(4,128)S(1)}, f32[32,256,4]{1,2,0:T(4,128)S(1)}, ...) while((s32[]{:T(128)}, f32[256,4]{0,1:T(4,128)S(1)}, ...), condition=%wide.region_11.12_spmd, body=%wide.region_10.11_spmd.sunk | while | flops 399365 | bytes 1630359 | solution.py:26
  343.3 2.6 fusion.83
  346.2 2.6 fusion.83
  363.7 2.6 fusion.83
  366.6 2.6 fusion.83
  369.5 2.6 fusion.83
  372.4 2.6 fusion.83
  375.3 2.6 fusion.83
  378.3 2.6 fusion.83
  381.2 2.6 fusion.83
  384.1 2.6 fusion.83
  387.0 2.6 fusion.83
  389.9 2.6 fusion.83
  392.8 2.6 fusion.83
  395.7 2.6 fusion.83
  398.6 2.6 fusion.83
  401.6 2.6 fusion.83
  419.0 2.6 fusion.83
  421.9 2.6 fusion.83
  424.8 2.6 fusion.83
  433.7 6.7 %convolution_convert_fusion = bf16[520,4096]{1,0:T(8,128)(2,1)} fusion(bf16[512,4096]{1,0:T(8,128)(2,1)} %param.17, bf16[8,512]{0,1:T(8,128)(2,1)S(1)} %bitcast.129, bf16[512,512]{0,1:T(8,128)(2,1)S(1)} %fusion.29), kind=kOutput, calls=%fused_computation.16 | convolution fusion | flops 2184232960 | bytes 8986624 | tf_op jit(solution)/shard_map/dot_general | solution.py:156
  440.4 37.9 %reduce-scatter.2.cloned.1.call-done = bf16[520,512]{1,0:T(8,128)(2,1)} async-done(((bf16[520,4096]{1,0:T(8,128)(2,1)}), bf16[520,512]{1,0:T(8,128)(2,1)}) %reduce-scatter.2.cloned.1.call-update) | async-done | bytes 532496 | tf_op jit(solution)/shard_map/reduce_scatter | solution.py:157
  (181 shorter events, 67.6 us)
Async XLA Ops:
  7.2 9.4 %copy-start = (bf16[4096,128]{1,0:T(8,128)(2,1)S(1)}, bf16[4096,128]{1,0:T(8,128)(2,1)}, u32[]{:S(2)}) copy-start(bf16[4096,128]{1,0:T(8,128)(2,1)} %param.15) | copy-start | bytes 3145732
  7.2 5.7 %copy-start.6 = (bf16[8,4096]{1,0:T(8,128)(2,1)S(1)}, bf16[8,4096]{1,0:T(8,128)(2,1)}, u32[]{:S(2)}) copy-start(bf16[8,4096]{1,0:T(8,128)(2,1)} %param.12) | copy-start | bytes 196612
  7.2 5.7 %copy-start.10 = (f32[4096]{0:T(1024)S(1)}, f32[4096]{0:T(1024)}, u32[]{:S(2)}) copy-start(f32[4096]{0:T(1024)} %param.13) | copy-start | bytes 49156
  7.2 170.4 %all-reduce.4.cloned.1.call-start = ((), (), s32[]{:S(2)}) async-start(), calls=%async_computation.3 | async-start | bytes 524288 | tf_op jit(solution)/shard_map/psum | solution.py:16
  7.3 5.7 %copy-start.2 = (bf16[512,4096]{1,0:T(8,128)(2,1)S(1)}, bf16[512,4096]{1,0:T(8,128)(2,1)}, u32[]{:S(2)}) copy-start(bf16[512,4096]{1,0:T(8,128)(2,1)} %param.11) | copy-start | bytes 12582916
  16.6 3.6 copy-start.3
  16.6 3.7 copy-start.11
  21.7 12.2 %copy-start.9 = (bf16[520,128]{1,0:T(8,128)(2,1)}, bf16[520,128]{1,0:T(8,128)(2,1)S(1)}, u32[]{:S(2)}) copy-start(bf16[520,128]{1,0:T(8,128)(2,1)S(1)} %fusion.20) | copy-start | bytes 399364
  25.2 297.3 %all-gather.5.cloned.1.call-start = ((), (), s32[]{:S(2)}) async-start(), calls=%async_computation.2 | async-start | bytes 17301504 | tf_op jit(solution)/shard_map/all_gather | solution.py:20
  36.4 0.8 copy-start.4
  89.4 88.2 %copy-start.7 = (bf16[512,128]{1,0:T(8,128)(2,1)S(1)}, bf16[512,128]{1,0:T(8,128)(2,1)}, u32[]{:S(2)}) copy-start(bf16[512,128]{1,0:T(8,128)(2,1)} %get-tuple-element.225) | copy-start | bytes 393220
  92.0 386.3 %reduce-scatter.2.cloned.1.call-start = ((), (), s32[]{:S(2)}) async-start(), calls=%async_computation.1 | async-start | bytes 4792320 | tf_op jit(solution)/shard_map/reduce_scatter | solution.py:157
  177.6 3.2 copy-start.5
  177.6 3.2 copy-start.8
  177.7 3.2 copy-start.12
  433.7 47.8 %copy-start.1 = (bf16[4096,128]{1,0:T(8,128)(2,1)S(1)}, bf16[4096,128]{1,0:T(8,128)(2,1)}, u32[]{:S(2)}) copy-start(bf16[4096,128]{1,0:T(8,128)(2,1)} %param.15) | copy-start | bytes 3145732
Sparse Core Ops, SparseCore 0:
  25.4 145.8 all-reduce.3
  174.2 148.2 all-gather.4
  440.5 37.7 reduce-scatter.1
where the time goes:
time: 491 us; the launch traced here: 488 us
  waiting for transfers between devices  175 us (36%)
  blocking collectives  135 us (27%)
  other arithmetic  98.6 us (20%)
  local copies, waits for them, and re-layouts  36.6 us (7%)
  matrix products  27.1 us (6%)
  between operations  14.8 us (3%)
    all_gather x1, waiting for transfers between devices, combined_all(): everything = jax.tree.map(lambda part: lax.all_gather(part, axis), value)  137 us
    all_gather x2, blocking collectives, combined_all(): everything = jax.tree.map(lambda part: lax.all_gather(part, axis), value)  83.2 us
    add x31, other arithmetic, merge_parts(): mixture_a * factor_a[..., None] + mixture_b * factor_b[..., None]  79.9 us
    all_gather x1, blocking collectives, body(): gathered = lax.all_gather(question_query, 'blk', axis=0, tiled=True)  51.3 us
    reduce_scatter x1, waiting for transfers between devices, body(): lax.psum_scatter(term_rows.astype(jnp.bfloat16), 'kv', scatter_dimension=...  37.9 us
    while x2, local copies, waits for them, and re-layouts, combined_all(): return lax.fori_loop(1, lax.axis_size(axis), turn, initial)  19.4 us
    dot_general x3, matrix products, project(): product = jnp.dot(normed, weight, preferred_element_type=jnp.float32)  11.8 us
  transfers between devices with their start and end apart: 3, of which 2 were waited for; matrix products, arithmetic and copies ran while one was open for 5% of the time, Pallas kernels for 0%

commit v1 on v0

v1 whole, which is shorter than its diff:
```python
import functools

import jax
import jax.numpy as jnp
import numpy as np
from jax import lax
from jax.experimental import pallas as pl
from jax.experimental.pallas import tpu as pltpu
from jax.sharding import PartitionSpec as P

HD = 128
HEADS = 4
BLK = 512
QROWS = 8
NX, NZ, NY, NC = 4, 8, 4, 2
N_BLK, N_KV = NX * NZ, NY * NC
QN = N_BLK * QROWS
D = 4096
FEAT = D // N_KV
KC = 512
ROWS = 256

epsilon = 1e-05
rope_base = 500000.0
masked_score = -1e30
q_scale = float(HD**-0.5 * np.log2(np.e))
log2_e = float(np.log2(np.e))

bf16 = jnp.bfloat16
f32 = jnp.float32


def angle_tables(positions):
    inverse_freq = rope_base ** (-2.0 * np.arange(HD // 2, dtype=np.float64) / HD)
    angles = np.asarray(positions, np.float64)[:, None] * inverse_freq[None, :]
    angles = np.concatenate([angles, angles], 1)
    return np.cos(angles).astype(np.float32), np.sin(angles).astype(np.float32)


def params(semantics=1, limit=40):
    return pltpu.CompilerParams(
        dimension_semantics=("arbitrary",) * semantics, vmem_limit_bytes=limit * 2**20
    )


def cost(flops, bytes_accessed, transcendentals=0):
    return pl.CostEstimate(
        flops=flops, bytes_accessed=bytes_accessed, transcendentals=transcendentals
    )


def add_angles(first, second):
    return (
        first[0] * second[0] - first[1] * second[1],
        first[1] * second[0] + first[0] * second[1],
    )


def rotated(head, cosine, sine_signed):
    return head * cosine + pltpu.roll(head, HD // 2, 1) * sine_signed


def signed(sine):
    lane = lax.broadcasted_iota(jnp.int32, sine.shape, 1)
    return jnp.where(lane < HD // 2, -sine, sine)


def dot(a, b):
    return jnp.dot(a, b, preferred_element_type=f32)


def dot_t(a, b):
    return lax.dot_general(a, b, (((1,), (1,)), ((), ())), preferred_element_type=f32)


def lane_folded(values):
    total = values[:, :HD]
    for part in range(1, values.shape[1] // HD):
        total = total + values[:, part * HD : (part + 1) * HD]
    return total


def squares_to_factor(squares):
    mean = jnp.sum(squares, axis=-1, keepdims=True) * (1.0 / D)
    return lax.rsqrt(mean + epsilon)


def question_kernel(
    len_ref, where_ref, x_ref, gain_ref, wq_ref, wk_ref, wv_ref, ct_ref, st_ref, cb_ref, sb_ref,
    q_ref, kv_ref, acc_ref, sq_ref,
):
    step = pl.program_id(0)

    @pl.when(step == 0)
    def _():
        acc_ref[...] = jnp.zeros_like(acc_ref)
        sq_ref[...] = jnp.zeros_like(sq_ref)

    x = x_ref[...].astype(f32)
    sq_ref[...] += lane_folded(x * x)
    scaled = (x * gain_ref[...]).astype(bf16)
    acc_ref[:, : HEADS * HD] += dot(scaled, wq_ref[...])
    acc_ref[:, HEADS * HD : (HEADS + 1) * HD] += dot(scaled, wk_ref[...])
    acc_ref[:, (HEADS + 1) * HD :] += dot(scaled, wv_ref[...])

    @pl.when(step == pl.num_programs(0) - 1)
    def _():
        factor = squares_to_factor(sq_ref[...])
        total = len_ref[0]
        for b in range(1, N_BLK):
            total = total + len_ref[b]
        high, low = total // BLK, lax.rem(total, BLK)
        base = add_angles(
            (cb_ref[pl.ds(high, 1), :], sb_ref[pl.ds(high, 1), :]),
            (ct_ref[pl.ds(low, 1), :], st_ref[pl.ds(low, 1), :]),
        )
        rows = pl.ds(pl.multiple_of(where_ref[0] * QROWS, QROWS), QROWS)
        cosine, sine = add_angles((ct_ref[rows, :], st_ref[rows, :]), base)
        sine = signed(sine)
        for h in range(HEADS + 1):
            head = acc_ref[:, h * HD : (h + 1) * HD] * factor
            head = rotated(head, cosine, sine)
            if h < HEADS:
                q_ref[:, h * HD : (h + 1) * HD] = (head * q_scale).astype(bf16)
            else:
                kv_ref[:, :HD] = head.astype(bf16)
        kv_ref[:, HD:] = (acc_ref[:, (HEADS + 1) * HD :] * factor).astype(bf16)


def whole(shape):
    return pl.BlockSpec(shape, lambda *_: (0,) * len(shape))


smem = pl.BlockSpec(memory_space=pltpu.SMEM)


def question_projection(block_len, where, question, gain, wq, wk, wv, tables):
    return pl.pallas_call(
        question_kernel,
        grid=(D // KC,),
        in_specs=[
            smem,
            smem,
            pl.BlockSpec((QROWS, KC), lambda k: (0, k)),
            pl.BlockSpec((1, KC), lambda k: (0, k)),
            pl.BlockSpec((KC, HEADS * HD), lambda k: (k, 0)),
            pl.BlockSpec((KC, HD), lambda k: (k, 0)),
            pl.BlockSpec((KC, HD), lambda k: (k, 0)),
            whole((BLK, HD)),
            whole((BLK, HD)),
            whole((N_BLK + 1, HD)),
            whole((N_BLK + 1, HD)),
        ],
        out_specs=[whole((QROWS, HEADS * HD)), whole((QROWS, 2 * HD))],
        out_shape=[
            jax.ShapeDtypeStruct((QROWS, HEADS * HD), bf16),
            jax.ShapeDtypeStruct((QROWS, 2 * HD), bf16),
        ],
        scratch_shapes=[
            pltpu.VMEM((QROWS, (HEADS + 2) * HD), f32),
            pltpu.VMEM((QROWS, HD), f32),
        ],
        compiler_params=params(),
        cost_estimate=cost(2 * QROWS * D * 768 * 32, D * 768 * 2),
        name="question_projection",
    )(block_len, where, question, gain, wq, wk, wv, *tables)


def kv_kernel(
    where_ref, x_ref, gain_ref, wk_ref, wv_ref, ct_ref, st_ref, cb_ref, sb_ref,
    kv_ref, factor_ref, acc_ref, sq_ref,
):
    step = pl.program_id(0)

    @pl.when(step == 0)
    def _():
        acc_ref[...] = jnp.zeros_like(acc_ref)
        sq_ref[...] = jnp.zeros_like(sq_ref)

    x = x_ref[...].astype(f32)
    sq_ref[...] += lane_folded(x * x)
    scaled = (x * gain_ref[...]).astype(bf16)
    weights = jnp.concatenate([wk_ref[...], wv_ref[...]], axis=1)
    acc_ref[...] += dot(scaled, weights)

    @pl.when(step == pl.num_programs(0) - 1)
    def _():
        factor = squares_to_factor(sq_ref[...])
        block = pl.ds(where_ref[0], 1)
        cosine, sine = add_angles(
            (ct_ref[...], st_ref[...]), (cb_ref[block, :], sb_ref[block, :])
        )
        head = rotated(acc_ref[:, :HD] * factor, cosine, signed(sine))
        kv_ref[:, :HD] = head.astype(bf16)
        kv_ref[:, HD:] = (acc_ref[:, HD:] * factor).astype(bf16)
        factor_ref[...] = jnp.broadcast_to(factor, factor_ref.shape)


def kv_projection(where, context, gain, wk, wv, tables):
    return pl.pallas_call(
        kv_kernel,
        grid=(D // KC,),
        in_specs=[
            smem,
            pl.BlockSpec((BLK, KC), lambda k: (0, k)),
            pl.BlockSpec((1, KC), lambda k: (0, k)),
            pl.BlockSpec((KC, HD), lambda k: (k, 0)),
            pl.BlockSpec((KC, HD), lambda k: (k, 0)),
            whole((BLK, HD)),
            whole((BLK, HD)),
            whole((N_BLK + 1, HD)),
            whole((N_BLK + 1, HD)),
        ],
        out_specs=[whole((BLK, 2 * HD)), whole((BLK, HD))],
        out_shape=[
            jax.ShapeDtypeStruct((BLK, 2 * HD), bf16),
            jax.ShapeDtypeStruct((BLK, HD), f32),
        ],
        scratch_shapes=[pltpu.VMEM((BLK, 2 * HD), f32), pltpu.VMEM((BLK, HD), f32)],
        compiler_params=params(),
        cost_estimate=cost(2 * BLK * D * 256 * 3, D * 256 * 2 + BLK * D * 2),
        name="kv_projection",
    )(where, context, gain, wk, wv, *tables)


def query_kernel(
    where_ref, x_ref, gain_ref, wq_ref, factor_ref, ct_ref, st_ref, cb_ref, sb_ref,
    q_ref, acc_ref,
):
    step = pl.program_id(0)

    @pl.when(step == 0)
    def _():
        acc_ref[...] = jnp.zeros_like(acc_ref)

    scaled = (x_ref[...].astype(f32) * gain_ref[...]).astype(bf16)
    acc_ref[...] += dot(scaled, wq_ref[...])

    @pl.when(step == pl.num_programs(0) - 1)
    def _():
        block = pl.ds(where_ref[0], 1)
        cosine, sine = add_angles(
            (ct_ref[...], st_ref[...]), (cb_ref[block, :], sb_ref[block, :])
        )
        scale = factor_ref[...] * q_scale
        cosine, sine = cosine * scale, signed(sine) * scale
        for h in range(HEADS):
            head = acc_ref[:, h * HD : (h + 1) * HD]
            q_ref[h] = rotated(head, cosine, sine).astype(bf16)


def query_projection(where, context, gain, wq, factor, tables):
    return pl.pallas_call(
        query_kernel,
        grid=(D // KC,),
        in_specs=[
            smem,
            pl.BlockSpec((BLK, KC), lambda k: (0, k)),
            pl.BlockSpec((1, KC), lambda k: (0, k)),
            pl.BlockSpec((KC, HEADS * HD), lambda k: (k, 0)),
            whole((BLK, HD)),
            whole((BLK, HD)),
            whole((BLK, HD)),
            whole((N_BLK + 1, HD)),
            whole((N_BLK + 1, HD)),
        ],
        out_specs=whole((HEADS, BLK, HD)),
        out_shape=jax.ShapeDtypeStruct((HEADS, BLK, HD), bf16),
        scratch_shapes=[pltpu.VMEM((BLK, HEADS * HD), f32)],
        compiler_params=params(),
        cost_estimate=cost(2 * BLK * D * 512, D * 512 * 2 + BLK * D * 2),
        name="query_projection",
    )(where, context, gain, wq, factor, *tables)


def with_ones(values):
    return jnp.concatenate([values, jnp.ones_like(values)], axis=1)


def own_kernel(q_ref, kv_ref, o_ref, lse_ref):
    row = lax.broadcasted_iota(jnp.int32, (ROWS, ROWS), 0)
    column = lax.broadcasted_iota(jnp.int32, (ROWS, ROWS), 1)
    causal = column <= row
    for h in range(HEADS):
        for r in range(BLK // ROWS):
            rows = slice(r * ROWS, (r + 1) * ROWS)
            q = q_ref[h, rows, :]
            diagonal = dot_t(q, kv_ref[rows, :HD])
            diagonal = jnp.where(causal, diagonal, masked_score)
            highest = jnp.max(diagonal, axis=-1, keepdims=True)
            if r:
                earlier = dot_t(q, kv_ref[: r * ROWS, :HD])
                highest = jnp.maximum(highest, jnp.max(earlier, axis=-1, keepdims=True))
            weights = jnp.exp2(diagonal - highest).astype(bf16)
            mixture = dot(weights, with_ones(kv_ref[rows, HD:]))
            if r:
                weights = jnp.exp2(earlier - highest).astype(bf16)
                mixture = mixture + dot(weights, with_ones(kv_ref[: r * ROWS, HD:]))
            totals = mixture[:, HD:]
            o_ref[h, rows, :] = mixture[:, :HD] / totals
            lse_ref[h, rows, :] = highest + jnp.log(totals) * log2_e


def own_attention(q, kv):
    return pl.pallas_call(
        own_kernel,
        out_shape=[jax.ShapeDtypeStruct((HEADS, BLK, HD), f32)] * 2,
        in_specs=[pl.BlockSpec(memory_space=pltpu.VMEM)] * 2,
        out_specs=[pl.BlockSpec(memory_space=pltpu.VMEM)] * 2,
        compiler_params=pltpu.CompilerParams(vmem_limit_bytes=40 * 2**20),
        cost_estimate=cost(HEADS * BLK * BLK * HD * 8, 3 * 2**20, HEADS * BLK * BLK),
        name="own_attention",
    )(q, kv)


def gathered_source(group, x_at, z_at):
    dx = group % 4
    dz = (group // 4) % 4
    dz = jnp.where(dz == 3, -1, dz) + 4 * (group // 16)
    return ((x_at - dx + NX) % NX) * NZ + (z_at - dz + 2 * NZ) % NZ


def question_attention_kernel(len_ref, where_ref, qa_ref, qb_ref, kv_ref, own_ref, out_ref, buf_ref):
    blk_at = where_ref[0]
    x_at, z_at = blk_at // NZ, lax.rem(blk_at, NZ)
    live = lax.broadcasted_iota(jnp.int32, (QN, BLK), 1) < len_ref[blk_at]
    group = lax.broadcasted_iota(jnp.int32, (QN, HD), 0)
    question_id = gathered_source(group // QROWS, x_at, z_at) * QROWS + group % QROWS
    key_id = lax.broadcasted_iota(jnp.int32, (QN, HD), 1)
    seen = (key_id < QROWS) & (key_id + blk_at * QROWS <= question_id)
    own = jnp.concatenate([own_ref[...].astype(f32), jnp.zeros((HD - QROWS, 2 * HD), f32)], 0)
    own = own.astype(bf16)
    values = with_ones(kv_ref[:, HD:])
    own_values = with_ones(own[:, HD:])
    lane = key_id
    tile = jnp.zeros((QN, HD), f32)
    for h in range(HEADS):
        cols = slice(h * HD, (h + 1) * HD)
        q = jnp.concatenate([qa_ref[:, cols], qb_ref[:, cols]], axis=0)
        scores = jnp.where(live, dot_t(q, kv_ref[:, :HD]), masked_score)
        own_scores = jnp.where(seen, dot_t(q, own[:, :HD]), masked_score)
        highest = jnp.maximum(
            jnp.max(scores, axis=-1, keepdims=True), jnp.max(own_scores, axis=-1, keepdims=True)
        )
        mixture = dot(jnp.exp2(scores - highest).astype(bf16), values)
        mixture = mixture + dot(jnp.exp2(own_scores - highest).astype(bf16), own_values)
        totals = mixture[:, HD:]
        buf_ref[:, cols] = mixture[:, :HD] / totals
        lse = highest + jnp.log(totals) * log2_e
        tile = jnp.where(lane // 32 == h, lse, tile)
    high = tile.astype(bf16).astype(f32)
    rest = tile - high
    middle = rest.astype(bf16).astype(f32)
    piece = lane % 32
    buf_ref[:, HEADS * HD :] = jnp.where(
        piece == 0, high, jnp.where(piece == 1, middle, jnp.where(piece == 2, rest - middle, 0.0))
    )
    for g in range(N_BLK):
        source = gathered_source(jnp.int32(g), x_at, z_at)
        out_ref[source] = buf_ref[g * QROWS : (g + 1) * QROWS, :].astype(bf16)


def question_attention(block_len, where, first_half, second_half, kv, own):
    width = (HEADS + 1) * HD
    vmem = pl.BlockSpec(memory_space=pltpu.VMEM)
    return pl.pallas_call(
        question_attention_kernel,
        out_shape=jax.ShapeDtypeStruct((N_BLK, QROWS, width), bf16),
        in_specs=[smem, smem, vmem, vmem, vmem, vmem],
        out_specs=vmem,
        scratch_shapes=[pltpu.VMEM((QN, width), f32)],
        compiler_params=pltpu.CompilerParams(vmem_limit_bytes=40 * 2**20),
        cost_estimate=cost(HEADS * QN * 640 * HD * 8, 2**20, HEADS * QN * 640),
        name="question_attention",
    )(block_len, where, first_half, second_half, kv, own)


def context_kernel(
    len_ref, where_ref, q_ref, o_ref, lse_ref, a0_ref, a1_ref, a2_ref, a3_ref, w_hbm,
    keep_ref, send_ref, w_ref, akv_ref, att_ref, sem,
):
    step = pl.program_id(0)
    blk_at, kv_at = where_ref[0], where_ref[1]
    y_at, c_at = kv_at // NC, lax.rem(kv_at, NC)
    copy = pltpu.make_async_copy(w_hbm, w_ref, sem)

    @pl.when(step == 0)
    def _():
        copy.start()
        x_at = blk_at // NZ
        for x, ref in enumerate((a0_ref, a1_ref, a2_ref, a3_ref)):

            @pl.when(x_at == x)
            def _(ref=ref):
                akv_ref[...] = ref[...]

    first = blk_at == 0
    row = lax.broadcasted_iota(jnp.int32, (ROWS, HD), 0) + step * ROWS
    valid = row < len_ref[blk_at]
    values = with_ones(akv_ref[:, HD:])
    for h in range(HEADS):
        scores = dot_t(q_ref[h], akv_ref[:, :HD])
        highest = jnp.max(scores, axis=-1, keepdims=True)
        mixture = dot(jnp.exp2(scores - highest).astype(bf16), values)
        own_lse = lse_ref[h]
        top = jnp.where(first, own_lse, jnp.maximum(own_lse, highest))
        own_part = jnp.exp2(own_lse - top)
        anchor_part = jnp.where(first, 0.0, jnp.exp2(jnp.minimum(highest - top, 0.0)))
        result = (o_ref[h] * own_part + mixture[:, :HD] * anchor_part) / (
            own_part + mixture[:, HD:] * anchor_part
        )
        att_ref[:, h * HD : (h + 1) * HD] = jnp.where(valid, result, 0.0).astype(bf16)

    @pl.when(step == 0)
    def _():
        copy.wait()

    for d in range(NY):
        to_y = lax.rem(y_at + d, NY)
        for out, to_c in ((send_ref, 1 - c_at), (keep_ref, c_at)):
            column = pl.multiple_of((to_y * NC + to_c) * FEAT, FEAT)
            out[d] = dot(att_ref[...], w_ref[:, pl.ds(column, FEAT)]).astype(bf16)


def context_attention(block_len, where, q, own_o, own_lse, anchors, w_out):
    part = pl.BlockSpec((HEADS, ROWS, HD), lambda r: (0, r, 0))
    out = pl.BlockSpec((NY, ROWS, FEAT), lambda r: (0, r, 0))
    return pl.pallas_call(
        context_kernel,
        grid=(BLK // ROWS,),
        in_specs=[smem, smem, part, part, part]
        + [whole((BLK, 2 * HD))] * 4
        + [pl.BlockSpec(memory_space=pl.ANY)],
        out_specs=[out, out],
        out_shape=[jax.ShapeDtypeStruct((NY, BLK, FEAT), bf16)] * 2,
        scratch_shapes=[
            pltpu.VMEM((HEADS * HD, D), bf16),
            pltpu.VMEM((BLK, 2 * HD), bf16),
            pltpu.VMEM((ROWS, HEADS * HD), bf16),
            pltpu.SemaphoreType.DMA,
        ],
        compiler_params=params(),
        cost_estimate=cost(2 * BLK * 512 * D + HEADS * BLK * BLK * HD * 8, 12 * 2**20, HEADS * BLK * BLK),
        name="context_attention",
    )(block_len, where, q, own_o, own_lse, *anchors, w_out)


def merge_kernel(qlen_ref, where_ref, parts_ref, w_ref, out_ref, att_ref):
    @pl.when(pl.program_id(0) == 0)
    def _():
        parts = parts_ref[...].astype(f32)
        row = lax.broadcasted_iota(jnp.int32, (QROWS, HD), 0) + where_ref[0] * QROWS
        valid = row < qlen_ref[0]
        stats = parts[:, :, HEADS * HD :]
        for h in range(HEADS):
            at = h * 32
            lse = (stats[:, :, at : at + 1] + stats[:, :, at + 1 : at + 2]) + stats[:, :, at + 2 : at + 3]
            top = jnp.max(lse, axis=0, keepdims=True)
            share = jnp.exp2(lse - top)
            mixture = jnp.sum(parts[:, :, h * HD : (h + 1) * HD] * share, axis=0)
            result = mixture / jnp.sum(share, axis=0)
            att_ref[:, h * HD : (h + 1) * HD] = jnp.where(valid, result, 0.0)

    out_ref[0] = dot(att_ref[...].astype(bf16), w_ref[...]).astype(bf16)


def merge_and_project(question_len, where, parts, w_out):
    return pl.pallas_call(
        merge_kernel,
        grid=(N_KV,),
        in_specs=[
            smem,
            smem,
            whole(parts.shape),
            pl.BlockSpec((HEADS * HD, FEAT), lambda k: (0, k)),
        ],
        out_specs=pl.BlockSpec((1, QROWS, FEAT), lambda k: (k, 0, 0)),
        out_shape=jax.ShapeDtypeStruct((N_KV, QROWS, FEAT), bf16),
        scratch_shapes=[pltpu.VMEM((QROWS, HEADS * HD), f32)],
        compiler_params=params(),
        cost_estimate=cost(2 * QROWS * 512 * D * 32, 5 * 2**20),
        name="merge_and_project",
    )(question_len, where, parts, w_out)


def shift_x(value, by):
    pairs = [(x * NZ + z, (x + by) % NX * NZ + z) for x in range(NX) for z in range(NZ)]
    return lax.ppermute(value, "blk", pairs)


def shift_z(value, by):
    pairs = [(x * NZ + z, x * NZ + (z + by) % NZ) for x in range(NX) for z in range(NZ)]
    return lax.ppermute(value, "blk", pairs)


def shift_y(value, by):
    pairs = [(y * NC + c, (y + by) % NY * NC + c) for y in range(NY) for c in range(NC)]
    return lax.ppermute(value, "kv", pairs)


def swap_cores(value):
    pairs = [(y * NC + c, y * NC + 1 - c) for y in range(NY) for c in range(NC)]
    return lax.ppermute(value, "kv", pairs)


def gather_questions(queries):
    rows = jnp.concatenate([queries] + [shift_x(queries, k) for k in (1, 2, 3)], 0)
    rows = jnp.concatenate([rows] + [shift_z(rows, k) for k in (1, 2, -1)], 0)
    return rows, shift_z(rows, 4)


def anchors_of(kv, blk_at):
    z_at = blk_at % NZ
    first = jnp.where(blk_at == 0, kv, jnp.zeros_like(kv))
    held = first + lax.ppermute(kv, "blk", [(0, 3)]) + lax.ppermute(kv, "blk", [(0, 5)])
    held = (
        held
        + lax.ppermute(held, "blk", [(0, 1), (3, 4), (5, 6)])
        + lax.ppermute(held, "blk", [(0, 7), (3, 2)])
    )
    others = [
        lax.ppermute(held, "blk", [(z, x * NZ + z) for z in range(NZ)]) for x in range(1, NX)
    ]
    return [held] + others


def body(context, question, norm_gain, w_query, w_key, w_value, w_out, block_len, question_len):
    blk_at = lax.axis_index("blk").astype(jnp.int32)
    kv_at = lax.axis_index("kv").astype(jnp.int32)
    where = jnp.stack([blk_at, kv_at])
    tables = [jnp.asarray(t) for t in angle_tables(np.arange(BLK))]
    tables += [jnp.asarray(t) for t in angle_tables(np.arange(N_BLK + 1) * BLK)]
    gain = norm_gain.reshape(1, D)

    own_q, own_kv = question_projection(
        block_len, where, question, gain, w_query, w_key, w_value, tables
    )
    first_half, second_half = gather_questions(own_q)
    kv, factor = kv_projection(where, context, gain, w_key, w_value, tables)
    anchors = anchors_of(kv, blk_at)
    q = query_projection(where, context, gain, w_query, factor, tables)
    own_o, own_lse = own_attention(q, kv)
    parts = question_attention(block_len, where, first_half, second_half, kv, own_kv)

    keep, send = context_attention(block_len, where, q, own_o, own_lse, anchors, w_out)
    got = swap_cores(send)

    def both(d):
        return (keep[d].astype(f32) + got[d].astype(f32)).astype(bf16)

    arrived = [shift_y(both(d), d) for d in (1, 3, 2)]
    context_out = keep[0].astype(f32) + got[0].astype(f32)
    for part in arrived:
        context_out = context_out + part.astype(f32)

    parts = lax.all_to_all(parts, "blk", 0, 0)
    question_part = merge_and_project(question_len, where, parts, w_out)
    question_part = lax.all_to_all(question_part, "kv", 0, 0)
    question_out = jnp.sum(question_part.astype(f32), axis=0)
    return context_out.astype(bf16), question_out.astype(bf16)


def solution(mesh):
    return jax.shard_map(
        body,
        mesh=mesh,
        in_specs=(
            P("blk", None),
            P("blk", None),
            P(),
            P(None, "kv"),
            P(None, "kv"),
            P(None, "kv"),
            P("kv", None),
            P(),
            P(),
        ),
        out_specs=(P("blk", "kv"), P("blk", "kv")),
        check_vma=False,
    )
```

time: 491 us -> 133 us (0.27)
  waiting for transfers between devices: 175 us -> 34.1 us
  blocking collectives: 135 us -> 9.9 us
  other arithmetic: 98.6 us -> 6.2 us
  starting transfers between devices: 0.3 us -> 37.9 us
  matrix products: 27.1 us -> 0 us
  Pallas kernels: 0 us -> 25.7 us
  local copies, waits for them, and re-layouts: 36.6 us -> 15.4 us
  between operations: 14.8 us -> 1.69 us
    all_gather x1 -> x0, waiting for transfers between devices: 137 us -> none  [combined_all(): everything = jax.tree.map(lambda part: lax.all_gather(part, axis), value)]
    all_gather x3 -> x0, blocking collectives: 135 us -> none  [the longest x2 83.2 us: combined_all(): everything = jax.tree.map(lambda part: lax.all_gather(part, axis), value)]
    add x65 -> x2, other arithmetic: 81.4 us -> 0.09 us  [the longest x1 0.05 us: anchors_of(): first + lax.ppermute(kv, 'blk', [(0, 3)])]
    reduce_scatter x1 -> x0, waiting for transfers between devices: 37.9 us -> none  [body(): lax.psum_scatter(term_rows.astype(jnp.bfloat16), 'kv', scatter_dimension=...]
    ppermute x0 -> x18, waiting for transfers between devices: none -> 31.4 us  [the longest x1 20.3 us: anchors_of(): lax.ppermute(held, 'blk', [(0, 1), (3, 4), (5, 6)])]
    dot_general x8 -> x0, matrix products: 27.1 us -> none  [the longest x3 11.8 us: project(): product = jnp.dot(normed, weight, preferred_element_type=jnp.float32)]
    ppermute x0 -> x18, starting transfers between devices: none -> 26.6 us  [the longest x4 11.2 us: shift_z(): return lax.ppermute(value, 'blk', pairs)]
    pallas_call x0 -> x7, Pallas kernels: none -> 25.7 us  [the longest x1 6.79 us: context_attention(): pl.pallas_call(context_kernel, grid=(BLK // ROWS,), in_specs=[smem, smem,...]
  transfers between devices with their start and end apart: 3 -> 19, of which waited for: 2 -> 5; matrix products, arithmetic and copies ran while one was open for 5% -> 3% of each run, Pallas kernels for 0% -> 11%
where the time goes in v1:
time: 133 us; the launch traced here: 131 us
  starting transfers between devices  37.9 us (28%)
  waiting for transfers between devices  34.1 us (26%)
  Pallas kernels  25.7 us (19%)
  local copies, waits for them, and re-layouts  15.4 us (12%)
  blocking collectives  9.9 us (7%)
  other arithmetic  6.2 us (5%)
  between operations  1.69 us (1%)
    ppermute x1, waiting for transfers between devices, anchors_of(): lax.ppermute(held, 'blk', [(0, 1), (3, 4), (5, 6)])  20.3 us
    unnamed x49, local copies, waits for them, and re-layouts  15.3 us
    all_to_all x1, starting transfers between devices, body(): parts = lax.all_to_all(parts, 'blk', 0, 0)  11.3 us
    ppermute x4, starting transfers between devices, shift_z(): return lax.ppermute(value, 'blk', pairs)  11.2 us
    all_to_all x1, blocking collectives, body(): question_part = lax.all_to_all(question_part, 'kv', 0, 0)  9.9 us
    pallas_call x1, Pallas kernels, context_attention(): pl.pallas_call(context_kernel, grid=(BLK // ROWS,), in_specs=[smem, smem,...  6.79 us
    ppermute x4, waiting for transfers between devices, shift_z(): return lax.ppermute(value, 'blk', pairs)  6.49 us
    ppermute x3, starting transfers between devices, shift_y(): return lax.ppermute(value, 'kv', pairs)  5.83 us
  transfers between devices with their start and end apart: 19, of which 5 were waited for; matrix products, arithmetic and copies ran while one was open for 3% of the time, Pallas kernels for 11%

profile of v1, /device:TPU:32, one launch (start us, length us, event | category | flops | bytes accessed | tf_op | source)
XLA Modules:
  0.0 130.8 jit_solution(3390560714218439752)
XLA Ops:
  0.7 2.2 %copy-done.4 = bf16[512,4096]{1,0:T(8,128)(2,1)S(1)} copy-done((bf16[512,4096]{1,0:T(8,128)(2,1)S(1)}, bf16[512,4096]{1,0:T(8,128)(2,1)}, u32[]{:S(2)}) %copy-start.4) | copy-done | bytes 4194328
  4.8 1.2 copy-done.10
  9.4 3.9 %kv_projection.1 = (bf16[512,256]{1,0:T(8,128)(2,1)S(1)}, f32[512,128]{1,0:T(8,128)S(1)}) custom-call(s32[2]{0:T(128)S(1)} %pad_add_fusion.where_ref, bf16[512,4096]{1,0:T(8,128)(2,1)S(1)} %copy-done.4, f32[1,4096]{1,0:T(1,128)S(1)} %bitcast.17, bf16[4096,128]{1,0:T(8,128)(2,1)S(1)} %copy-done.10, bf16[4096,128]{1,0:T(8,128)(2,1)S(1)} %copy-done.12, ...), custom_call_target="tpu_custom_call" | custom-call | flops 3221225472 | bytes 6291456 | tf_op jit(solution)/shard_map/kv_projection/pallas_call | solution.py:200
  15.7 1.3 collective-permute-start.2
  17.0 20.3 %collective-permute-done.2 = bf16[512,256]{1,0:T(8,128)(2,1)S(1)} collective-permute-done((bf16[512,256]{1,0:T(8,128)(2,1)S(1)}, bf16[512,256]{1,0:T(8,128)(2,1)S(1)}, u32[]{:S(2)}, u32[]{:S(2)}) %collective-permute-start.2) | collective-permute-done | bytes 262176 | tf_op jit(solution)/shard_map/ppermute | solution.py:518
  37.3 1.3 collective-permute-start.6
  38.6 1.3 collective-permute-start.5
  39.9 1.3 collective-permute-start.4
  41.2 2.2 %copy-done = bf16[4096,512]{1,0:T(8,128)(2,1)S(1)} copy-done((bf16[4096,512]{1,0:T(8,128)(2,1)S(1)}, bf16[4096,512]{1,0:T(8,128)(2,1)}, u32[]{:S(2)}) %copy-start) | copy-done | bytes 4194328
  43.4 2.2 %copy-done.5 = bf16[512,4096]{1,0:T(8,128)(2,1)S(1)} copy-done((bf16[512,4096]{1,0:T(8,128)(2,1)S(1)}, bf16[512,4096]{1,0:T(8,128)(2,1)}, u32[]{:S(2)}) %copy-start.5) | copy-done | bytes 4194328
  45.6 5.0 %query_projection.1.q_ref = bf16[4,512,128]{2,1,0:T(8,128)(2,1)S(1)} custom-call(s32[2]{0:T(128)S(1)} %pad_add_fusion.where_ref, bf16[512,4096]{1,0:T(8,128)(2,1)S(1)} %copy-done.5, f32[1,4096]{1,0:T(1,128)S(1)} %bitcast.18, bf16[4096,512]{1,0:T(8,128)(2,1)S(1)} %copy-done, f32[512,128]{1,0:T(8,128)S(1)} %get-tuple-element.10.factor_ref, ...), custom_call_target="tpu_custom_call" | custom-call | flops 2147483648 | bytes 8388608 | tf_op jit(solution)/shard_map/query_projection/pallas_call | solution.py:253
  50.6 1.8 %own_attention.1 = (f32[4,512,128]{2,1,0:T(8,128)S(1)}, f32[4,512,128]{2,1,0:T(8,128)S(1)}) custom-call(bf16[4,512,128]{2,1,0:T(8,128)(2,1)S(1)} %query_projection.1.q_ref, bf16[512,256]{1,0:T(8,128)(2,1)S(1)} %get-tuple-element.11.kv_ref), custom_call_target="tpu_custom_call" | custom-call | flops 1073741824 | bytes 3145728 | tf_op jit(solution)/shard_map/own_attention/pallas_call | solution.py:305
  52.6 6.8 %context_attention.1 = (bf16[4,512,512]{2,1,0:T(8,128)(2,1)S(1)}, bf16[4,512,512]{2,1,0:T(8,128)(2,1)}) custom-call(s32[32]{0:T(128)S(1)} %copy-done.21, s32[2]{0:T(128)S(1)} %pad_add_fusion.where_ref, bf16[4,512,128]{2,1,0:T(8,128)(2,1)S(1)} %query_projection.1.q_ref, f32[4,512,128]{2,1,0:T(8,128)S(1)} %get-tuple-element.12.o_ref, ...), custom_call_target="tpu_custom_call" | custom-call | flops 3221225472 | bytes 12582912 | tf_op jit(solution)/shard_map/context_attention/pallas_call | solution.py:428
  59.6 2.5 %question_projection.1 = (bf16[8,512]{1,0:T(8,128)(2,1)S(1)}, bf16[8,256]{1,0:T(8,128)(2,1)S(1)}) custom-call(s32[32]{0:T(128)S(1)} %copy-done.21, s32[2]{0:T(128)S(1)} %pad_add_fusion.where_ref, bf16[8,4096]{1,0:T(8,128)(2,1)S(1)} %copy-done.18, f32[1,4096]{1,0:T(1,128)S(1)} %bitcast.19, bf16[4096,512]{1,0:T(8,128)(2,1)S(1)} %copy-done.1, ...), custom_call_target="tpu_custom_call" | custom-call | flops 1610612736 | bytes 6291456 | tf_op jit(solution)/shard_map/question_projection/pallas_call | solution.py:138
  62.2 1.8 %collective-permute-start.12 = (bf16[8,512]{1,0:T(8,128)(2,1)S(1)}, bf16[8,512]{1,0:T(8,128)(2,1)S(1)}, u32[]{:S(2)}, u32[]{:S(2)}) collective-permute-start(bf16[8,512]{1,0:T(8,128)(2,1)S(1)} %get-tuple-element.16), channel_id=1, source_target_pairs={{0,128},{8,136},{16,144},{24,152},{32,160},{40,168},{48,176},{56,1... | collective-permute-start | bytes 24584 | tf_op jit(solution)/shard_map/ppermute | solution.py:488
  64.2 4.6 %collective-permute-done.11 = bf16[8,512]{1,0:T(8,128)(2,1)S(1)} collective-permute-done((bf16[8,512]{1,0:T(8,128)(2,1)S(1)}, bf16[8,512]{1,0:T(8,128)(2,1)S(1)}, u32[]{:S(2)}, u32[]{:S(2)}) %collective-permute-start.11) | collective-permute-done | bytes 8224 | tf_op jit(solution)/shard_map/ppermute | solution.py:488
  68.9 2.1 %collective-permute-start.14 = (bf16[32,512]{1,0:T(8,128)(2,1)S(1)}, bf16[32,512]{1,0:T(8,128)(2,1)S(1)}, u32[]{:S(2)}, u32[]{:S(2)}) collective-permute-start(bf16[32,512]{1,0:T(8,128)(2,1)S(1)} %get-tuple-element.21), channel_id=1, source_target_pairs={{0,8},{8,16},{16,24},{24,32},{32,40},{40,48},{48,56},{56,0},{64,72... | collective-permute-start | bytes 98312 | tf_op jit(solution)/shard_map/ppermute | solution.py:493
  71.0 4.0 %collective-permute-start.15 = (bf16[32,512]{1,0:T(8,128)(2,1)S(1)}, bf16[32,512]{1,0:T(8,128)(2,1)S(1)}, u32[]{:S(2)}, u32[]{:S(2)}) collective-permute-start(bf16[32,512]{1,0:T(8,128)(2,1)S(1)} %get-tuple-element.21), channel_id=1, source_target_pairs={{0,16},{8,24},{16,32},{24,40},{32,48},{40,56},{48,0},{56,8},{64,80... | collective-permute-start | bytes 98312 | tf_op jit(solution)/shard_map/ppermute | solution.py:493
  75.0 2.4 %collective-permute-done.15 = bf16[32,512]{1,0:T(8,128)(2,1)S(1)} collective-permute-done((bf16[32,512]{1,0:T(8,128)(2,1)S(1)}, bf16[32,512]{1,0:T(8,128)(2,1)S(1)}, u32[]{:S(2)}, u32[]{:S(2)}) %collective-permute-start.15) | collective-permute-done | bytes 32800 | tf_op jit(solution)/shard_map/ppermute | solution.py:493
  77.4 5.0 %collective-permute-start.17 = (bf16[128,512]{1,0:T(8,128)(2,1)S(1)}, bf16[128,512]{1,0:T(8,128)(2,1)S(1)}, u32[]{:S(2)}, u32[]{:S(2)}) collective-permute-start(bf16[128,512]{1,0:T(8,128)(2,1)S(1)} %constant_dynamic-update-slice_fusion.4.qa_ref), channel_id=1, source_target_pairs={{0,32},{8,40},{16,48},{24,56},{32,0},{40,8},{48,16},{56,24},{64,96... | collective-permute-start | bytes 393224 | tf_op jit(solution)/shard_map/ppermute | solution.py:493
  82.4 4.1 %collective-permute-done.17.qb_ref = bf16[128,512]{1,0:T(8,128)(2,1)S(1)} collective-permute-done((bf16[128,512]{1,0:T(8,128)(2,1)S(1)}, bf16[128,512]{1,0:T(8,128)(2,1)S(1)}, u32[]{:S(2)}, u32[]{:S(2)}) %collective-permute-start.17) | collective-permute-done | bytes 131104 | tf_op jit(solution)/shard_map/ppermute | solution.py:493
  86.5 3.0 %question_attention.1 = bf16[32,8,640]{2,1,0:T(8,128)(2,1)} custom-call(s32[32]{0:T(128)S(1)} %copy-done.21, s32[2]{0:T(128)S(1)} %pad_add_fusion.where_ref, bf16[128,512]{1,0:T(8,128)(2,1)S(1)} %constant_dynamic-update-slice_fusion.4.qa_ref, bf16[128,512]{1,0:T(8,128)(2,1)S(1)} %collective-permute-done.17.qb_ref, ...), custom_call_target="tpu_custom_call" | custom-call | flops 671088640 | bytes 1048576 | tf_op jit(solution)/shard_map/question_attention/pallas_call | solution.py:366
  89.5 11.3 %all-to-all-start = ((bf16[32,8,640]{2,1,0:T(8,128)(2,1)}), bf16[32,8,640]{2,1,0:T(8,128)(2,1)S(1)}, u32[]{:S(2)}, u32[]{:S(2)}) async-start(bf16[32,8,640]{2,1,0:T(8,128)(2,1)} %question_attention.1), calls=%async_computation | async-start | bytes 655360 | tf_op jit(solution)/shard_map/all_to_all | solution.py:556
  100.9 2.8 %fusion.3 = (bf16[512,512]{1,0:T(8,128)(2,1)}, bf16[512,512]{1,0:T(8,128)(2,1)}, bf16[512,512]{1,0:T(8,128)(2,1)S(1)}) fusion(bf16[4,512,512]{2,1,0:T(8,128)(2,1)} %collective-permute-done.7, bf16[4,512,512]{2,1,0:T(8,128)(2,1)S(1)} %get-tuple-element.14), kind=kLoop, calls=%fused_computation.7 | loop fusion | flops 3145728 | bytes 4718592 | tf_op jit(solution)/shard_map/convert_element_type | solution.py:549
  103.6 1.6 %collective-permute-start.8 = (bf16[512,512]{1,0:T(8,128)(2,1)}, bf16[512,512]{1,0:T(8,128)(2,1)}, u32[]{:S(2)}, u32[]{:S(2)}) collective-permute-start(bf16[512,512]{1,0:T(8,128)(2,1)} %get-tuple-element.18), channel_id=1, source_target_pairs={{0,2},{1,3},{2,4},{3,5},{4,6},{5,7},{6,0},{7,1},{8,10},{9,11},{10,... | collective-permute-start | bytes 1572872 | tf_op jit(solution)/shard_map/ppermute | solution.py:498
  105.2 2.9 %collective-permute-start.10 = (bf16[512,512]{1,0:T(8,128)(2,1)}, bf16[512,512]{1,0:T(8,128)(2,1)}, u32[]{:S(2)}, u32[]{:S(2)}) collective-permute-start(bf16[512,512]{1,0:T(8,128)(2,1)} %get-tuple-element.19), channel_id=1, source_target_pairs={{0,4},{1,5},{2,6},{3,7},{4,0},{5,1},{6,2},{7,3},{8,12},{9,13},{10,... | collective-permute-start | bytes 1572872 | tf_op jit(solution)/shard_map/ppermute | solution.py:498
  108.1 1.3 %collective-permute-start.9 = (bf16[512,512]{1,0:T(8,128)(2,1)S(1)}, bf16[512,512]{1,0:T(8,128)(2,1)}, u32[]{:S(2)}, u32[]{:S(2)}) collective-permute-start(bf16[512,512]{1,0:T(8,128)(2,1)S(1)} %get-tuple-element.20), channel_id=1, source_target_pairs={{0,6},{1,7},{2,0},{3,1},{4,2},{5,3},{6,4},{7,5},{8,14},{9,15},{10,... | collective-permute-start | bytes 1572872 | tf_op jit(solution)/shard_map/ppermute | solution.py:498
  110.1 2.6 %all-to-all-done.parts_ref = bf16[32,8,640]{2,1,0:T(8,128)(2,1)S(1)} async-done(((bf16[32,8,640]{2,1,0:T(8,128)(2,1)}), bf16[32,8,640]{2,1,0:T(8,128)(2,1)S(1)}, u32[]{:S(2)}, u32[]{:S(2)}) %all-to-all-start) | async-done | bytes 327712 | tf_op jit(solution)/shard_map/all_to_all | solution.py:556
  112.8 2.2 %copy-done.3 = bf16[512,4096]{1,0:T(8,128)(2,1)S(1)} copy-done((bf16[512,4096]{1,0:T(8,128)(2,1)S(1)}, bf16[512,4096]{1,0:T(8,128)(2,1)}, u32[]{:S(2)}) %copy-start.3) | copy-done | bytes 4194328
  114.9 2.7 %merge_and_project.1 = bf16[8,8,512]{2,1,0:T(8,128)(2,1)S(1)} custom-call(s32[1]{0:T(128)S(6)} %copy.24.qlen_ref, s32[2]{0:T(128)S(1)} %pad_add_fusion.where_ref, bf16[32,8,640]{2,1,0:T(8,128)(2,1)S(1)} %all-to-all-done.parts_ref, bf16[512,4096]{1,0:T(8,128)(2,1)S(1)} %copy-done.3), custom_call_target="tpu_custom_call" | custom-call | flops 1073741824 | bytes 5242880 | tf_op jit(solution)/shard_map/merge_and_project/pallas_call | solution.py:468
  117.7 9.9 %all_to_all.10 = bf16[8,8,512]{2,1,0:T(8,128)(2,1)S(1)} all-to-all(bf16[8,8,512]{2,1,0:T(8,128)(2,1)S(1)} %merge_and_project.1), channel_id=1, replica_groups=mesh['blk'=32,'kv'=8] {'kv'}, dimensions={0} | all-to-all | bytes 131072 | tf_op jit(solution)/shard_map/all_to_all | solution.py:558
  128.2 2.6 %fusion.2 = bf16[512,512]{1,0:T(8,128)(2,1)} fusion(bf16[512,512]{1,0:T(8,128)(2,1)} %collective-permute-done.10, bf16[512,512]{1,0:T(8,128)(2,1)} %collective-permute-done.9, bf16[512,512]{1,0:T(8,128)(2,1)} %collective-permute-done.8, bf16[4,512,512]{2,1,0:T(8,128)(2,1)} %collective-permute-done.7, bf16[4,512,512]{2,1,0:T(8,128)(2,1)S(1)} %get-tuple-element.14), kind=kLoop, calls=%fused_computation.3 | loop fusion | flops 2621440 | bytes 3145728 | tf_op jit(solution)/shard_map/convert_element_type | solution.py:560
  (71 shorter events, 8.8 us)
Async XLA Ops:
  0.7 2.2 %copy-start.4 = (bf16[512,4096]{1,0:T(8,128)(2,1)S(1)}, bf16[512,4096]{1,0:T(8,128)(2,1)}, u32[]{:S(2)}) copy-start(bf16[512,4096]{1,0:T(8,128)(2,1)} %x_ref.4) | copy-start | bytes 12582916
  13.4 27.9 %copy-start.7 = (f32[512,128]{1,0:T(8,128)S(1)}, f32[512,128]{1,0:T(8,128)}, u32[]{:S(2)}) copy-start(f32[512,128]{1,0:T(8,128)} %constant.24.clone.st_ref) | copy-start | bytes 786436
  13.4 27.9 %copy-start.9 = (f32[512,128]{1,0:T(8,128)S(1)}, f32[512,128]{1,0:T(8,128)}, u32[]{:S(2)}) copy-start(f32[512,128]{1,0:T(8,128)} %constant.23.clone.ct_ref) | copy-start | bytes 786436
  13.4 27.8 %copy-start.20 = (f32[4096]{0:T(1024)S(1)}, f32[4096]{0:T(1024)}, u32[]{:S(2)}) copy-start(f32[4096]{0:T(1024)} %param.15) | copy-start | bytes 49156
  13.4 1.5 %collective-permute-start.1 = (bf16[512,256]{1,0:T(8,128)(2,1)S(1)}, bf16[512,256]{1,0:T(8,128)(2,1)S(1)}, u32[]{:S(2)}, u32[]{:S(2)}) collective-permute-start(bf16[512,256]{1,0:T(8,128)(2,1)S(1)} %get-tuple-element.11.kv_ref), channel_id=1, source_target_pairs={{0,40},{1,41},{2,42},{3,43},{4,44},{5,45},{6,46},{7,47}} | collective-permute-start | bytes 786440 | tf_op jit(solution)/shard_map/ppermute | solution.py:515
  14.2 0.7 collective-permute-start
  15.0 2.0 %collective-permute-start.3 = (bf16[512,256]{1,0:T(8,128)(2,1)S(1)}, bf16[512,256]{1,0:T(8,128)(2,1)S(1)}, u32[]{:S(2)}, u32[]{:S(2)}) collective-permute-start(bf16[512,256]{1,0:T(8,128)(2,1)S(1)} %add_add_fusion.1), channel_id=1, source_target_pairs={{0,56},{24,16},{1,57},{25,17},{2,58},{26,18},{3,59},{27,19},{4,60}... | collective-permute-start | bytes 786440 | tf_op jit(solution)/shard_map/ppermute | solution.py:519
  15.7 21.6 %collective-permute-start.2 = (bf16[512,256]{1,0:T(8,128)(2,1)S(1)}, bf16[512,256]{1,0:T(8,128)(2,1)S(1)}, u32[]{:S(2)}, u32[]{:S(2)}) collective-permute-start(bf16[512,256]{1,0:T(8,128)(2,1)S(1)} %add_add_fusion.1), channel_id=1, source_target_pairs={{0,8},{24,32},{40,48},{1,9},{25,33},{41,49},{2,10},{26,34},{42,50}... | collective-permute-start | bytes 786440 | tf_op jit(solution)/shard_map/ppermute | solution.py:518
  37.3 15.2 %collective-permute-start.6 = (bf16[512,256]{1,0:T(8,128)(2,1)S(1)}, bf16[512,256]{1,0:T(8,128)(2,1)S(1)}, u32[]{:S(2)}, u32[]{:S(2)}) collective-permute-start(bf16[512,256]{1,0:T(8,128)(2,1)S(1)} %add_add_fusion.a0_ref), channel_id=1, source_target_pairs={{0,192},{8,200},{16,208},{24,216},{32,224},{40,232},{48,240},{56,2... | collective-permute-start | bytes 786440 | tf_op jit(solution)/shard_map/ppermute | solution.py:522
  38.6 13.9 %collective-permute-start.5 = (bf16[512,256]{1,0:T(8,128)(2,1)S(1)}, bf16[512,256]{1,0:T(8,128)(2,1)S(1)}, u32[]{:S(2)}, u32[]{:S(2)}) collective-permute-start(bf16[512,256]{1,0:T(8,128)(2,1)S(1)} %add_add_fusion.a0_ref), channel_id=1, source_target_pairs={{0,128},{8,136},{16,144},{24,152},{32,160},{40,168},{48,176},{56,1... | collective-permute-start | bytes 786440 | tf_op jit(solution)/shard_map/ppermute | solution.py:522
  39.9 12.6 %collective-permute-start.4 = (bf16[512,256]{1,0:T(8,128)(2,1)S(1)}, bf16[512,256]{1,0:T(8,128)(2,1)S(1)}, u32[]{:S(2)}, u32[]{:S(2)}) collective-permute-start(bf16[512,256]{1,0:T(8,128)(2,1)S(1)} %add_add_fusion.a0_ref), channel_id=1, source_target_pairs={{0,64},{8,72},{16,80},{24,88},{32,96},{40,104},{48,112},{56,120},{... | collective-permute-start | bytes 786440 | tf_op jit(solution)/shard_map/ppermute | solution.py:522
  41.2 2.2 %copy-start = (bf16[4096,512]{1,0:T(8,128)(2,1)S(1)}, bf16[4096,512]{1,0:T(8,128)(2,1)}, u32[]{:S(2)}) copy-start(bf16[4096,512]{1,0:T(8,128)(2,1)} %wq_ref.3) | copy-start | bytes 12582916
  45.6 6.9 %copy-start.2 = (bf16[512,4096]{1,0:T(8,128)(2,1)S(1)}, bf16[512,4096]{1,0:T(8,128)(2,1)}, u32[]{:S(2)}) copy-start(bf16[512,4096]{1,0:T(8,128)(2,1)} %w_ref.1) | copy-start | bytes 12582916
  52.5 7.0 %copy-start.1 = (bf16[4096,512]{1,0:T(8,128)(2,1)S(1)}, bf16[4096,512]{1,0:T(8,128)(2,1)}, u32[]{:S(2)}) copy-start(bf16[4096,512]{1,0:T(8,128)(2,1)} %wq_ref.3) | copy-start | bytes 12582916
  52.5 7.0 %copy-start.11 = (bf16[4096,128]{1,0:T(8,128)(2,1)S(1)}, bf16[4096,128]{1,0:T(8,128)(2,1)}, u32[]{:S(2)}) copy-start(bf16[4096,128]{1,0:T(8,128)(2,1)} %wk_ref.3) | copy-start | bytes 3145732
  52.6 7.0 %copy-start.13 = (bf16[4096,128]{1,0:T(8,128)(2,1)S(1)}, bf16[4096,128]{1,0:T(8,128)(2,1)}, u32[]{:S(2)}) copy-start(bf16[4096,128]{1,0:T(8,128)(2,1)} %wv_ref.3) | copy-start | bytes 3145732
  52.6 7.0 %copy-start.15 = (f32[33,128]{1,0:T(8,128)S(1)}, f32[33,128]{1,0:T(8,128)}, u32[]{:S(2)}) copy-start(f32[33,128]{1,0:T(8,128)} %constant.26.clone.sb_ref) | copy-start | bytes 50692
  52.6 7.0 %copy-start.17 = (f32[33,128]{1,0:T(8,128)S(1)}, f32[33,128]{1,0:T(8,128)}, u32[]{:S(2)}) copy-start(f32[33,128]{1,0:T(8,128)} %constant.25.clone.cb_ref) | copy-start | bytes 50692
  52.6 7.0 %copy-start.18 = (bf16[8,4096]{1,0:T(8,128)(2,1)S(1)}, bf16[8,4096]{1,0:T(8,128)(2,1)}, u32[]{:S(2)}) copy-start(bf16[8,4096]{1,0:T(8,128)(2,1)} %x_ref.5) | copy-start | bytes 196612
  59.4 41.4 %collective-permute-start.7 = (bf16[4,512,512]{2,1,0:T(8,128)(2,1)}, bf16[4,512,512]{2,1,0:T(8,128)(2,1)}, u32[]{:S(2)}, u32[]{:S(2)}) collective-permute-start(bf16[4,512,512]{2,1,0:T(8,128)(2,1)} %get-tuple-element.15), channel_id=1, source_target_pairs={{0,1},{1,0},{2,3},{3,2},{4,5},{5,4},{6,7},{7,6},{8,9},{9,8},{10,11... | collective-permute-start | bytes 6291464 | tf_op jit(solution)/shard_map/ppermute | solution.py:503
  62.1 6.8 %collective-permute-start.13 = (bf16[8,512]{1,0:T(8,128)(2,1)S(1)}, bf16[8,512]{1,0:T(8,128)(2,1)S(1)}, u32[]{:S(2)}, u32[]{:S(2)}) collective-permute-start(bf16[8,512]{1,0:T(8,128)(2,1)S(1)} %get-tuple-element.16), channel_id=1, source_target_pairs={{0,192},{8,200},{16,208},{24,216},{32,224},{40,232},{48,240},{56,2... | collective-permute-start | bytes 24584 | tf_op jit(solution)/shard_map/ppermute | solution.py:488
  62.2 6.7 %collective-permute-start.12 = (bf16[8,512]{1,0:T(8,128)(2,1)S(1)}, bf16[8,512]{1,0:T(8,128)(2,1)S(1)}, u32[]{:S(2)}, u32[]{:S(2)}) collective-permute-start(bf16[8,512]{1,0:T(8,128)(2,1)S(1)} %get-tuple-element.16), channel_id=1, source_target_pairs={{0,128},{8,136},{16,144},{24,152},{32,160},{40,168},{48,176},{56,1... | collective-permute-start | bytes 24584 | tf_op jit(solution)/shard_map/ppermute | solution.py:488
  64.0 4.9 %collective-permute-start.11 = (bf16[8,512]{1,0:T(8,128)(2,1)S(1)}, bf16[8,512]{1,0:T(8,128)(2,1)S(1)}, u32[]{:S(2)}, u32[]{:S(2)}) collective-permute-start(bf16[8,512]{1,0:T(8,128)(2,1)S(1)} %get-tuple-element.16), channel_id=1, source_target_pairs={{0,64},{8,72},{16,80},{24,88},{32,96},{40,104},{48,112},{56,120},{... | collective-permute-start | bytes 24584 | tf_op jit(solution)/shard_map/ppermute | solution.py:488
  68.9 6.1 %collective-permute-start.14 = (bf16[32,512]{1,0:T(8,128)(2,1)S(1)}, bf16[32,512]{1,0:T(8,128)(2,1)S(1)}, u32[]{:S(2)}, u32[]{:S(2)}) collective-permute-start(bf16[32,512]{1,0:T(8,128)(2,1)S(1)} %get-tuple-element.21), channel_id=1, source_target_pairs={{0,8},{8,16},{16,24},{24,32},{32,40},{40,48},{48,56},{56,0},{64,72... | collective-permute-start | bytes 98312 | tf_op jit(solution)/shard_map/ppermute | solution.py:493
  71.0 6.4 %collective-permute-start.16 = (bf16[32,512]{1,0:T(8,128)(2,1)S(1)}, bf16[32,512]{1,0:T(8,128)(2,1)S(1)}, u32[]{:S(2)}, u32[]{:S(2)}) collective-permute-start(bf16[32,512]{1,0:T(8,128)(2,1)S(1)} %get-tuple-element.21), channel_id=1, source_target_pairs={{0,56},{8,0},{16,8},{24,16},{32,24},{40,32},{48,40},{56,48},{64,12... | collective-permute-start | bytes 98312 | tf_op jit(solution)/shard_map/ppermute | solution.py:493
  71.0 6.4 %collective-permute-start.15 = (bf16[32,512]{1,0:T(8,128)(2,1)S(1)}, bf16[32,512]{1,0:T(8,128)(2,1)S(1)}, u32[]{:S(2)}, u32[]{:S(2)}) collective-permute-start(bf16[32,512]{1,0:T(8,128)(2,1)S(1)} %get-tuple-element.21), channel_id=1, source_target_pairs={{0,16},{8,24},{16,32},{24,40},{32,48},{40,56},{48,0},{56,8},{64,80... | collective-permute-start | bytes 98312 | tf_op jit(solution)/shard_map/ppermute | solution.py:493
  77.4 9.1 %collective-permute-start.17 = (bf16[128,512]{1,0:T(8,128)(2,1)S(1)}, bf16[128,512]{1,0:T(8,128)(2,1)S(1)}, u32[]{:S(2)}, u32[]{:S(2)}) collective-permute-start(bf16[128,512]{1,0:T(8,128)(2,1)S(1)} %constant_dynamic-update-slice_fusion.4.qa_ref), channel_id=1, source_target_pairs={{0,32},{8,40},{16,48},{24,56},{32,0},{40,8},{48,16},{56,24},{64,96... | collective-permute-start | bytes 393224 | tf_op jit(solution)/shard_map/ppermute | solution.py:493
  89.5 23.2 %all-to-all-start = ((bf16[32,8,640]{2,1,0:T(8,128)(2,1)}), bf16[32,8,640]{2,1,0:T(8,128)(2,1)S(1)}, u32[]{:S(2)}, u32[]{:S(2)}) async-start(bf16[32,8,640]{2,1,0:T(8,128)(2,1)} %question_attention.1), calls=%async_computation | async-start | bytes 655360 | tf_op jit(solution)/shard_map/all_to_all | solution.py:556
  103.6 24.5 %collective-permute-start.8 = (bf16[512,512]{1,0:T(8,128)(2,1)}, bf16[512,512]{1,0:T(8,128)(2,1)}, u32[]{:S(2)}, u32[]{:S(2)}) collective-permute-start(bf16[512,512]{1,0:T(8,128)(2,1)} %get-tuple-element.18), channel_id=1, source_target_pairs={{0,2},{1,3},{2,4},{3,5},{4,6},{5,7},{6,0},{7,1},{8,10},{9,11},{10,... | collective-permute-start | bytes 1572872 | tf_op jit(solution)/shard_map/ppermute | solution.py:498
  105.2 23.0 %collective-permute-start.10 = (bf16[512,512]{1,0:T(8,128)(2,1)}, bf16[512,512]{1,0:T(8,128)(2,1)}, u32[]{:S(2)}, u32[]{:S(2)}) collective-permute-start(bf16[512,512]{1,0:T(8,128)(2,1)} %get-tuple-element.19), channel_id=1, source_target_pairs={{0,4},{1,5},{2,6},{3,7},{4,0},{5,1},{6,2},{7,3},{8,12},{9,13},{10,... | collective-permute-start | bytes 1572872 | tf_op jit(solution)/shard_map/ppermute | solution.py:498
  108.1 20.1 %collective-permute-start.9 = (bf16[512,512]{1,0:T(8,128)(2,1)S(1)}, bf16[512,512]{1,0:T(8,128)(2,1)}, u32[]{:S(2)}, u32[]{:S(2)}) collective-permute-start(bf16[512,512]{1,0:T(8,128)(2,1)S(1)} %get-tuple-element.20), channel_id=1, source_target_pairs={{0,6},{1,7},{2,0},{3,1},{4,2},{5,3},{6,4},{7,5},{8,14},{9,15},{10,... | collective-permute-start | bytes 1572872 | tf_op jit(solution)/shard_map/ppermute | solution.py:498
  112.8 2.2 %copy-start.3 = (bf16[512,4096]{1,0:T(8,128)(2,1)S(1)}, bf16[512,4096]{1,0:T(8,128)(2,1)}, u32[]{:S(2)}) copy-start(bf16[512,4096]{1,0:T(8,128)(2,1)} %w_ref.1) | copy-start | bytes 12582916
  (9 other events, 10.6 us)

commit v2 on v0

v2 whole, which is shorter than its diff:
```python
import functools

import jax
import jax.numpy as jnp
import numpy as np
from jax import lax
from jax.experimental import pallas as pl
from jax.experimental.pallas import tpu as pltpu
from jax.sharding import PartitionSpec as P

HD = 128
HEADS = 4
BLK = 512
QROWS = 8
NX, NZ, NY, NC = 4, 8, 4, 2
N_BLK, N_KV = NX * NZ, NY * NC
QN = N_BLK * QROWS
D = 4096
FEAT = D // N_KV
KC = 512
ROWS = 256
QPAD = 16
ALL_ROWS = BLK + QPAD
FIRST = 272

epsilon = 1e-05
rope_base = 500000.0
masked_score = -1e30
q_scale = float(HD**-0.5 * np.log2(np.e))
log2_e = float(np.log2(np.e))

bf16 = jnp.bfloat16
f32 = jnp.float32


def angle_tables(positions):
    inverse_freq = rope_base ** (-2.0 * np.arange(HD // 2, dtype=np.float64) / HD)
    angles = np.asarray(positions, np.float64)[:, None] * inverse_freq[None, :]
    angles = np.concatenate([angles, angles], 1)
    return np.cos(angles).astype(np.float32), np.sin(angles).astype(np.float32)


def params(limit=24):
    return pltpu.CompilerParams(vmem_limit_bytes=limit * 2**20)


def cost(flops, bytes_accessed, transcendentals=0):
    return pl.CostEstimate(
        flops=flops, bytes_accessed=bytes_accessed, transcendentals=transcendentals
    )


def add_angles(first, second):
    return (
        first[0] * second[0] - first[1] * second[1],
        first[1] * second[0] + first[0] * second[1],
    )


def rotated(head, cosine, sine_signed):
    return head * cosine + pltpu.roll(head, HD // 2, 1) * sine_signed


def signed(sine):
    lane = lax.broadcasted_iota(jnp.int32, sine.shape, 1)
    return jnp.where(lane < HD // 2, -sine, sine)


def dot(a, b):
    return jnp.dot(a, b, preferred_element_type=f32)


def dot_t(a, b):
    return lax.dot_general(a, b, (((1,), (1,)), ((), ())), preferred_element_type=f32)


def lane_folded(values):
    total = values[:, :HD]
    for part in range(1, values.shape[1] // HD):
        total = total + values[:, part * HD : (part + 1) * HD]
    return total


def squares_to_factor(squares):
    mean = jnp.sum(squares, axis=-1, keepdims=True) * (1.0 / D)
    return lax.rsqrt(mean + epsilon)


smem = pl.BlockSpec(memory_space=pltpu.SMEM)
vmem = pl.BlockSpec(memory_space=pltpu.VMEM)
anywhere = pl.BlockSpec(memory_space=pl.ANY)


def with_ones(values):
    return jnp.concatenate([values, jnp.ones_like(values)], axis=1)


def slab(to_y, to_c):
    return pl.ds(pl.multiple_of((lax.rem(to_y, NY) * NC + to_c) * FEAT, FEAT), FEAT)


def projection_kernel(
    len_ref, x_hbm, question_hbm, gain_ref, wq_hbm, wk_hbm, wv_hbm, ct_ref, st_ref, cb_ref, sb_ref,
    q_ref, kv_ref, queries_ref, own_ref,
    x_ref, question_ref, wq_ref, wk_ref, wv_ref, scaled_ref, acc_ref, sq_ref, sems, question_sem,
):
    blk_at = lax.axis_index("blk")
    steps = D // KC
    width = HEADS * HD

    def copies(k):
        part = pl.ds(pl.multiple_of(k * KC, KC), KC)
        return [
            pltpu.make_async_copy(x_hbm.at[:, part], x_ref.at[:, part], sems.at[k, 0]),
            pltpu.make_async_copy(wq_hbm.at[part, :], wq_ref.at[part, :], sems.at[k, 1]),
            pltpu.make_async_copy(wk_hbm.at[part, :], wk_ref.at[part, :], sems.at[k, 2]),
            pltpu.make_async_copy(wv_hbm.at[part, :], wv_ref.at[part, :], sems.at[k, 3]),
        ]

    question_copy = pltpu.make_async_copy(question_hbm, question_ref, question_sem)
    question_copy.start()
    for k in range(3):
        for copy in copies(k):
            copy.start()
    acc_ref[...] = jnp.zeros_like(acc_ref)
    sq_ref[...] = jnp.zeros_like(sq_ref)
    question_copy.wait()

    def turn(k, _):
        for copy in copies(k):
            copy.wait()

        @pl.when(k + 3 < steps)
        def _():
            for copy in copies(k + 3):
                copy.start()

        part = pl.ds(pl.multiple_of(k * KC, KC), KC)
        gain = gain_ref[:, part]
        x = x_ref[:, part].astype(f32)
        sq_ref[:BLK] += lane_folded(x * x)
        scaled_ref[:BLK] = (x * gain).astype(bf16)
        x = question_ref[:, part].astype(f32)
        x = jnp.concatenate([x, jnp.zeros((QPAD - QROWS, KC), f32)], 0)
        sq_ref[BLK:] += lane_folded(x * x)
        scaled_ref[BLK:] = (x * gain).astype(bf16)
        acc_ref[:, :width] += dot(scaled_ref[...], wq_ref[part, :])
        acc_ref[:, width:] += dot(scaled_ref[...], jnp.concatenate([wk_ref[part, :], wv_ref[part, :]], axis=1))
        return 0

    lax.fori_loop(0, steps, turn, 0)

    factor = squares_to_factor(sq_ref[...])
    block = pl.ds(blk_at, 1)
    tokens = (ct_ref[...], st_ref[...])
    cosine, sine = add_angles(tokens, (cb_ref[block, :], sb_ref[block, :]))
    total = len_ref[0]
    for b in range(1, N_BLK):
        total = total + len_ref[b]
    high, low = pl.ds(total // BLK, 1), pl.ds(lax.rem(total, BLK), 1)
    base = add_angles((cb_ref[high, :], sb_ref[high, :]), (ct_ref[low, :], st_ref[low, :]))
    rows = pl.ds(pl.multiple_of(blk_at * QROWS, QROWS), QROWS)
    own_cosine, own_sine = add_angles((ct_ref[rows, :], st_ref[rows, :]), base)

    def heads_of(rows, cosine, sine):
        scale = factor[rows]
        cosine, sine = cosine * scale, signed(sine) * scale
        heads = [acc_ref[rows, h * HD : (h + 1) * HD] for h in range(HEADS + 2)]
        turned = [rotated(head, cosine, sine) for head in heads[: HEADS + 1]]
        return [head * q_scale for head in turned[:HEADS]], turned[HEADS], heads[HEADS + 1] * scale

    queries, key, value = heads_of(slice(0, BLK), cosine, sine)
    for h in range(HEADS):
        q_ref[h] = queries[h].astype(bf16)
    kv_ref[:, :HD] = key.astype(bf16)
    kv_ref[:, HD:] = value.astype(bf16)
    queries, key, value = heads_of(slice(BLK, BLK + QROWS), own_cosine, own_sine)
    own_ref[:, :HD] = key.astype(bf16)
    own_ref[:, HD:] = value.astype(bf16)
    queries = jnp.concatenate(queries, axis=1).astype(bf16)
    for b in range(N_BLK):
        queries_ref[b] = queries


def projections(block_len, context, question, gain, wq, wk, wv, tables):
    return pl.pallas_call(
        projection_kernel,
        in_specs=[smem, anywhere, anywhere, vmem, anywhere, anywhere, anywhere] + [vmem] * 4,
        out_specs=[vmem] * 4,
        out_shape=[
            jax.ShapeDtypeStruct((HEADS, BLK, HD), bf16),
            jax.ShapeDtypeStruct((BLK, 2 * HD), bf16),
            jax.ShapeDtypeStruct((N_BLK, QROWS, HEADS * HD), bf16),
            jax.ShapeDtypeStruct((QROWS, 2 * HD), bf16),
        ],
        scratch_shapes=[
            pltpu.VMEM((BLK, D), bf16),
            pltpu.VMEM((QROWS, D), bf16),
            pltpu.VMEM((D, HEADS * HD), bf16),
            pltpu.VMEM((D, HD), bf16),
            pltpu.VMEM((D, HD), bf16),
            pltpu.VMEM((BLK + QPAD, KC), bf16),
            pltpu.VMEM((BLK + QPAD, (HEADS + 2) * HD), f32),
            pltpu.VMEM((BLK + QPAD, HD), f32),
            pltpu.SemaphoreType.DMA((D // KC, 4)),
            pltpu.SemaphoreType.DMA,
        ],
        compiler_params=params(60),
        cost_estimate=cost(2 * BLK * D * 768, 12 * 2**20),
        name="projections",
    )(block_len, context, question, gain, wq, wk, wv, *tables)


def columns_kernel(w_hbm, _, keep_ref, send_ref, sems):
    kv_at = lax.axis_index("kv")
    y_at, c_at = kv_at // NC, lax.rem(kv_at, NC)
    copies = [
        pltpu.make_async_copy(w_hbm.at[:, slab(y_at + d, to_c)], target.at[d], sems.at[i, d])
        for i, (target, to_c) in enumerate(((send_ref, 1 - c_at), (keep_ref, c_at)))
        for d in range(NY)
    ]
    for copy in copies:
        copy.start()
    for copy in copies:
        copy.wait()


def columns(w_out, after):
    return pl.pallas_call(
        columns_kernel,
        in_specs=[anywhere] * 2,
        out_specs=[vmem] * 2,
        out_shape=[jax.ShapeDtypeStruct((NY, HEADS * HD, FEAT), bf16)] * 2,
        scratch_shapes=[pltpu.SemaphoreType.DMA((2, NY))],
        compiler_params=params(60),
        cost_estimate=cost(0, 8 * 2**20),
        name="columns",
    )(w_out, after)


def own_kernel(q_ref, kv_ref, _, o_ref, lse_ref):
    row = lax.broadcasted_iota(jnp.int32, (ROWS, ROWS), 0)
    column = lax.broadcasted_iota(jnp.int32, (ROWS, ROWS), 1)
    causal = column <= row
    for h in range(HEADS):
        for r in range(BLK // ROWS):
            rows = slice(r * ROWS, (r + 1) * ROWS)
            q = q_ref[h, rows, :]
            diagonal = dot_t(q, kv_ref[rows, :HD])
            diagonal = jnp.where(causal, diagonal, masked_score)
            highest = jnp.max(diagonal, axis=-1, keepdims=True)
            if r:
                earlier = dot_t(q, kv_ref[: r * ROWS, :HD])
                highest = jnp.maximum(highest, jnp.max(earlier, axis=-1, keepdims=True))
            weights = jnp.exp2(diagonal - highest).astype(bf16)
            mixture = dot(weights, with_ones(kv_ref[rows, HD:]))
            if r:
                weights = jnp.exp2(earlier - highest).astype(bf16)
                mixture = mixture + dot(weights, with_ones(kv_ref[: r * ROWS, HD:]))
            totals = mixture[:, HD:]
            o_ref[h, rows, :] = mixture[:, :HD] / totals
            lse_ref[h, rows, :] = highest + jnp.log(totals) * log2_e


def own_attention(q, kv, after):
    return pl.pallas_call(
        own_kernel,
        out_shape=[jax.ShapeDtypeStruct((HEADS, BLK, HD), f32)] * 2,
        in_specs=[vmem, vmem, anywhere],
        out_specs=[vmem] * 2,
        compiler_params=params(),
        cost_estimate=cost(HEADS * BLK * BLK * HD * 8, 3 * 2**20, HEADS * BLK * BLK),
        name="own_attention",
    )(q, kv, after)


def question_attention_kernel(len_ref, queries_ref, kv_ref, own_ref, out_ref):
    blk_at = lax.axis_index("blk")
    live = lax.broadcasted_iota(jnp.int32, (QN, BLK), 1) < len_ref[blk_at]
    question_id = lax.broadcasted_iota(jnp.int32, (QN, HD), 0)
    lane = lax.broadcasted_iota(jnp.int32, (QN, HD), 1)
    seen = (lane < QROWS) & (lane + blk_at * QROWS <= question_id)
    own = jnp.concatenate([own_ref[...].astype(f32), jnp.zeros((HD - QROWS, 2 * HD), f32)], 0)
    own = own.astype(bf16)
    values = with_ones(kv_ref[:, HD:])
    own_values = with_ones(own[:, HD:])
    tile = jnp.zeros((QN, HD), f32)
    for h in range(HEADS):
        cols = slice(h * HD, (h + 1) * HD)
        q = queries_ref[:, :, cols].reshape(QN, HD)
        scores = jnp.where(live, dot_t(q, kv_ref[:, :HD]), masked_score)
        own_scores = jnp.where(seen, dot_t(q, own[:, :HD]), masked_score)
        highest = jnp.maximum(
            jnp.max(scores, axis=-1, keepdims=True), jnp.max(own_scores, axis=-1, keepdims=True)
        )
        mixture = dot(jnp.exp2(scores - highest).astype(bf16), values)
        mixture = mixture + dot(jnp.exp2(own_scores - highest).astype(bf16), own_values)
        totals = mixture[:, HD:]
        out_ref[:, :, cols] = (mixture[:, :HD] / totals).reshape(N_BLK, QROWS, HD).astype(bf16)
        lse = highest + jnp.log(totals) * log2_e
        tile = jnp.where(lane // 32 == h, lse, tile)
    high = tile.astype(bf16).astype(f32)
    rest = tile - high
    middle = rest.astype(bf16).astype(f32)
    piece = lane % 32
    pieces = jnp.where(
        piece == 0, high, jnp.where(piece == 1, middle, jnp.where(piece == 2, rest - middle, 0.0))
    )
    out_ref[:, :, HEADS * HD :] = pieces.reshape(N_BLK, QROWS, HD).astype(bf16)


def question_attention(block_len, queries, kv, own):
    return pl.pallas_call(
        question_attention_kernel,
        out_shape=jax.ShapeDtypeStruct((N_BLK, QROWS, (HEADS + 1) * HD), bf16),
        in_specs=[smem] + [vmem] * 3,
        out_specs=vmem,
        compiler_params=params(),
        cost_estimate=cost(HEADS * QN * 640 * HD * 8, 2**20, HEADS * QN * 640),
        name="question_attention",
    )(block_len, queries, kv, own)


def merge_kernel(qlen_ref, parts_ref, _, out_ref):
    parts = parts_ref[...].astype(f32)
    row = lax.broadcasted_iota(jnp.int32, (QROWS, HD), 0) + lax.axis_index("blk") * QROWS
    valid = row < qlen_ref[0]
    stats = parts[:, :, HEADS * HD :]
    heads = []
    for h in range(HEADS):
        at = h * 32
        lse = (stats[:, :, at : at + 1] + stats[:, :, at + 1 : at + 2]) + stats[:, :, at + 2 : at + 3]
        top = jnp.max(lse, axis=0, keepdims=True)
        share = jnp.exp2(lse - top)
        mixture = jnp.sum(parts[:, :, h * HD : (h + 1) * HD] * share, axis=0)
        heads.append(jnp.where(valid, mixture / jnp.sum(share, axis=0), 0.0))
    rows = jnp.concatenate(heads, axis=1)
    out_ref[...] = jnp.concatenate(
        [rows, jnp.zeros((QPAD - QROWS, HEADS * HD), f32)], 0
    ).astype(bf16)


def merge_questions(question_len, parts, after):
    return pl.pallas_call(
        merge_kernel,
        in_specs=[smem, vmem, anywhere],
        out_specs=vmem,
        out_shape=jax.ShapeDtypeStruct((QPAD, HEADS * HD), bf16),
        compiler_params=params(),
        cost_estimate=cost(QN * 640 * 8, 2**19),
        name="merge_questions",
    )(question_len, parts, after)


def context_kernel(
    len_ref, q_ref, o_ref, lse_ref, akv_ref, att_ref
):
    blk_at = lax.axis_index("blk")
    first = blk_at == 0
    values = with_ones(akv_ref[:, HD:])
    for r in range(BLK // ROWS):
        rows = slice(r * ROWS, (r + 1) * ROWS)
        valid = lax.broadcasted_iota(jnp.int32, (ROWS, HD), 0) + r * ROWS < len_ref[blk_at]
        for h in range(HEADS):
            scores = dot_t(q_ref[h, rows, :], akv_ref[:, :HD])
            highest = jnp.max(scores, axis=-1, keepdims=True)
            mixture = dot(jnp.exp2(scores - highest).astype(bf16), values)
            own_lse = lse_ref[h, rows, :]
            top = jnp.where(first, own_lse, jnp.maximum(own_lse, highest))
            own_part = jnp.exp2(own_lse - top)
            anchor_part = jnp.where(first, 0.0, jnp.exp2(jnp.minimum(highest - top, 0.0)))
            result = (o_ref[h, rows, :] * own_part + mixture[:, :HD] * anchor_part) / (
                own_part + mixture[:, HD:] * anchor_part
            )
            att_ref[rows, h * HD : (h + 1) * HD] = jnp.where(valid, result, 0.0).astype(bf16)


def context_attention(block_len, q, own_o, own_lse, anchor):
    return pl.pallas_call(
        context_kernel,
        in_specs=[smem] + [vmem] * 4,
        out_specs=vmem,
        out_shape=jax.ShapeDtypeStruct((BLK, HEADS * HD), bf16),
        compiler_params=params(),
        cost_estimate=cost(HEADS * BLK * BLK * HD * 8 * 20, 4 * 2**20, HEADS * BLK * BLK),
        name="context_attention",
    )(block_len, q, own_o, own_lse, anchor)


def output_kernel(shares, *refs):
    rows_refs, (w_ref, w_other_ref), outs = refs[:4], refs[4:6], refs[6:-2]
    att_ref, other_ref = refs[-2:]
    for i, target in enumerate((att_ref, other_ref)):
        target[:BLK] = rows_refs[2 * i][...]
        target[BLK:] = rows_refs[2 * i + 1][...]
    for i, d in enumerate(shares):
        share = (dot(att_ref[...], w_ref[d]) + dot(other_ref[...], w_other_ref[d])).astype(bf16)
        if len(shares) == 1:
            outs[0][...] = share[:FIRST]
            outs[1][...] = share[FIRST:]
        else:
            outs[i][...] = share


def output_projection(shares, *operands):
    split = (FIRST, ALL_ROWS - FIRST) if len(shares) == 1 else (ALL_ROWS,) * len(shares)
    return pl.pallas_call(
        functools.partial(output_kernel, shares),
        in_specs=[vmem] * 6,
        out_specs=[vmem] * len(split),
        out_shape=[jax.ShapeDtypeStruct((rows, FEAT), bf16) for rows in split],
        scratch_shapes=[pltpu.VMEM((ALL_ROWS, HEADS * HD), bf16)] * 2,
        compiler_params=params(),
        cost_estimate=cost(4 * ALL_ROWS * HEADS * HD * FEAT * len(shares), 3 * 2**20),
        name="output_projection",
    )(*operands)


def relay_kernel(near_ref, far_ref, first_ref, second_ref, near_out, far_out):
    near_out[:FIRST] = (near_ref[:FIRST].astype(f32) + first_ref[...].astype(f32)).astype(bf16)
    near_out[FIRST:] = near_ref[FIRST:]
    far_out[:FIRST] = far_ref[:FIRST]
    far_out[FIRST:] = (far_ref[FIRST:].astype(f32) + second_ref[...].astype(f32)).astype(bf16)


def relay(near, far, first, second):
    return pl.pallas_call(
        relay_kernel,
        in_specs=[vmem] * 4,
        out_specs=[vmem] * 2,
        out_shape=[jax.ShapeDtypeStruct((ALL_ROWS, FEAT), bf16)] * 2,
        compiler_params=params(),
        cost_estimate=cost(ALL_ROWS * FEAT, ALL_ROWS * FEAT * 10),
        name="relay",
    )(near, far, first, second)


def finish_kernel(own_ref, left_ref, right_ref, out_ref, question_ref):
    total = own_ref[...].astype(f32) + left_ref[...].astype(f32) + right_ref[...].astype(f32)
    out_ref[...] = total[:BLK].astype(bf16)
    question_ref[...] = total[BLK : BLK + QROWS].astype(bf16)


def finish(own, left, right):
    return pl.pallas_call(
        finish_kernel,
        in_specs=[vmem] * 3,
        out_specs=[vmem] * 2,
        out_shape=[
            jax.ShapeDtypeStruct((BLK, FEAT), bf16),
            jax.ShapeDtypeStruct((QROWS, FEAT), bf16),
        ],
        compiler_params=params(),
        cost_estimate=cost(BLK * FEAT * 3, BLK * FEAT * 8),
        name="finish",
    )(own, left, right)


def sum_kernel(*refs):
    total = refs[0][...].astype(f32)
    for ref in refs[1:-2]:
        total = total + ref[...].astype(f32)
    refs[-1][...] = total.astype(bf16)


def sum_of(*parts, after):
    return pl.pallas_call(
        sum_kernel,
        in_specs=[vmem] * len(parts) + [anywhere],
        out_specs=vmem,
        out_shape=jax.ShapeDtypeStruct(parts[0].shape, bf16),
        compiler_params=params(),
        cost_estimate=cost(BLK * 256 * 3, BLK * 256 * 8),
        name="sum_of",
    )(*parts, after)


def shift_y(value, by):
    pairs = [(y * NC + c, (y + by) % NY * NC + c) for y in range(NY) for c in range(NC)]
    return lax.ppermute(value, "kv", pairs)


def swap_cores(value):
    pairs = [(y * NC + c, y * NC + 1 - c) for y in range(NY) for c in range(NC)]
    return lax.ppermute(value, "kv", pairs)


def body(context, question, norm_gain, w_query, w_key, w_value, w_out, block_len, question_len):
    blk_at = lax.axis_index("blk")
    tables = [jnp.asarray(t) for t in angle_tables(np.arange(BLK))]
    tables += [jnp.asarray(t) for t in angle_tables(np.arange(N_BLK + 1) * BLK)]

    q, kv, queries, own_kv = projections(
        block_len, context, question, norm_gain.reshape(1, D), w_query, w_key, w_value, tables
    )
    held = jnp.where(blk_at == 0, kv, jnp.zeros_like(kv))
    held = held + lax.ppermute(kv, "blk", [(0, 3)]) + lax.ppermute(kv, "blk", [(0, 5)])
    queries = lax.all_to_all(queries, "blk", 0, 0)
    w_keep, w_send = columns(w_out, held)
    own_o, own_lse = own_attention(q, kv, w_send)
    w_other = swap_cores(w_send)
    second = lax.ppermute(held, "blk", [(0, 1), (3, 4), (5, 6)])
    third = lax.ppermute(held, "blk", [(0, 7), (3, 2)])
    held = sum_of(held, second, third, after=own_o)
    anchor = jnp.where(blk_at < NZ, held, jnp.zeros_like(held))
    for x in range(1, NX):
        anchor = anchor + lax.ppermute(held, "blk", [(z, x * NZ + z) for z in range(NZ)])
    parts = question_attention(block_len, queries, kv, own_kv)
    parts = lax.all_to_all(parts, "blk", 0, 0)

    rows = context_attention(block_len, q, own_o, own_lse, anchor)
    other_rows = swap_cores(rows)
    questions = merge_questions(question_len, parts, rows)
    operands = (rows, questions, other_rows, swap_cores(questions), w_keep, w_other)
    across = output_projection((2,), *operands)
    first, second = shift_y(across[0], 1), shift_y(across[1], 3)
    near, far, own = output_projection((1, 3, 0), *operands)
    near, far = relay(near, far, first, second)
    return finish(own, shift_y(near, 1), shift_y(far, 3))


def solution(mesh):
    return jax.shard_map(
        body,
        mesh=mesh,
        in_specs=(
            P("blk", None),
            P("blk", None),
            P(),
            P(None, "kv"),
            P(None, "kv"),
            P(None, "kv"),
            P("kv", None),
            P(),
            P(),
        ),
        out_specs=(P("blk", "kv"), P("blk", "kv")),
        check_vma=False,
    )
```

time: 491 us -> 98 us (0.20)
  waiting for transfers between devices: 175 us -> 29.3 us
  blocking collectives: 135 us -> 0 us
  other arithmetic: 98.6 us -> 1.07 us
  starting transfers between devices: 0.3 us -> 33.8 us
  local copies, waits for them, and re-layouts: 36.6 us -> 3.43 us
  Pallas kernels: 0 us -> 28.1 us
  matrix products: 27.1 us -> 0 us
  between operations: 14.8 us -> 1.6 us
    all_gather x1 -> x0, waiting for transfers between devices: 137 us -> none  [combined_all(): everything = jax.tree.map(lambda part: lax.all_gather(part, axis), value)]
    all_gather x3 -> x0, blocking collectives: 135 us -> none  [the longest x2 83.2 us: combined_all(): everything = jax.tree.map(lambda part: lax.all_gather(part, axis), value)]
    add x65 -> x2, other arithmetic: 81.4 us -> 1.07 us  [the longest x1 1.02 us: body(): anchor + lax.ppermute(held, 'blk', [(z, x * NZ + z) for z in range(NZ)])]
    reduce_scatter x1 -> x0, waiting for transfers between devices: 37.9 us -> none  [body(): lax.psum_scatter(term_rows.astype(jnp.bfloat16), 'kv', scatter_dimension=...]
    pallas_call x0 -> x11, Pallas kernels: none -> 28.1 us  [the longest x1 9.69 us: projections(): pl.pallas_call(projection_kernel, in_specs=[smem, anywhere, anywhere, vme...]
    dot_general x8 -> x0, matrix products: 27.1 us -> none  [the longest x3 11.8 us: project(): product = jnp.dot(normed, weight, preferred_element_type=jnp.float32)]
    ppermute x0 -> x14, waiting for transfers between devices: none -> 21.5 us  [the longest x4 14.8 us: shift_y(): return lax.ppermute(value, 'kv', pairs)]
    while x2 -> x0, local copies, waits for them, and re-layouts: 19.4 us -> none  [combined_all(): return lax.fori_loop(1, lax.axis_size(axis), turn, initial)]
  transfers between devices with their start and end apart: 3 -> 16, of which waited for: 2 -> 6; matrix products, arithmetic and copies ran while one was open for 5% -> 1% of each run, Pallas kernels for 0% -> 15%
where the time goes in v2:
time: 98 us; the launch traced here: 97.3 us
  starting transfers between devices  33.8 us (34%)
  waiting for transfers between devices  29.3 us (30%)
  Pallas kernels  28.1 us (29%)
  local copies, waits for them, and re-layouts  3.43 us (4%)
  between operations  1.6 us (2%)
  other arithmetic  1.07 us (1%)
    ppermute x4, waiting for transfers between devices, shift_y(): return lax.ppermute(value, 'kv', pairs)  14.8 us
    all_to_all x1, starting transfers between devices, body(): queries = lax.all_to_all(queries, 'blk', 0, 0)  12.3 us
    pallas_call x1, Pallas kernels, projections(): pl.pallas_call(projection_kernel, in_specs=[smem, anywhere, anywhere, vme...  9.69 us
    all_to_all x1, waiting for transfers between devices, body(): parts = lax.all_to_all(parts, 'blk', 0, 0)  7.76 us
    ppermute x4, starting transfers between devices, shift_y(): return lax.ppermute(value, 'kv', pairs)  6.66 us
    all_to_all x1, starting transfers between devices, body(): parts = lax.all_to_all(parts, 'blk', 0, 0)  6.48 us
    pallas_call x2, Pallas kernels, output_projection(): pl.pallas_call(functools.partial(output_kernel, shares), in_specs=[vmem]...  5.74 us
    ppermute x1, waiting for transfers between devices, body(): second = lax.ppermute(held, 'blk', [(0, 1), (3, 4), (5, 6)])  5.51 us
  transfers between devices with their start and end apart: 16, of which 6 were waited for; matrix products, arithmetic and copies ran while one was open for 1% of the time, Pallas kernels for 15%

profile of v2, /device:TPU:32, one launch (start us, length us, event | category | flops | bytes accessed | tf_op | source)
XLA Modules:
  0.0 97.3 jit_solution(15932689894723131927)
XLA Ops:
  0.6 9.7 %projections.1 = (bf16[4,512,128]{2,1,0:T(8,128)(2,1)}, bf16[512,256]{1,0:T(8,128)(2,1)}, bf16[32,8,512]{2,1,0:T(8,128)(2,1)}, bf16[8,256]{1,0:T(8,128)(2,1)}) custom-call(s32[32]{0:T(128)} %len_ref.5, bf16[512,4096]{1,0:T(8,128)(2,1)} %x_hbm.1, bf16[8,4096]{1,0:T(8,128)(2,1)} %question_hbm.1, f32[1,4096]{1,0:T(1,128)} %bitcast.1, bf16[4096,512]{1,0:T(8,128)(2,1)} %wq_hbm.1, ...), custom_call_target="tpu_custom_call" | custom-call | flops 3221225472 | bytes 12582912 | tf_op jit(solution)/shard_map/projections/pallas_call | solution.py:186
  10.3 0.8 collective-permute-start.1
  11.2 0.7 collective-permute-start
  11.9 12.3 %all-to-all-start = ((bf16[32,8,512]{2,1,0:T(8,128)(2,1)}), bf16[32,8,512]{2,1,0:T(8,128)(2,1)S(1)}, u32[]{:S(2)}, u32[]{:S(2)}) async-start(bf16[32,8,512]{2,1,0:T(8,128)(2,1)} %get-tuple-element.22), calls=%async_computation | async-start | bytes 524288 | tf_op jit(solution)/shard_map/all_to_all | solution.py:498
  24.2 0.8 collective-permute-start.3
  25.1 1.3 %collective-permute-start.2 = (bf16[512,256]{1,0:T(8,128)(2,1)S(1)}, bf16[512,256]{1,0:T(8,128)(2,1)S(1)}, u32[]{:S(2)}, u32[]{:S(2)}) collective-permute-start(bf16[512,256]{1,0:T(8,128)(2,1)S(1)} %add_add_fusion.1._.refs_0_), channel_id=1, source_target_pairs={{0,8},{24,32},{40,48},{1,9},{25,33},{41,49},{2,10},{26,34},{42,50}... | collective-permute-start | bytes 786440 | tf_op jit(solution)/shard_map/ppermute | solution.py:502
  26.4 4.2 %columns.1 = (bf16[4,512,512]{2,1,0:T(8,128)(2,1)}, bf16[4,512,512]{2,1,0:T(8,128)(2,1)}) custom-call(bf16[512,4096]{1,0:T(8,128)(2,1)} %w_hbm.1, bf16[512,256]{1,0:T(8,128)(2,1)} %copy-done), custom_call_target="tpu_custom_call" | custom-call | bytes 8388608 | tf_op jit(solution)/shard_map/columns/pallas_call | solution.py:229
  30.6 1.8 %own_attention.1 = (f32[4,512,128]{2,1,0:T(8,128)S(1)}, f32[4,512,128]{2,1,0:T(8,128)S(1)}) custom-call(bf16[4,512,128]{2,1,0:T(8,128)(2,1)S(1)} %copy-done.9, bf16[512,256]{1,0:T(8,128)(2,1)S(1)} %copy-done.5, bf16[4,512,512]{2,1,0:T(8,128)(2,1)} %get-tuple-element.19._), custom_call_target="tpu_custom_call" | custom-call | flops 1073741824 | bytes 3145728 | tf_op jit(solution)/shard_map/own_attention/pallas_call | solution.py:266
  32.5 5.5 %collective-permute-done.2.refs_1_ = bf16[512,256]{1,0:T(8,128)(2,1)S(1)} collective-permute-done((bf16[512,256]{1,0:T(8,128)(2,1)S(1)}, bf16[512,256]{1,0:T(8,128)(2,1)S(1)}, u32[]{:S(2)}, u32[]{:S(2)}) %collective-permute-start.2) | collective-permute-done | bytes 262176 | tf_op jit(solution)/shard_map/ppermute | solution.py:502
  38.0 0.9 copy-done.1
  39.1 1.3 %collective-permute-start.6 = (bf16[512,256]{1,0:T(8,128)(2,1)S(1)}, bf16[512,256]{1,0:T(8,128)(2,1)S(1)}, u32[]{:S(2)}, u32[]{:S(2)}) collective-permute-start(bf16[512,256]{1,0:T(8,128)(2,1)S(1)} %sum_of.1), channel_id=1, source_target_pairs={{0,192},{8,200},{16,208},{24,216},{32,224},{40,232},{48,240},{56,2... | collective-permute-start | bytes 786440 | tf_op jit(solution)/shard_map/ppermute | solution.py:507
  40.4 1.3 %collective-permute-start.5 = (bf16[512,256]{1,0:T(8,128)(2,1)S(1)}, bf16[512,256]{1,0:T(8,128)(2,1)S(1)}, u32[]{:S(2)}, u32[]{:S(2)}) collective-permute-start(bf16[512,256]{1,0:T(8,128)(2,1)S(1)} %sum_of.1), channel_id=1, source_target_pairs={{0,128},{8,136},{16,144},{24,152},{32,160},{40,168},{48,176},{56,1... | collective-permute-start | bytes 786440 | tf_op jit(solution)/shard_map/ppermute | solution.py:507
  41.7 2.0 %collective-permute-start.4 = (bf16[512,256]{1,0:T(8,128)(2,1)S(1)}, bf16[512,256]{1,0:T(8,128)(2,1)}, u32[]{:S(2)}, u32[]{:S(2)}) collective-permute-start(bf16[512,256]{1,0:T(8,128)(2,1)S(1)} %sum_of.1), channel_id=1, source_target_pairs={{0,64},{8,72},{16,80},{24,88},{32,96},{40,104},{48,112},{56,120},{... | collective-permute-start | bytes 786440 | tf_op jit(solution)/shard_map/ppermute | solution.py:507
  43.7 2.8 %question_attention.1 = bf16[32,8,640]{2,1,0:T(8,128)(2,1)} custom-call(s32[32]{0:T(128)S(1)} %copy-done.6, bf16[32,8,512]{2,1,0:T(8,128)(2,1)S(1)} %all-to-all-done.queries_ref, bf16[512,256]{1,0:T(8,128)(2,1)S(1)} %copy-done.5, bf16[8,256]{1,0:T(8,128)(2,1)S(1)} %copy-done.10), custom_call_target="tpu_custom_call" | custom-call | flops 671088640 | bytes 1048576 | tf_op jit(solution)/shard_map/question_attention/pallas_call | solution.py:313
  46.6 6.5 %all-to-all-start.1 = ((bf16[32,8,640]{2,1,0:T(8,128)(2,1)}), bf16[32,8,640]{2,1,0:T(8,128)(2,1)S(1)}, u32[]{:S(2)}, u32[]{:S(2)}) async-start(bf16[32,8,640]{2,1,0:T(8,128)(2,1)} %question_attention.1), calls=%async_computation.1 | async-start | bytes 655360 | tf_op jit(solution)/shard_map/all_to_all | solution.py:509
  53.1 1.0 %add_add_fusion.akv_ref = bf16[512,256]{1,0:T(8,128)(2,1)S(1)} fusion(bf16[512,256]{1,0:T(8,128)(2,1)S(1)} %collective-permute-done.6, bf16[512,256]{1,0:T(8,128)(2,1)S(1)} %collective-permute-done.5, bf16[512,256]{1,0:T(8,128)(2,1)} %collective-permute-done.4, bf16[512,256]{1,0:T(8,128)(2,1)S(1)} %sum_of.1, pred[]{:T(512)S(6)} %lt.3), kind=kLoop, calls=%fused_computation | loop fusion | flops 524288 | bytes 1310721 | tf_op jit(solution)/shard_map/add | solution.py:507
  54.2 1.2 %copy-done.4 = f32[4,512,128]{2,1,0:T(8,128)S(1)} copy-done((f32[4,512,128]{2,1,0:T(8,128)S(1)}, f32[4,512,128]{2,1,0:T(8,128)}, u32[]{:S(2)}) %copy-start.4) | copy-done | bytes 1048600
  55.4 1.2 %copy-done.8 = f32[4,512,128]{2,1,0:T(8,128)S(1)} copy-done((f32[4,512,128]{2,1,0:T(8,128)S(1)}, f32[4,512,128]{2,1,0:T(8,128)}, u32[]{:S(2)}) %copy-start.8) | copy-done | bytes 1048600
  56.6 2.2 %context_attention.1._.refs_0_ = bf16[512,512]{1,0:T(8,128)(2,1)S(1)} custom-call(s32[32]{0:T(128)S(1)} %copy-done.6, bf16[4,512,128]{2,1,0:T(8,128)(2,1)S(1)} %copy-done.9, f32[4,512,128]{2,1,0:T(8,128)S(1)} %copy-done.4, f32[4,512,128]{2,1,0:T(8,128)S(1)} %copy-done.8, bf16[512,256]{1,0:T(8,128)(2,1)S(1)} %add_add_fusion.akv_ref), custom_call_target="tpu_custom_call" | custom-call | flops 21474836480 | bytes 4194304 | tf_op jit(solution)/shard_map/context_attention/pallas_call | solution.py:379
  59.6 7.8 %all-to-all-done.1.parts_ref = bf16[32,8,640]{2,1,0:T(8,128)(2,1)S(1)} async-done(((bf16[32,8,640]{2,1,0:T(8,128)(2,1)}), bf16[32,8,640]{2,1,0:T(8,128)(2,1)S(1)}, u32[]{:S(2)}, u32[]{:S(2)}) %all-to-all-start.1) | async-done | bytes 327712 | tf_op jit(solution)/shard_map/all_to_all | solution.py:509
  67.3 0.4 merge_questions.1.refs_1_
  67.8 1.2 %collective-permute-done.8.refs_3_ = bf16[16,512]{1,0:T(8,128)(2,1)S(1)} collective-permute-done((bf16[16,512]{1,0:T(8,128)(2,1)S(1)}, bf16[16,512]{1,0:T(8,128)(2,1)S(1)}, u32[]{:S(2)}, u32[]{:S(2)}) %collective-permute-start.8) | collective-permute-done | bytes 16416 | tf_op jit(solution)/shard_map/ppermute | solution.py:485
  69.0 2.3 %output_projection.3 = (bf16[272,512]{1,0:T(8,128)(2,1)S(1)}, bf16[256,512]{1,0:T(8,128)(2,1)S(1)}) custom-call(bf16[512,512]{1,0:T(8,128)(2,1)S(1)} %context_attention.1._.refs_0_, bf16[16,512]{1,0:T(8,128)(2,1)S(1)} %merge_questions.1.refs_1_, bf16[512,512]{1,0:T(8,128)(2,1)S(1)} %collective-permute-done.7.refs_2_, ...), custom_call_target="tpu_custom_call" | custom-call | flops 553648128 | bytes 3145728 | tf_op jit(solution)/shard_map/output_projection/pallas_call | solution.py:407
  71.3 1.6 %collective-permute-start.10 = (bf16[272,512]{1,0:T(8,128)(2,1)S(1)}, bf16[272,512]{1,0:T(8,128)(2,1)S(1)}, u32[]{:S(2)}, u32[]{:S(2)}) collective-permute-start(bf16[272,512]{1,0:T(8,128)(2,1)S(1)} %get-tuple-element.28), channel_id=1, source_target_pairs={{0,2},{1,3},{2,4},{3,5},{4,6},{5,7},{6,0},{7,1},{8,10},{9,11},{10,... | collective-permute-start | bytes 835592 | tf_op jit(solution)/shard_map/ppermute | solution.py:480
  72.9 1.7 %collective-permute-start.11 = (bf16[256,512]{1,0:T(8,128)(2,1)S(1)}, bf16[256,512]{1,0:T(8,128)(2,1)S(1)}, u32[]{:S(2)}, u32[]{:S(2)}) collective-permute-start(bf16[256,512]{1,0:T(8,128)(2,1)S(1)} %get-tuple-element.29), channel_id=1, source_target_pairs={{0,6},{1,7},{2,0},{3,1},{4,2},{5,3},{6,4},{7,5},{8,14},{9,15},{10,... | collective-permute-start | bytes 786440 | tf_op jit(solution)/shard_map/ppermute | solution.py:480
  74.6 3.4 %output_projection.2 = (bf16[528,512]{1,0:T(8,128)(2,1)S(1)}, bf16[528,512]{1,0:T(8,128)(2,1)S(1)}, bf16[528,512]{1,0:T(8,128)(2,1)S(1)}) custom-call(bf16[512,512]{1,0:T(8,128)(2,1)S(1)} %context_attention.1._.refs_0_, bf16[16,512]{1,0:T(8,128)(2,1)S(1)} %merge_questions.1.refs_1_, bf16[512,512]{1,0:T(8,128)(2,1)S(1)} %collective-permute-done.7.refs_2_, ...), custom_call_target="tpu_custom_call" | custom-call | flops 1660944384 | bytes 3145728 | tf_op jit(solution)/shard_map/output_projection/pallas_call | solution.py:407
  78.1 3.0 %collective-permute-done.11.second_ref = bf16[256,512]{1,0:T(8,128)(2,1)S(1)} collective-permute-done((bf16[256,512]{1,0:T(8,128)(2,1)S(1)}, bf16[256,512]{1,0:T(8,128)(2,1)S(1)}, u32[]{:S(2)}, u32[]{:S(2)}) %collective-permute-start.11) | collective-permute-done | bytes 262176 | tf_op jit(solution)/shard_map/ppermute | solution.py:480
  81.0 0.3 collective-permute-done.10.first_ref
  81.5 1.3 %collective-permute-start.12 = (bf16[528,512]{1,0:T(8,128)(2,1)S(1)}, bf16[528,512]{1,0:T(8,128)(2,1)S(1)}, u32[]{:S(2)}, u32[]{:S(2)}) collective-permute-start(bf16[528,512]{1,0:T(8,128)(2,1)S(1)} %get-tuple-element.30), channel_id=1, source_target_pairs={{0,2},{1,3},{2,4},{3,5},{4,6},{5,7},{6,0},{7,1},{8,10},{9,11},{10,... | collective-permute-start | bytes 1622024 | tf_op jit(solution)/shard_map/ppermute | solution.py:480
  82.8 2.0 %collective-permute-start.13 = (bf16[528,512]{1,0:T(8,128)(2,1)S(1)}, bf16[528,512]{1,0:T(8,128)(2,1)S(1)}, u32[]{:S(2)}, u32[]{:S(2)}) collective-permute-start(bf16[528,512]{1,0:T(8,128)(2,1)S(1)} %get-tuple-element.31), channel_id=1, source_target_pairs={{0,6},{1,7},{2,0},{3,1},{4,2},{5,3},{6,4},{7,5},{8,14},{9,15},{10,... | collective-permute-start | bytes 1622024 | tf_op jit(solution)/shard_map/ppermute | solution.py:480
  84.8 11.6 %collective-permute-done.12.left_ref = bf16[528,512]{1,0:T(8,128)(2,1)S(1)} collective-permute-done((bf16[528,512]{1,0:T(8,128)(2,1)S(1)}, bf16[528,512]{1,0:T(8,128)(2,1)S(1)}, u32[]{:S(2)}, u32[]{:S(2)}) %collective-permute-start.12) | collective-permute-done | bytes 540704 | tf_op jit(solution)/shard_map/ppermute | solution.py:480
  96.4 1.0 %finish.1 = (bf16[512,512]{1,0:T(8,128)(2,1)}, bf16[8,512]{1,0:T(8,128)(2,1)}) custom-call(bf16[528,512]{1,0:T(8,128)(2,1)S(1)} %get-tuple-element.25.own_ref, bf16[528,512]{1,0:T(8,128)(2,1)S(1)} %collective-permute-done.12.left_ref, bf16[528,512]{1,0:T(8,128)(2,1)S(1)} %collective-permute-done.13.right_ref), custom_call_target="tpu_custom_call" | custom-call | flops 786432 | bytes 2097152 | tf_op jit(solution)/shard_map/finish/pallas_call | solution.py:445
  (35 shorter events, 0.5 us)
Async XLA Ops:
  10.3 20.3 %copy-start.5 = (bf16[512,256]{1,0:T(8,128)(2,1)S(1)}, bf16[512,256]{1,0:T(8,128)(2,1)}, u32[]{:S(2)}) copy-start(bf16[512,256]{1,0:T(8,128)(2,1)} %get-tuple-element.18.kv_ref) | copy-start | bytes 786436
  10.3 20.3 %copy-start.9 = (bf16[4,512,128]{2,1,0:T(8,128)(2,1)S(1)}, bf16[4,512,128]{2,1,0:T(8,128)(2,1)}, u32[]{:S(2)}) copy-start(bf16[4,512,128]{2,1,0:T(8,128)(2,1)} %get-tuple-element.17.q_ref) | copy-start | bytes 1572868
  10.3 13.8 %collective-permute-start.1 = (bf16[512,256]{1,0:T(8,128)(2,1)}, bf16[512,256]{1,0:T(8,128)(2,1)S(1)}, u32[]{:S(2)}, u32[]{:S(2)}) collective-permute-start(bf16[512,256]{1,0:T(8,128)(2,1)} %get-tuple-element.18.kv_ref), channel_id=1, source_target_pairs={{0,40},{1,41},{2,42},{3,43},{4,44},{5,45},{6,46},{7,47}} | collective-permute-start | bytes 786440 | tf_op jit(solution)/shard_map/ppermute | solution.py:497
  11.2 13.0 %collective-permute-start = (bf16[512,256]{1,0:T(8,128)(2,1)}, bf16[512,256]{1,0:T(8,128)(2,1)S(1)}, u32[]{:S(2)}, u32[]{:S(2)}) collective-permute-start(bf16[512,256]{1,0:T(8,128)(2,1)} %get-tuple-element.18.kv_ref), channel_id=1, source_target_pairs={{0,24},{1,25},{2,26},{3,27},{4,28},{5,29},{6,30},{7,31}} | collective-permute-start | bytes 786440 | tf_op jit(solution)/shard_map/ppermute | solution.py:497
  11.9 31.9 %all-to-all-start = ((bf16[32,8,512]{2,1,0:T(8,128)(2,1)}), bf16[32,8,512]{2,1,0:T(8,128)(2,1)S(1)}, u32[]{:S(2)}, u32[]{:S(2)}) async-start(bf16[32,8,512]{2,1,0:T(8,128)(2,1)} %get-tuple-element.22), calls=%async_computation | async-start | bytes 524288 | tf_op jit(solution)/shard_map/all_to_all | solution.py:498
  24.2 2.2 %copy-start = (bf16[512,256]{1,0:T(8,128)(2,1)}, bf16[512,256]{1,0:T(8,128)(2,1)S(1)}, u32[]{:S(2)}) copy-start(bf16[512,256]{1,0:T(8,128)(2,1)S(1)} %add_add_fusion.1._.refs_0_) | copy-start | bytes 786436
  24.2 19.5 %copy-start.6 = (s32[32]{0:T(128)S(1)}, s32[32]{0:T(128)}, u32[]{:S(2)}) copy-start(s32[32]{0:T(128)} %len_ref.5) | copy-start | bytes 388
  24.2 19.5 %copy-start.10 = (bf16[8,256]{1,0:T(8,128)(2,1)S(1)}, bf16[8,256]{1,0:T(8,128)(2,1)}, u32[]{:S(2)}) copy-start(bf16[8,256]{1,0:T(8,128)(2,1)} %get-tuple-element.23.own_ref) | copy-start | bytes 12292
  24.2 8.3 %collective-permute-start.3 = (bf16[512,256]{1,0:T(8,128)(2,1)S(1)}, bf16[512,256]{1,0:T(8,128)(2,1)S(1)}, u32[]{:S(2)}, u32[]{:S(2)}) collective-permute-start(bf16[512,256]{1,0:T(8,128)(2,1)S(1)} %add_add_fusion.1._.refs_0_), channel_id=1, source_target_pairs={{0,56},{24,16},{1,57},{25,17},{2,58},{26,18},{3,59},{27,19},{4,60}... | collective-permute-start | bytes 786440 | tf_op jit(solution)/shard_map/ppermute | solution.py:503
  25.1 13.0 %collective-permute-start.2 = (bf16[512,256]{1,0:T(8,128)(2,1)S(1)}, bf16[512,256]{1,0:T(8,128)(2,1)S(1)}, u32[]{:S(2)}, u32[]{:S(2)}) collective-permute-start(bf16[512,256]{1,0:T(8,128)(2,1)S(1)} %add_add_fusion.1._.refs_0_), channel_id=1, source_target_pairs={{0,8},{24,32},{40,48},{1,9},{25,33},{41,49},{2,10},{26,34},{42,50}... | collective-permute-start | bytes 786440 | tf_op jit(solution)/shard_map/ppermute | solution.py:502
  32.5 6.6 %copy-start.3 = (f32[4,512,128]{2,1,0:T(8,128)}, f32[4,512,128]{2,1,0:T(8,128)S(1)}, u32[]{:S(2)}) copy-start(f32[4,512,128]{2,1,0:T(8,128)S(1)} %get-tuple-element.20.refs_3_.o_ref) | copy-start | bytes 3145732
  32.5 21.7 %copy-start.7 = (f32[4,512,128]{2,1,0:T(8,128)}, f32[4,512,128]{2,1,0:T(8,128)S(1)}, u32[]{:S(2)}) copy-start(f32[4,512,128]{2,1,0:T(8,128)S(1)} %get-tuple-element.21.lse_ref) | copy-start | bytes 3145732
  38.0 1.0 copy-start.1
  39.1 14.0 %collective-permute-start.6 = (bf16[512,256]{1,0:T(8,128)(2,1)S(1)}, bf16[512,256]{1,0:T(8,128)(2,1)S(1)}, u32[]{:S(2)}, u32[]{:S(2)}) collective-permute-start(bf16[512,256]{1,0:T(8,128)(2,1)S(1)} %sum_of.1), channel_id=1, source_target_pairs={{0,192},{8,200},{16,208},{24,216},{32,224},{40,232},{48,240},{56,2... | collective-permute-start | bytes 786440 | tf_op jit(solution)/shard_map/ppermute | solution.py:507
  40.4 12.7 %collective-permute-start.5 = (bf16[512,256]{1,0:T(8,128)(2,1)S(1)}, bf16[512,256]{1,0:T(8,128)(2,1)S(1)}, u32[]{:S(2)}, u32[]{:S(2)}) collective-permute-start(bf16[512,256]{1,0:T(8,128)(2,1)S(1)} %sum_of.1), channel_id=1, source_target_pairs={{0,128},{8,136},{16,144},{24,152},{32,160},{40,168},{48,176},{56,1... | collective-permute-start | bytes 786440 | tf_op jit(solution)/shard_map/ppermute | solution.py:507
  41.7 11.4 %collective-permute-start.4 = (bf16[512,256]{1,0:T(8,128)(2,1)S(1)}, bf16[512,256]{1,0:T(8,128)(2,1)}, u32[]{:S(2)}, u32[]{:S(2)}) collective-permute-start(bf16[512,256]{1,0:T(8,128)(2,1)S(1)} %sum_of.1), channel_id=1, source_target_pairs={{0,64},{8,72},{16,80},{24,88},{32,96},{40,104},{48,112},{56,120},{... | collective-permute-start | bytes 786440 | tf_op jit(solution)/shard_map/ppermute | solution.py:507
  43.7 25.2 %collective-permute-start.9 = (bf16[4,512,512]{2,1,0:T(8,128)(2,1)}, bf16[4,512,512]{2,1,0:T(8,128)(2,1)}, u32[]{:S(2)}, u32[]{:S(2)}) collective-permute-start(bf16[4,512,512]{2,1,0:T(8,128)(2,1)} %get-tuple-element.19._), channel_id=1, source_target_pairs={{0,1},{1,0},{2,3},{3,2},{4,5},{5,4},{6,7},{7,6},{8,9},{9,8},{10,11... | collective-permute-start | bytes 6291464 | tf_op jit(solution)/shard_map/ppermute | solution.py:485
  46.6 20.7 %all-to-all-start.1 = ((bf16[32,8,640]{2,1,0:T(8,128)(2,1)}), bf16[32,8,640]{2,1,0:T(8,128)(2,1)S(1)}, u32[]{:S(2)}, u32[]{:S(2)}) async-start(bf16[32,8,640]{2,1,0:T(8,128)(2,1)} %question_attention.1), calls=%async_computation.1 | async-start | bytes 655360 | tf_op jit(solution)/shard_map/all_to_all | solution.py:509
  54.1 1.2 %copy-start.4 = (f32[4,512,128]{2,1,0:T(8,128)S(1)}, f32[4,512,128]{2,1,0:T(8,128)}, u32[]{:S(2)}) copy-start(f32[4,512,128]{2,1,0:T(8,128)} %copy-done.3) | copy-start | bytes 3145732
  55.4 1.2 %copy-start.8 = (f32[4,512,128]{2,1,0:T(8,128)S(1)}, f32[4,512,128]{2,1,0:T(8,128)}, u32[]{:S(2)}) copy-start(f32[4,512,128]{2,1,0:T(8,128)} %copy-done.7) | copy-start | bytes 3145732
  56.6 12.4 %copy-start.2 = (bf16[4,512,512]{2,1,0:T(8,128)(2,1)S(1)}, bf16[4,512,512]{2,1,0:T(8,128)(2,1)}, u32[]{:S(2)}) copy-start(bf16[4,512,512]{2,1,0:T(8,128)(2,1)} %get-tuple-element.24.refs_4_) | copy-start | bytes 6291460
  58.8 10.1 %collective-permute-start.7 = (bf16[512,512]{1,0:T(8,128)(2,1)S(1)}, bf16[512,512]{1,0:T(8,128)(2,1)S(1)}, u32[]{:S(2)}, u32[]{:S(2)}) collective-permute-start(bf16[512,512]{1,0:T(8,128)(2,1)S(1)} %context_attention.1._.refs_0_), channel_id=1, source_target_pairs={{0,1},{1,0},{2,3},{3,2},{4,5},{5,4},{6,7},{7,6},{8,9},{9,8},{10,11... | collective-permute-start | bytes 1572872 | tf_op jit(solution)/shard_map/ppermute | solution.py:485
  67.7 1.3 %collective-permute-start.8 = (bf16[16,512]{1,0:T(8,128)(2,1)S(1)}, bf16[16,512]{1,0:T(8,128)(2,1)S(1)}, u32[]{:S(2)}, u32[]{:S(2)}) collective-permute-start(bf16[16,512]{1,0:T(8,128)(2,1)S(1)} %merge_questions.1.refs_1_), channel_id=1, source_target_pairs={{0,1},{1,0},{2,3},{3,2},{4,5},{5,4},{6,7},{7,6},{8,9},{9,8},{10,11... | collective-permute-start | bytes 49160 | tf_op jit(solution)/shard_map/ppermute | solution.py:485
  71.3 10.1 %collective-permute-start.10 = (bf16[272,512]{1,0:T(8,128)(2,1)S(1)}, bf16[272,512]{1,0:T(8,128)(2,1)S(1)}, u32[]{:S(2)}, u32[]{:S(2)}) collective-permute-start(bf16[272,512]{1,0:T(8,128)(2,1)S(1)} %get-tuple-element.28), channel_id=1, source_target_pairs={{0,2},{1,3},{2,4},{3,5},{4,6},{5,7},{6,0},{7,1},{8,10},{9,11},{10,... | collective-permute-start | bytes 835592 | tf_op jit(solution)/shard_map/ppermute | solution.py:480
  72.9 8.1 %collective-permute-start.11 = (bf16[256,512]{1,0:T(8,128)(2,1)S(1)}, bf16[256,512]{1,0:T(8,128)(2,1)S(1)}, u32[]{:S(2)}, u32[]{:S(2)}) collective-permute-start(bf16[256,512]{1,0:T(8,128)(2,1)S(1)} %get-tuple-element.29), channel_id=1, source_target_pairs={{0,6},{1,7},{2,0},{3,1},{4,2},{5,3},{6,4},{7,5},{8,14},{9,15},{10,... | collective-permute-start | bytes 786440 | tf_op jit(solution)/shard_map/ppermute | solution.py:480
  81.5 14.9 %collective-permute-start.12 = (bf16[528,512]{1,0:T(8,128)(2,1)S(1)}, bf16[528,512]{1,0:T(8,128)(2,1)S(1)}, u32[]{:S(2)}, u32[]{:S(2)}) collective-permute-start(bf16[528,512]{1,0:T(8,128)(2,1)S(1)} %get-tuple-element.30), channel_id=1, source_target_pairs={{0,2},{1,3},{2,4},{3,5},{4,6},{5,7},{6,0},{7,1},{8,10},{9,11},{10,... | collective-permute-start | bytes 1622024 | tf_op jit(solution)/shard_map/ppermute | solution.py:480
  82.8 13.5 %collective-permute-start.13 = (bf16[528,512]{1,0:T(8,128)(2,1)S(1)}, bf16[528,512]{1,0:T(8,128)(2,1)S(1)}, u32[]{:S(2)}, u32[]{:S(2)}) collective-permute-start(bf16[528,512]{1,0:T(8,128)(2,1)S(1)} %get-tuple-element.31), channel_id=1, source_target_pairs={{0,6},{1,7},{2,0},{3,1},{4,2},{5,3},{6,4},{7,5},{8,14},{9,15},{10,... | collective-permute-start | bytes 1622024 | tf_op jit(solution)/shard_map/ppermute | solution.py:480

commit v3 on v2

v3 whole, which is shorter than its diff:
```python
import functools

import jax
import jax.numpy as jnp
import numpy as np
from jax import lax
from jax.experimental import pallas as pl
from jax.experimental.pallas import tpu as pltpu
from jax.sharding import PartitionSpec as P

HD = 128
HEADS = 4
BLK = 512
QROWS = 8
NX, NZ, NY, NC = 4, 8, 4, 2
N_BLK, N_KV = NX * NZ, NY * NC
QN = N_BLK * QROWS
D = 4096
FEAT = D // N_KV
KC = 1024
ROWS = 256
QPAD = 16
CONTEXT_LIMIT = 58

epsilon = 1e-05
rope_base = 500000.0
masked_score = -1e30
q_scale = float(HD**-0.5 * np.log2(np.e))
log2_e = float(np.log2(np.e))

bf16 = jnp.bfloat16
f32 = jnp.float32


def angle_tables(positions):
    inverse_freq = rope_base ** (-2.0 * np.arange(HD // 2, dtype=np.float64) / HD)
    angles = np.asarray(positions, np.float64)[:, None] * inverse_freq[None, :]
    angles = np.concatenate([angles, angles], 1)
    return np.cos(angles).astype(np.float32), np.sin(angles).astype(np.float32)


def params(limit=24):
    return pltpu.CompilerParams(vmem_limit_bytes=limit * 2**20)


def cost(flops, bytes_accessed, transcendentals=0):
    return pl.CostEstimate(
        flops=flops, bytes_accessed=bytes_accessed, transcendentals=transcendentals
    )


def add_angles(first, second):
    return (
        first[0] * second[0] - first[1] * second[1],
        first[1] * second[0] + first[0] * second[1],
    )


def rotated(head, cosine, sine_signed):
    return head * cosine + pltpu.roll(head, HD // 2, 1) * sine_signed


def signed(sine):
    lane = lax.broadcasted_iota(jnp.int32, sine.shape, 1)
    return jnp.where(lane < HD // 2, -sine, sine)


def dot(a, b):
    return jnp.dot(a, b, preferred_element_type=f32)


def dot_t(a, b):
    return lax.dot_general(a, b, (((1,), (1,)), ((), ())), preferred_element_type=f32)


def lane_folded(values):
    total = values[:, :HD]
    for part in range(1, values.shape[1] // HD):
        total = total + values[:, part * HD : (part + 1) * HD]
    return total


def squares_to_factor(squares):
    mean = jnp.sum(squares, axis=-1, keepdims=True) * (1.0 / D)
    return lax.rsqrt(mean + epsilon)


smem = pl.BlockSpec(memory_space=pltpu.SMEM)
vmem = pl.BlockSpec(memory_space=pltpu.VMEM)
anywhere = pl.BlockSpec(memory_space=pl.ANY)


def with_ones(values):
    return jnp.concatenate([values, jnp.ones_like(values)], axis=1)


def projection_kernel(
    len_ref, x_hbm, question_hbm, gain_ref, wq_hbm, wk_hbm, wv_hbm, ct_hbm, st_hbm, cb_ref, sb_ref,
    q_ref, kv_ref, queries_ref, own_ref, ct_ref, st_ref, table_sems,
    x_ref, question_ref, wq_ref, wk_ref, wv_ref, scaled_ref, acc_ref, sq_ref, sems, question_sem,
):
    blk_at = lax.axis_index("blk")
    steps = D // KC
    width = HEADS * HD

    def copies(k):
        part = pl.ds(pl.multiple_of(k * KC, KC), KC)
        return [
            pltpu.make_async_copy(x_hbm.at[:, part], x_ref.at[:, part], sems.at[k, 0]),
            pltpu.make_async_copy(wq_hbm.at[part, :], wq_ref.at[part, :], sems.at[k, 1]),
            pltpu.make_async_copy(wk_hbm.at[part, :], wk_ref.at[part, :], sems.at[k, 2]),
            pltpu.make_async_copy(wv_hbm.at[part, :], wv_ref.at[part, :], sems.at[k, 3]),
        ]

    question_copy = pltpu.make_async_copy(question_hbm, question_ref, question_sem)
    question_copy.start()
    for k in range(2):
        for copy in copies(k):
            copy.start()
    table_copies = [
        pltpu.make_async_copy(ct_hbm, ct_ref, table_sems.at[0]),
        pltpu.make_async_copy(st_hbm, st_ref, table_sems.at[1]),
    ]
    for copy in table_copies:
        copy.start()
    acc_ref[...] = jnp.zeros_like(acc_ref)
    sq_ref[...] = jnp.zeros_like(sq_ref)
    question_copy.wait()

    def turn(k, _):
        for copy in copies(k):
            copy.wait()

        @pl.when(k + 2 < steps)
        def _():
            for copy in copies(k + 2):
                copy.start()

        part = pl.ds(pl.multiple_of(k * KC, KC), KC)
        gain = gain_ref[:, part]
        x = x_ref[:, part].astype(f32)
        sq_ref[:BLK] += lane_folded(x * x)
        scaled_ref[:BLK] = (x * gain).astype(bf16)
        x = question_ref[:, part].astype(f32)
        x = jnp.concatenate([x, jnp.zeros((QPAD - QROWS, KC), f32)], 0)
        sq_ref[BLK:] += lane_folded(x * x)
        scaled_ref[BLK:] = (x * gain).astype(bf16)
        acc_ref[:, :width] += dot(scaled_ref[...], wq_ref[part, :])
        acc_ref[:, width:] += dot(scaled_ref[...], jnp.concatenate([wk_ref[part, :], wv_ref[part, :]], axis=1))
        return 0

    lax.fori_loop(0, steps, turn, 0)
    for copy in table_copies:
        copy.wait()

    factor = squares_to_factor(sq_ref[...])
    block = pl.ds(blk_at, 1)
    tokens = (ct_ref[...], st_ref[...])
    cosine, sine = add_angles(tokens, (cb_ref[block, :], sb_ref[block, :]))
    total = len_ref[0]
    for b in range(1, N_BLK):
        total = total + len_ref[b]
    high, low = pl.ds(total // BLK, 1), pl.ds(lax.rem(total, BLK), 1)
    base = add_angles((cb_ref[high, :], sb_ref[high, :]), (ct_ref[low, :], st_ref[low, :]))
    rows = pl.ds(pl.multiple_of(blk_at * QROWS, QROWS), QROWS)
    own_cosine, own_sine = add_angles((ct_ref[rows, :], st_ref[rows, :]), base)

    def heads_of(rows, cosine, sine):
        scale = factor[rows]
        cosine, sine = cosine * scale, signed(sine) * scale
        heads = [acc_ref[rows, h * HD : (h + 1) * HD] for h in range(HEADS + 2)]
        turned = [rotated(head, cosine, sine) for head in heads[: HEADS + 1]]
        return [head * q_scale for head in turned[:HEADS]], turned[HEADS], heads[HEADS + 1] * scale

    queries, key, value = heads_of(slice(0, BLK), cosine, sine)
    for h in range(HEADS):
        q_ref[h] = queries[h].astype(bf16)
    kv_ref[:, :HD] = key.astype(bf16)
    kv_ref[:, HD:] = value.astype(bf16)
    queries, key, value = heads_of(slice(BLK, BLK + QROWS), own_cosine, own_sine)
    own_ref[:, :HD] = key.astype(bf16)
    own_ref[:, HD:] = value.astype(bf16)
    queries = jnp.concatenate(queries, axis=1).astype(bf16)
    for b in range(N_BLK):
        queries_ref[b] = queries


def projections(block_len, context, question, gain, wq, wk, wv, tables):
    return pl.pallas_call(
        projection_kernel,
        in_specs=[smem, anywhere, anywhere, vmem] + [anywhere] * 5 + [vmem] * 2,
        out_specs=[vmem] * 4,
        out_shape=[
            jax.ShapeDtypeStruct((HEADS, BLK, HD), bf16),
            jax.ShapeDtypeStruct((BLK, 2 * HD), bf16),
            jax.ShapeDtypeStruct((N_BLK, QROWS, HEADS * HD), bf16),
            jax.ShapeDtypeStruct((QROWS, 2 * HD), bf16),
        ],
        scratch_shapes=[
            pltpu.VMEM((BLK, HD), f32),
            pltpu.VMEM((BLK, HD), f32),
            pltpu.SemaphoreType.DMA((2,)),
            pltpu.VMEM((BLK, D), bf16),
            pltpu.VMEM((QROWS, D), bf16),
            pltpu.VMEM((D, HEADS * HD), bf16),
            pltpu.VMEM((D, HD), bf16),
            pltpu.VMEM((D, HD), bf16),
            pltpu.VMEM((BLK + QPAD, KC), bf16),
            pltpu.VMEM((BLK + QPAD, (HEADS + 2) * HD), f32),
            pltpu.VMEM((BLK + QPAD, HD), f32),
            pltpu.SemaphoreType.DMA((D // KC, 4)),
            pltpu.SemaphoreType.DMA,
        ],
        compiler_params=params(60),
        cost_estimate=cost(2 * BLK * D * 768, 12 * 2**20),
        name="projections",
    )(block_len, context, question, gain, wq, wk, wv, *tables)


def question_attention_kernel(len_ref, queries_ref, kv_ref, own_ref, out_ref, token_ref):
    token_ref[...] = jnp.zeros_like(token_ref)
    blk_at = lax.axis_index("blk")
    live = lax.broadcasted_iota(jnp.int32, (QN, BLK), 1) < len_ref[blk_at]
    question_id = lax.broadcasted_iota(jnp.int32, (QN, HD), 0)
    lane = lax.broadcasted_iota(jnp.int32, (QN, HD), 1)
    seen = (lane < QROWS) & (lane + blk_at * QROWS <= question_id)
    own = jnp.concatenate([own_ref[...].astype(f32), jnp.zeros((HD - QROWS, 2 * HD), f32)], 0)
    own = own.astype(bf16)
    values = with_ones(kv_ref[:, HD:])
    own_values = with_ones(own[:, HD:])
    tile = jnp.zeros((QN, HD), f32)
    for h in range(HEADS):
        cols = slice(h * HD, (h + 1) * HD)
        q = queries_ref[:, :, cols].reshape(QN, HD)
        scores = jnp.where(live, dot_t(q, kv_ref[:, :HD]), masked_score)
        own_scores = jnp.where(seen, dot_t(q, own[:, :HD]), masked_score)
        highest = jnp.maximum(
            jnp.max(scores, axis=-1, keepdims=True), jnp.max(own_scores, axis=-1, keepdims=True)
        )
        mixture = dot(jnp.exp2(scores - highest).astype(bf16), values)
        mixture = mixture + dot(jnp.exp2(own_scores - highest).astype(bf16), own_values)
        totals = mixture[:, HD:]
        out_ref[:, :, cols] = (mixture[:, :HD] / totals).reshape(N_BLK, QROWS, HD)
        lse = highest + jnp.log(totals) * log2_e
        tile = jnp.where(lane // 32 == h, lse, tile)
    out_ref[:, :, HEADS * HD :] = tile.reshape(N_BLK, QROWS, HD)


def question_attention(block_len, queries, kv, own):
    return pl.pallas_call(
        question_attention_kernel,
        out_shape=[
            jax.ShapeDtypeStruct((N_BLK, QROWS, (HEADS + 1) * HD), f32),
            jax.ShapeDtypeStruct((8, HD), f32),
        ],
        in_specs=[smem] + [vmem] * 3,
        out_specs=[vmem] * 2,
        compiler_params=params(),
        cost_estimate=cost(HEADS * QN * 640 * HD * 8, 2**20, HEADS * QN * 640),
        name="question_attention",
    )(block_len, queries, kv, own)


def merged(qlen_ref, parts_ref):
    row = lax.broadcasted_iota(jnp.int32, (QROWS, HD), 0) + lax.axis_index("blk") * QROWS
    valid = row < qlen_ref[0]
    heads = []
    for h in range(HEADS):
        lse = parts_ref[:, :, HEADS * HD + h * 32 : HEADS * HD + h * 32 + 1]
        top = jnp.max(lse, axis=0, keepdims=True)
        share = jnp.exp2(lse - top)
        mixture = jnp.sum(parts_ref[:, :, h * HD : (h + 1) * HD] * share, axis=0)
        heads.append(jnp.where(valid, mixture / jnp.sum(share, axis=0), 0.0))
    rows = jnp.concatenate(heads, axis=1)
    return jnp.concatenate([rows, jnp.zeros((QPAD - QROWS, HEADS * HD), f32)], 0).astype(bf16)


def context_kernel(
    len_ref, q_ref, kv_ref, akv_ref, w_hbm, _, *refs
):
    keep_refs, send_refs, (att_ref, w_ref, sem) = refs[:NY], refs[NY : 2 * NY], refs[2 * NY :]
    blk_at, kv_at = lax.axis_index("blk"), lax.axis_index("kv")
    y_at, c_at = kv_at // NC, lax.rem(kv_at, NC)
    copy = pltpu.make_async_copy(w_hbm, w_ref, sem)
    copy.start()
    first = blk_at == 0
    row = lax.broadcasted_iota(jnp.int32, (ROWS, ROWS), 0)
    causal = lax.broadcasted_iota(jnp.int32, (ROWS, ROWS), 1) <= row
    anchor_values = with_ones(akv_ref[:, HD:])
    values = with_ones(kv_ref[:, HD:])
    for r in range(BLK // ROWS):
        rows, before = slice(r * ROWS, (r + 1) * ROWS), slice(0, r * ROWS)
        valid = lax.broadcasted_iota(jnp.int32, (ROWS, HD), 0) + r * ROWS < len_ref[blk_at]
        for h in range(HEADS):
            q = q_ref[h, rows, :]
            anchor = dot_t(q, akv_ref[:, :HD])
            own = [jnp.where(causal, dot_t(q, kv_ref[rows, :HD]), masked_score)]
            if r:
                own.append(dot_t(q, kv_ref[before, :HD]))
            highest = jnp.max(own[0], axis=-1, keepdims=True)
            for scores in own[1:]:
                highest = jnp.maximum(highest, jnp.max(scores, axis=-1, keepdims=True))
            anchor_highest = jnp.max(anchor, axis=-1, keepdims=True)
            highest = jnp.where(first, highest, jnp.maximum(highest, anchor_highest))
            weights = jnp.exp2(anchor - jnp.where(first, -masked_score, highest))
            mixture = dot(weights.astype(bf16), anchor_values)
            for scores, at in zip(own, (rows, before)):
                mixture = mixture + dot(jnp.exp2(scores - highest).astype(bf16), values[at])
            result = mixture[:, :HD] / mixture[:, HD:]
            att_ref[rows, h * HD : (h + 1) * HD] = jnp.where(valid, result, 0.0).astype(bf16)
    copy.wait()
    for d in range(NY):
        to_y = lax.rem(y_at + d, NY)
        for ref, to_c in ((send_refs[d], 1 - c_at), (keep_refs[d], c_at)):
            columns = pl.ds(pl.multiple_of((to_y * NC + to_c) * FEAT, FEAT), FEAT)
            ref[...] = dot(att_ref[...], w_ref[:, columns]).astype(bf16)


def context_attention(block_len, q, kv, anchor, w_out, after):
    return pl.pallas_call(
        context_kernel,
        in_specs=[smem] + [vmem] * 3 + [anywhere] * 2,
        out_specs=[vmem] * (2 * NY),
        out_shape=[jax.ShapeDtypeStruct((BLK, FEAT), bf16)] * (2 * NY),
        scratch_shapes=[
            pltpu.VMEM((BLK, HEADS * HD), bf16),
            pltpu.VMEM((HEADS * HD, D), bf16),
            pltpu.SemaphoreType.DMA,
        ],
        compiler_params=params(CONTEXT_LIMIT),
        cost_estimate=cost(HEADS * BLK * BLK * HD * 8 * 20, 4 * 2**20, HEADS * BLK * BLK),
        name="context_attention",
    )(block_len, q, kv, anchor, w_out, after)


def question_output_kernel(qlen_ref, parts_ref, w_hbm, _, keep_ref, send_ref, w_ref, sem):
    copy = pltpu.make_async_copy(w_hbm, w_ref, sem)
    copy.start()
    kv_at = lax.axis_index("kv")
    y_at, c_at = kv_at // NC, lax.rem(kv_at, NC)
    rows = merged(qlen_ref, parts_ref)
    copy.wait()
    for d in range(NY):
        to_y = lax.rem(y_at + d, NY)
        for ref, to_c in ((send_ref, 1 - c_at), (keep_ref, c_at)):
            columns = pl.ds(pl.multiple_of((to_y * NC + to_c) * FEAT, FEAT), FEAT)
            ref[d] = dot(rows, w_ref[:, columns]).astype(bf16)


def question_output(question_len, parts, w_out, after):
    return pl.pallas_call(
        question_output_kernel,
        in_specs=[smem, vmem] + [anywhere] * 2,
        out_specs=[vmem] * 2,
        out_shape=[jax.ShapeDtypeStruct((NY, QPAD, FEAT), bf16)] * 2,
        scratch_shapes=[pltpu.VMEM((HEADS * HD, D), bf16), pltpu.SemaphoreType.DMA],
        compiler_params=params(CONTEXT_LIMIT),
        cost_estimate=cost(400 * 256 * HEADS * HD * FEAT * NY, 4 * 2**20),
        name="question_output",
    )(question_len, parts, w_out, after)


def total_of(*parts):
    total = parts[0].astype(f32)
    for part in parts[1:]:
        total = total + part.astype(f32)
    return total.astype(bf16)


def across_kernel(keep_ref, got_ref, first_ref, second_ref):
    first_ref[...] = total_of(keep_ref[:ROWS], got_ref[:ROWS])
    second_ref[...] = total_of(keep_ref[ROWS:], got_ref[ROWS:])


def across_sum(keep, got):
    return pl.pallas_call(
        across_kernel,
        in_specs=[vmem] * 2,
        out_specs=[vmem] * 2,
        out_shape=[jax.ShapeDtypeStruct((ROWS, FEAT), bf16)] * 2,
        compiler_params=params(),
        cost_estimate=cost(0, 0),
        name="across_sum",
    )(keep, got)


def others_kernel(near_keep, near_got, far_keep, far_got, near_a, near_b, far_a, far_b):
    near_a[...] = total_of(near_keep[:ROWS], near_got[:ROWS])
    near_b[...] = total_of(near_keep[ROWS:], near_got[ROWS:])
    far_a[...] = total_of(far_keep[:ROWS], far_got[:ROWS])
    far_b[...] = total_of(far_keep[ROWS:], far_got[ROWS:])


def others_sum(*parts):
    return pl.pallas_call(
        others_kernel,
        in_specs=[vmem] * 4,
        out_specs=[vmem] * 4,
        out_shape=[jax.ShapeDtypeStruct((ROWS, FEAT), bf16)] * 4,
        compiler_params=params(),
        cost_estimate=cost(0, 0),
        name="others_sum",
    )(*parts)


def relay_kernel(
    near_ref, far_ref, first_ref, second_ref, q_keep, q_got, _, __,
    near_out, far_out, q_own_out, q_across_out,
):
    near_out[:ROWS] = total_of(near_ref[...], first_ref[...])
    far_out[:ROWS] = total_of(far_ref[...], second_ref[...])
    for d, out in enumerate((q_own_out, near_out.at[ROWS:], q_across_out, far_out.at[ROWS:])):
        out[...] = total_of(q_keep[d], q_got[d])


def relay(*parts):
    half = jax.ShapeDtypeStruct((ROWS + QPAD, FEAT), bf16)
    return pl.pallas_call(
        relay_kernel,
        in_specs=[vmem] * 6 + [anywhere] * 2,
        out_specs=[vmem] * 4,
        out_shape=[half] * 2 + [jax.ShapeDtypeStruct((QPAD, FEAT), bf16)] * 2,
        compiler_params=params(),
        cost_estimate=cost(BLK * FEAT, BLK * FEAT * 10),
        name="relay",
    )(*parts)


def finish_kernel(
    keep, got, left_a, left_b, right_a, right_b, q_own, q_across, out_ref, question_ref
):
    out_ref[:ROWS] = total_of(keep[:ROWS], got[:ROWS], left_a[:ROWS], right_a[...])
    out_ref[ROWS:] = total_of(keep[ROWS:], got[ROWS:], left_b[...], right_b[:ROWS])
    question = total_of(q_own[...], left_a[ROWS:], right_b[ROWS:], q_across[...])
    question_ref[...] = question[:QROWS]


def finish(*parts):
    return pl.pallas_call(
        finish_kernel,
        in_specs=[vmem] * len(parts),
        out_specs=[vmem] * 2,
        out_shape=[
            jax.ShapeDtypeStruct((BLK, FEAT), bf16),
            jax.ShapeDtypeStruct((QROWS, FEAT), bf16),
        ],
        compiler_params=params(),
        cost_estimate=cost(BLK * FEAT * 4, BLK * FEAT * 10),
        name="finish",
    )(*parts)


def sum_kernel(*refs):
    total = refs[0][...].astype(f32)
    for ref in refs[1:-2]:
        total = total + ref[...].astype(f32)
    refs[-1][...] = total.astype(bf16)


def sum_of(*parts, after):
    return pl.pallas_call(
        sum_kernel,
        in_specs=[vmem] * len(parts) + [anywhere],
        out_specs=vmem,
        out_shape=jax.ShapeDtypeStruct(parts[0].shape, bf16),
        compiler_params=params(),
        cost_estimate=cost(BLK * 256 * 3, BLK * 256 * 8),
        name="sum_of",
    )(*parts, after)


def to_blocks(pairs):
    return [(a * NZ + b, c * NZ + d) for (a, b), (c, d) in pairs.items()]


def shift_y(value, by):
    pairs = [(y * NC + c, (y + by) % NY * NC + c) for y in range(NY) for c in range(NC)]
    return lax.ppermute(value, "kv", pairs)


def swap_cores(value):
    pairs = [(y * NC + c, y * NC + 1 - c) for y in range(NY) for c in range(NC)]
    return lax.ppermute(value, "kv", pairs)


def body(context, question, norm_gain, w_query, w_key, w_value, w_out, block_len, question_len):
    blk_at = lax.axis_index("blk")
    tables = [jnp.asarray(t) for t in angle_tables(np.arange(BLK))]
    tables += [jnp.asarray(t) for t in angle_tables(np.arange(N_BLK + 1) * BLK)]

    q, kv, queries, own_kv = projections(
        block_len, context, question, norm_gain.reshape(1, D), w_query, w_key, w_value, tables
    )
    held = jnp.where(blk_at == 0, kv, jnp.zeros_like(kv))
    held = held + lax.ppermute(kv, "blk", to_blocks({(0, 0): (2, 0)}))
    held = held + lax.ppermute(kv, "blk", to_blocks({(0, 0): (0, 3)}))
    held = held + lax.ppermute(kv, "blk", to_blocks({(0, 0): (0, 5)}))
    queries = lax.all_to_all(queries, "blk", 0, 0)
    within = {(0, 0): (0, 1), (0, 3): (0, 4), (0, 5): (0, 6)}, {(0, 0): (0, 7), (0, 3): (0, 2)}
    second = lax.ppermute(held, "blk", to_blocks({**within[0], (2, 0): (2, 3)}))
    third = lax.ppermute(held, "blk", to_blocks({**within[1], (2, 0): (2, 5)}))
    parts, token = question_attention(block_len, queries, kv, own_kv)
    held = sum_of(held, second, third, after=token)
    anchor = held
    for x, pairs in zip((1, 3), within):
        pairs = {(2, a): (2, b) for (_, a), (_, b) in pairs.items()}
        across = {(0, z): (x, z) for z in range(NZ)}
        anchor = anchor + lax.ppermute(held, "blk", to_blocks({**across, **pairs}))
    parts = lax.all_to_all(parts, "blk", 0, 0)

    products = context_attention(block_len, q, kv, anchor, w_out, token)
    keep, send = products[:NY], products[NY:]
    first, second = across_sum(keep[2], swap_cores(send[2]))
    near_a, near_b, far_a, far_b = others_sum(
        keep[1], swap_cores(send[1]), keep[3], swap_cores(send[3])
    )
    left_b, right_a = shift_y(near_b, 1), shift_y(far_a, 3)
    q_keep, q_send = question_output(question_len, parts, w_out, first)
    first, second = shift_y(first, 1), shift_y(second, 3)
    near, far, q_own, q_across = relay(
        near_a, far_b, first, second, q_keep, swap_cores(q_send), left_b, right_a
    )
    left_a, right_b = shift_y(near, 1), shift_y(far, 3)
    q_across = shift_y(q_across, 2)
    own = keep[0], swap_cores(send[0])
    return finish(*own, left_a, left_b, right_a, right_b, q_own, q_across)


def solution(mesh):
    return jax.shard_map(
        body,
        mesh=mesh,
        in_specs=(
            P("blk", None),
            P("blk", None),
            P(),
            P(None, "kv"),
            P(None, "kv"),
            P(None, "kv"),
            P("kv", None),
            P(),
            P(),
        ),
        out_specs=(P("blk", "kv"), P("blk", "kv")),
        check_vma=False,
    )
```

time: 98 us -> 90.5 us (0.923)
  waiting for transfers between devices: 29.3 us -> 17.8 us
  starting transfers between devices: 33.8 us -> 37.2 us
  local copies, waits for them, and re-layouts: 3.43 us -> 5.62 us
  Pallas kernels: 28.1 us -> 26.3 us
    all_to_all x1, waiting for transfers between devices: 0.01 us -> 10.3 us  [body(): queries = lax.all_to_all(queries, 'blk', 0, 0)]
    all_to_all x1, waiting for transfers between devices: 7.76 us -> 0.01 us  [body(): parts = lax.all_to_all(parts, 'blk', 0, 0)]
    ppermute x4 -> x7, waiting for transfers between devices: 14.8 us -> 7.09 us  [shift_y(): return lax.ppermute(value, 'kv', pairs)]
    ppermute x7, waiting for transfers between devices: 5.53 us -> 0.02 us  [the longest x2 0.01 us: body(): anchor = anchor + lax.ppermute(held, 'blk', to_blocks({**across, **pairs}))]
    ppermute x4 -> x7, starting transfers between devices: 6.66 us -> 11.4 us  [shift_y(): return lax.ppermute(value, 'kv', pairs)]
    unnamed x22 -> x20, local copies, waits for them, and re-layouts: 3.43 us -> 5.62 us
    all_to_all x1, starting transfers between devices: 6.48 us -> 5.02 us  [body(): parts = lax.all_to_all(parts, 'blk', 0, 0)]
    pallas_call x9 -> x7, Pallas kernels: 18.3 us -> 17.2 us  [the longest x1 7.47 us: context_attention(): pl.pallas_call(context_kernel, in_specs=[smem] + [vmem] * 3 + [anywhere]...]
  transfers between devices with their start and end apart: 16 -> 21, of which waited for: 6 -> 5; matrix products, arithmetic and copies ran while one was open for 1% -> 1% of each run, Pallas kernels for 15% -> 18%
where the time goes in v3:
time: 90.5 us; the launch traced here: 89.2 us
  starting transfers between devices  37.2 us (41%)
  Pallas kernels  26.3 us (29%)
  waiting for transfers between devices  17.8 us (20%)
  local copies, waits for them, and re-layouts  5.62 us (6%)
  between operations  1.51 us (2%)
    all_to_all x1, starting transfers between devices, body(): queries = lax.all_to_all(queries, 'blk', 0, 0)  11.6 us
    ppermute x7, starting transfers between devices, shift_y(): return lax.ppermute(value, 'kv', pairs)  11.4 us
    all_to_all x1, waiting for transfers between devices, body(): queries = lax.all_to_all(queries, 'blk', 0, 0)  10.3 us
    pallas_call x1, Pallas kernels, projections(): pl.pallas_call(projection_kernel, in_specs=[smem, anywhere, anywhere, vme...  9.01 us
    pallas_call x1, Pallas kernels, context_attention(): pl.pallas_call(context_kernel, in_specs=[smem] + [vmem] * 3 + [anywhere]...  7.47 us
    ppermute x7, waiting for transfers between devices, shift_y(): return lax.ppermute(value, 'kv', pairs)  7.09 us
    unnamed x20, local copies, waits for them, and re-layouts  5.62 us
    all_to_all x1, starting transfers between devices, body(): parts = lax.all_to_all(parts, 'blk', 0, 0)  5.02 us
  transfers between devices with their start and end apart: 21, of which 5 were waited for; matrix products, arithmetic and copies ran while one was open for 1% of the time, Pallas kernels for 18%

profile of v3, /device:TPU:32, one launch (start us, length us, event | category | flops | bytes accessed | tf_op | source)
XLA Modules:
  0.0 89.2 jit_solution(15535361854946139815)
XLA Ops:
  0.6 9.0 %projections.1 = (bf16[4,512,128]{2,1,0:T(8,128)(2,1)}, bf16[512,256]{1,0:T(8,128)(2,1)}, bf16[32,8,512]{2,1,0:T(8,128)(2,1)}, bf16[8,256]{1,0:T(8,128)(2,1)}) custom-call(s32[32]{0:T(128)} %len_ref.5, bf16[512,4096]{1,0:T(8,128)(2,1)} %x_hbm.1, bf16[8,4096]{1,0:T(8,128)(2,1)} %question_hbm.1, f32[1,4096]{1,0:T(1,128)} %bitcast.1, bf16[4096,512]{1,0:T(8,128)(2,1)} %wq_hbm.1, ...), custom_call_target="tpu_custom_call" | custom-call | flops 3221225472 | bytes 12582912 | tf_op jit(solution)/shard_map/projections/pallas_call | solution.py:189
  9.7 0.7 collective-permute-start
  10.3 0.7 collective-permute-start.1
  11.0 0.7 collective-permute-start.2
  11.7 11.6 %all-to-all-start = ((bf16[32,8,512]{2,1,0:T(8,128)(2,1)}), bf16[32,8,512]{2,1,0:T(8,128)(2,1)S(1)}, u32[]{:S(2)}, u32[]{:S(2)}) async-start(bf16[32,8,512]{2,1,0:T(8,128)(2,1)} %get-tuple-element.30), calls=%async_computation | async-start | bytes 524288 | tf_op jit(solution)/shard_map/all_to_all | solution.py:498
  23.5 1.3 %collective-permute-start.3 = (bf16[512,256]{1,0:T(8,128)(2,1)S(1)}, bf16[512,256]{1,0:T(8,128)(2,1)S(1)}, u32[]{:S(2)}, u32[]{:S(2)}) collective-permute-start(bf16[512,256]{1,0:T(8,128)(2,1)S(1)} %add_add_fusion.1.refs_0_), channel_id=1, source_target_pairs={{0,8},{24,32},{40,48},{128,152},{1,9},{25,33},{41,49},{129,153},{2... | collective-permute-start | bytes 786440 | tf_op jit(solution)/shard_map/ppermute | solution.py:500
  24.8 0.7 collective-permute-start.4
  25.5 10.3 %all-to-all-done.queries_ref = bf16[32,8,512]{2,1,0:T(8,128)(2,1)S(1)} async-done(((bf16[32,8,512]{2,1,0:T(8,128)(2,1)}), bf16[32,8,512]{2,1,0:T(8,128)(2,1)S(1)}, u32[]{:S(2)}, u32[]{:S(2)}) %all-to-all-start) | async-done | bytes 262176 | tf_op jit(solution)/shard_map/all_to_all | solution.py:498
  35.7 0.9 %copy-done.4 = bf16[512,256]{1,0:T(8,128)(2,1)S(1)} copy-done((bf16[512,256]{1,0:T(8,128)(2,1)S(1)}, bf16[512,256]{1,0:T(8,128)(2,1)}, u32[]{:S(2)}) %copy-start.4) | copy-done | bytes 262168
  36.7 0.7 copy-done.9
  37.4 3.0 %question_attention.1 = (f32[32,8,640]{2,1,0:T(8,128)}, f32[8,128]{1,0:T(8,128)S(1)}) custom-call(s32[32]{0:T(128)S(1)} %copy-done.8, bf16[32,8,512]{2,1,0:T(8,128)(2,1)S(1)} %all-to-all-done.queries_ref, bf16[512,256]{1,0:T(8,128)(2,1)S(1)} %copy-done.4, bf16[8,256]{1,0:T(8,128)(2,1)S(1)} %copy-done.9), custom_call_target="tpu_custom_call" | custom-call | flops 671088640 | bytes 1048576 | tf_op jit(solution)/shard_map/question_attention/pallas_call | solution.py:250
  40.5 2.5 %collective-permute-start.5 = (bf16[512,256]{1,0:T(8,128)(2,1)S(1)}, bf16[512,256]{1,0:T(8,128)(2,1)S(1)}, u32[]{:S(2)}, u32[]{:S(2)}) collective-permute-start(bf16[512,256]{1,0:T(8,128)(2,1)S(1)} %sum_of.1), channel_id=1, source_target_pairs={{0,64},{8,72},{16,80},{24,88},{32,96},{40,104},{48,112},{56,120},{... | collective-permute-start | bytes 786440 | tf_op jit(solution)/shard_map/ppermute | solution.py:508
  43.0 1.3 %collective-permute-start.6 = (bf16[512,256]{1,0:T(8,128)(2,1)S(1)}, bf16[512,256]{1,0:T(8,128)(2,1)S(1)}, u32[]{:S(2)}, u32[]{:S(2)}) collective-permute-start(bf16[512,256]{1,0:T(8,128)(2,1)S(1)} %sum_of.1), channel_id=1, source_target_pairs={{0,192},{8,200},{16,208},{24,216},{32,224},{40,232},{48,240},{56,2... | collective-permute-start | bytes 786440 | tf_op jit(solution)/shard_map/ppermute | solution.py:508
  44.3 5.0 %all-to-all-start.1 = ((f32[32,8,640]{2,1,0:T(8,128)}), f32[32,8,640]{2,1,0:T(8,128)}, u32[]{:S(2)}, u32[]{:S(2)}) async-start(f32[32,8,640]{2,1,0:T(8,128)} %get-tuple-element.45), calls=%async_computation.1 | async-start | bytes 1310720 | tf_op jit(solution)/shard_map/all_to_all | solution.py:509
  49.4 0.7 add_add_fusion.akv_ref
  50.1 7.5 %context_attention.1 = (bf16[512,512]{1,0:T(8,128)(2,1)}, bf16[512,512]{1,0:T(8,128)(2,1)}, bf16[512,512]{1,0:T(8,128)(2,1)}, bf16[512,512]{1,0:T(8,128)(2,1)}, ...) custom-call(s32[32]{0:T(128)} %len_ref.5, ...), custom_call_target="tpu_custom_call" | custom-call | flops 21474836480 | bytes 4194304 | tf_op jit(solution)/shard_map/context_attention/pallas_call | solution.py:320
  59.8 1.0 %copy-done = bf16[512,512]{1,0:T(8,128)(2,1)S(1)} copy-done((bf16[512,512]{1,0:T(8,128)(2,1)S(1)}, bf16[512,512]{1,0:T(8,128)(2,1)}, u32[]{:S(2)}) %copy-start) | copy-done | bytes 524312
  61.0 1.8 %collective-permute-start.11 = (bf16[256,512]{1,0:T(8,128)(2,1)S(1)}, bf16[256,512]{1,0:T(8,128)(2,1)S(1)}, u32[]{:S(2)}, u32[]{:S(2)}) collective-permute-start(bf16[256,512]{1,0:T(8,128)(2,1)S(1)} %get-tuple-element.43._), channel_id=1, source_target_pairs={{0,2},{1,3},{2,4},{3,5},{4,6},{5,7},{6,0},{7,1},{8,10},{9,11},{10,... | collective-permute-start | bytes 786440 | tf_op jit(solution)/shard_map/ppermute | solution.py:478
  62.8 1.7 %collective-permute-start.12 = (bf16[256,512]{1,0:T(8,128)(2,1)S(1)}, bf16[256,512]{1,0:T(8,128)(2,1)S(1)}, u32[]{:S(2)}, u32[]{:S(2)}) collective-permute-start(bf16[256,512]{1,0:T(8,128)(2,1)S(1)} %get-tuple-element.44), channel_id=1, source_target_pairs={{0,6},{1,7},{2,0},{3,1},{4,2},{5,3},{6,4},{7,5},{8,14},{9,15},{10,... | collective-permute-start | bytes 786440 | tf_op jit(solution)/shard_map/ppermute | solution.py:478
  64.5 1.0 %copy-done.2 = bf16[512,512]{1,0:T(8,128)(2,1)S(1)} copy-done((bf16[512,512]{1,0:T(8,128)(2,1)S(1)}, bf16[512,512]{1,0:T(8,128)(2,1)}, u32[]{:S(2)}) %copy-start.2) | copy-done | bytes 524312
  65.5 1.0 %copy-done.3 = bf16[512,512]{1,0:T(8,128)(2,1)S(1)} copy-done((bf16[512,512]{1,0:T(8,128)(2,1)S(1)}, bf16[512,512]{1,0:T(8,128)(2,1)}, u32[]{:S(2)}) %copy-start.3) | copy-done | bytes 524312
  66.6 0.9 others_sum.1
  67.8 2.9 %collective-permute-start.15 = (bf16[256,512]{1,0:T(8,128)(2,1)S(1)}, bf16[256,512]{1,0:T(8,128)(2,1)S(1)}, u32[]{:S(2)}, u32[]{:S(2)}) collective-permute-start(bf16[256,512]{1,0:T(8,128)(2,1)S(1)} %get-tuple-element.49), channel_id=1, source_target_pairs={{0,6},{1,7},{2,0},{3,1},{4,2},{5,3},{6,4},{7,5},{8,14},{9,15},{10,... | collective-permute-start | bytes 786440 | tf_op jit(solution)/shard_map/ppermute | solution.py:478
  70.7 4.6 %question_output.1 = (bf16[4,16,512]{2,1,0:T(8,128)(2,1)}, bf16[4,16,512]{2,1,0:T(8,128)(2,1)}) custom-call(s32[1]{0:T(128)S(6)} %copy.15.qlen_ref, f32[32,8,640]{2,1,0:T(8,128)} %all-to-all-done.1.parts_ref, bf16[512,4096]{1,0:T(8,128)(2,1)} %w_hbm.3, bf16[256,512]{1,0:T(8,128)(2,1)} %copy-done.7), custom_call_target="tpu_custom_call" | custom-call | flops 107374182400 | bytes 4194304 | tf_op jit(solution)/shard_map/question_output/pallas_call | solution.py:351
  75.4 1.4 %collective-permute-done.14._.left_b = bf16[256,512]{1,0:T(8,128)(2,1)S(1)} collective-permute-done((bf16[256,512]{1,0:T(8,128)(2,1)}, bf16[256,512]{1,0:T(8,128)(2,1)S(1)}, u32[]{:S(2)}, u32[]{:S(2)}) %collective-permute-start.14) | collective-permute-done | bytes 262176 | tf_op jit(solution)/shard_map/ppermute | solution.py:478
  76.8 0.8 copy-done.5
  77.8 1.3 %collective-permute-start.16 = (bf16[272,512]{1,0:T(8,128)(2,1)S(1)}, bf16[272,512]{1,0:T(8,128)(2,1)S(1)}, u32[]{:S(2)}, u32[]{:S(2)}) collective-permute-start(bf16[272,512]{1,0:T(8,128)(2,1)S(1)} %get-tuple-element.50), channel_id=1, source_target_pairs={{0,2},{1,3},{2,4},{3,5},{4,6},{5,7},{6,0},{7,1},{8,10},{9,11},{10,... | collective-permute-start | bytes 835592 | tf_op jit(solution)/shard_map/ppermute | solution.py:478
  79.1 2.0 %collective-permute-start.17 = (bf16[272,512]{1,0:T(8,128)(2,1)S(1)}, bf16[272,512]{1,0:T(8,128)(2,1)S(1)}, u32[]{:S(2)}, u32[]{:S(2)}) collective-permute-start(bf16[272,512]{1,0:T(8,128)(2,1)S(1)} %get-tuple-element.51), channel_id=1, source_target_pairs={{0,6},{1,7},{2,0},{3,1},{4,2},{5,3},{6,4},{7,5},{8,14},{9,15},{10,... | collective-permute-start | bytes 835592 | tf_op jit(solution)/shard_map/ppermute | solution.py:478
  81.1 1.4 %collective-permute-start.18 = (bf16[16,512]{1,0:T(8,128)(2,1)S(1)}, bf16[16,512]{1,0:T(8,128)(2,1)S(1)}, u32[]{:S(2)}, u32[]{:S(2)}) collective-permute-start(bf16[16,512]{1,0:T(8,128)(2,1)S(1)} %get-tuple-element.53), channel_id=1, source_target_pairs={{0,4},{1,5},{2,6},{3,7},{4,0},{5,1},{6,2},{7,3},{8,12},{9,13},{10,... | collective-permute-start | bytes 49160 | tf_op jit(solution)/shard_map/ppermute | solution.py:478
  82.5 5.1 %collective-permute-done.18.q_across = bf16[16,512]{1,0:T(8,128)(2,1)S(1)} collective-permute-done((bf16[16,512]{1,0:T(8,128)(2,1)S(1)}, bf16[16,512]{1,0:T(8,128)(2,1)S(1)}, u32[]{:S(2)}, u32[]{:S(2)}) %collective-permute-start.18) | collective-permute-done | bytes 16416 | tf_op jit(solution)/shard_map/ppermute | solution.py:478
  87.6 0.6 collective-permute-done.16.left_a
  88.2 1.1 %finish.1 = (bf16[512,512]{1,0:T(8,128)(2,1)}, bf16[8,512]{1,0:T(8,128)(2,1)}) custom-call(bf16[512,512]{1,0:T(8,128)(2,1)S(1)} %copy-done.1, bf16[512,512]{1,0:T(8,128)(2,1)S(1)} %collective-permute-done.7.got, bf16[272,512]{1,0:T(8,128)(2,1)S(1)} %collective-permute-done.16.left_a, bf16[256,512]{1,0:T(8,128)(2,1)S(1)} %collective-permute-done.14._.left_b, ...), custom_call_target="tpu_custom_call" | custom-call | flops 1048576 | bytes 2621440 | tf_op jit(solution)/shard_map/finish/pallas_call | solution.py:439
  (41 shorter events, 2.5 us)
Async XLA Ops:
  0.6 35.1 %copy-start.8 = (s32[32]{0:T(128)S(1)}, s32[32]{0:T(128)}, u32[]{:S(2)}) copy-start(s32[32]{0:T(128)} %len_ref.5) | copy-start | bytes 388
  9.7 13.7 %collective-permute-start = (bf16[512,256]{1,0:T(8,128)(2,1)}, bf16[512,256]{1,0:T(8,128)(2,1)S(1)}, u32[]{:S(2)}, u32[]{:S(2)}) collective-permute-start(bf16[512,256]{1,0:T(8,128)(2,1)} %get-tuple-element.29.kv_ref), channel_id=1, source_target_pairs={{0,128},{1,129},{2,130},{3,131},{4,132},{5,133},{6,134},{7,135}} | collective-permute-start | bytes 786440 | tf_op jit(solution)/shard_map/ppermute | solution.py:495
  10.3 13.0 %collective-permute-start.1 = (bf16[512,256]{1,0:T(8,128)(2,1)}, bf16[512,256]{1,0:T(8,128)(2,1)S(1)}, u32[]{:S(2)}, u32[]{:S(2)}) collective-permute-start(bf16[512,256]{1,0:T(8,128)(2,1)} %get-tuple-element.29.kv_ref), channel_id=1, source_target_pairs={{0,24},{1,25},{2,26},{3,27},{4,28},{5,29},{6,30},{7,31}} | collective-permute-start | bytes 786440 | tf_op jit(solution)/shard_map/ppermute | solution.py:496
  11.0 12.4 %collective-permute-start.2 = (bf16[512,256]{1,0:T(8,128)(2,1)}, bf16[512,256]{1,0:T(8,128)(2,1)S(1)}, u32[]{:S(2)}, u32[]{:S(2)}) collective-permute-start(bf16[512,256]{1,0:T(8,128)(2,1)} %get-tuple-element.29.kv_ref), channel_id=1, source_target_pairs={{0,40},{1,41},{2,42},{3,43},{4,44},{5,45},{6,46},{7,47}} | collective-permute-start | bytes 786440 | tf_op jit(solution)/shard_map/ppermute | solution.py:497
  11.7 24.0 %all-to-all-start = ((bf16[32,8,512]{2,1,0:T(8,128)(2,1)}), bf16[32,8,512]{2,1,0:T(8,128)(2,1)S(1)}, u32[]{:S(2)}, u32[]{:S(2)}) async-start(bf16[32,8,512]{2,1,0:T(8,128)(2,1)} %get-tuple-element.30), calls=%async_computation | async-start | bytes 524288 | tf_op jit(solution)/shard_map/all_to_all | solution.py:498
  23.5 16.9 %collective-permute-start.3 = (bf16[512,256]{1,0:T(8,128)(2,1)S(1)}, bf16[512,256]{1,0:T(8,128)(2,1)S(1)}, u32[]{:S(2)}, u32[]{:S(2)}) collective-permute-start(bf16[512,256]{1,0:T(8,128)(2,1)S(1)} %add_add_fusion.1.refs_0_), channel_id=1, source_target_pairs={{0,8},{24,32},{40,48},{128,152},{1,9},{25,33},{41,49},{129,153},{2... | collective-permute-start | bytes 786440 | tf_op jit(solution)/shard_map/ppermute | solution.py:500
  24.8 15.6 %collective-permute-start.4 = (bf16[512,256]{1,0:T(8,128)(2,1)S(1)}, bf16[512,256]{1,0:T(8,128)(2,1)S(1)}, u32[]{:S(2)}, u32[]{:S(2)}) collective-permute-start(bf16[512,256]{1,0:T(8,128)(2,1)S(1)} %add_add_fusion.1.refs_0_), channel_id=1, source_target_pairs={{0,56},{24,16},{128,168},{1,57},{25,17},{129,169},{2,58},{26,18},{... | collective-permute-start | bytes 786440 | tf_op jit(solution)/shard_map/ppermute | solution.py:501
  35.7 1.0 %copy-start.4 = (bf16[512,256]{1,0:T(8,128)(2,1)S(1)}, bf16[512,256]{1,0:T(8,128)(2,1)}, u32[]{:S(2)}) copy-start(bf16[512,256]{1,0:T(8,128)(2,1)} %get-tuple-element.29.kv_ref) | copy-start | bytes 786436
  36.7 0.7 copy-start.9
  40.3 9.8 %copy-start.6 = (f32[8,128]{1,0:T(8,128)}, f32[8,128]{1,0:T(8,128)S(1)}, u32[]{:S(2)}) copy-start(f32[8,128]{1,0:T(8,128)S(1)} %get-tuple-element.32.refs_3_._) | copy-start | bytes 12292
  40.5 8.9 %collective-permute-start.5 = (bf16[512,256]{1,0:T(8,128)(2,1)S(1)}, bf16[512,256]{1,0:T(8,128)(2,1)S(1)}, u32[]{:S(2)}, u32[]{:S(2)}) collective-permute-start(bf16[512,256]{1,0:T(8,128)(2,1)S(1)} %sum_of.1), channel_id=1, source_target_pairs={{0,64},{8,72},{16,80},{24,88},{32,96},{40,104},{48,112},{56,120},{... | collective-permute-start | bytes 786440 | tf_op jit(solution)/shard_map/ppermute | solution.py:508
  43.0 6.4 %collective-permute-start.6 = (bf16[512,256]{1,0:T(8,128)(2,1)S(1)}, bf16[512,256]{1,0:T(8,128)(2,1)S(1)}, u32[]{:S(2)}, u32[]{:S(2)}) collective-permute-start(bf16[512,256]{1,0:T(8,128)(2,1)S(1)} %sum_of.1), channel_id=1, source_target_pairs={{0,192},{8,200},{16,208},{24,216},{32,224},{40,232},{48,240},{56,2... | collective-permute-start | bytes 786440 | tf_op jit(solution)/shard_map/ppermute | solution.py:508
  44.3 26.3 %all-to-all-start.1 = ((f32[32,8,640]{2,1,0:T(8,128)}), f32[32,8,640]{2,1,0:T(8,128)}, u32[]{:S(2)}, u32[]{:S(2)}) async-start(f32[32,8,640]{2,1,0:T(8,128)} %get-tuple-element.45), calls=%async_computation.1 | async-start | bytes 1310720 | tf_op jit(solution)/shard_map/all_to_all | solution.py:509
  57.6 2.2 %collective-permute-start.10 = (bf16[512,512]{1,0:T(8,128)(2,1)}, bf16[512,512]{1,0:T(8,128)(2,1)S(1)}, u32[]{:S(2)}, u32[]{:S(2)}) collective-permute-start(bf16[512,512]{1,0:T(8,128)(2,1)} %get-tuple-element.42), channel_id=1, source_target_pairs={{0,1},{1,0},{2,3},{3,2},{4,5},{5,4},{6,7},{7,6},{8,9},{9,8},{10,11... | collective-permute-start | bytes 1572872 | tf_op jit(solution)/shard_map/ppermute | solution.py:483
  57.7 6.8 %collective-permute-start.8 = (bf16[512,512]{1,0:T(8,128)(2,1)}, bf16[512,512]{1,0:T(8,128)(2,1)S(1)}, u32[]{:S(2)}, u32[]{:S(2)}) collective-permute-start(bf16[512,512]{1,0:T(8,128)(2,1)} %get-tuple-element.36), channel_id=1, source_target_pairs={{0,1},{1,0},{2,3},{3,2},{4,5},{5,4},{6,7},{7,6},{8,9},{9,8},{10,11... | collective-permute-start | bytes 1572872 | tf_op jit(solution)/shard_map/ppermute | solution.py:483
  58.2 6.3 %collective-permute-start.9 = (bf16[512,512]{1,0:T(8,128)(2,1)}, bf16[512,512]{1,0:T(8,128)(2,1)S(1)}, u32[]{:S(2)}, u32[]{:S(2)}) collective-permute-start(bf16[512,512]{1,0:T(8,128)(2,1)} %get-tuple-element.38), channel_id=1, source_target_pairs={{0,1},{1,0},{2,3},{3,2},{4,5},{5,4},{6,7},{7,6},{8,9},{9,8},{10,11... | collective-permute-start | bytes 1572872 | tf_op jit(solution)/shard_map/ppermute | solution.py:483
  58.9 23.6 %collective-permute-start.7 = (bf16[512,512]{1,0:T(8,128)(2,1)}, bf16[512,512]{1,0:T(8,128)(2,1)S(1)}, u32[]{:S(2)}, u32[]{:S(2)}) collective-permute-start(bf16[512,512]{1,0:T(8,128)(2,1)} %get-tuple-element.34), channel_id=1, source_target_pairs={{0,1},{1,0},{2,3},{3,2},{4,5},{5,4},{6,7},{7,6},{8,9},{9,8},{10,11... | collective-permute-start | bytes 1572872 | tf_op jit(solution)/shard_map/ppermute | solution.py:483
  59.8 1.0 %copy-start = (bf16[512,512]{1,0:T(8,128)(2,1)S(1)}, bf16[512,512]{1,0:T(8,128)(2,1)}, u32[]{:S(2)}) copy-start(bf16[512,512]{1,0:T(8,128)(2,1)} %get-tuple-element.41.keep_ref) | copy-start | bytes 1572868
  61.0 9.7 %copy-start.7 = (bf16[256,512]{1,0:T(8,128)(2,1)}, bf16[256,512]{1,0:T(8,128)(2,1)S(1)}, u32[]{:S(2)}) copy-start(bf16[256,512]{1,0:T(8,128)(2,1)S(1)} %get-tuple-element.43._) | copy-start | bytes 786436
  61.0 14.3 %collective-permute-start.11 = (bf16[256,512]{1,0:T(8,128)(2,1)S(1)}, bf16[256,512]{1,0:T(8,128)(2,1)S(1)}, u32[]{:S(2)}, u32[]{:S(2)}) collective-permute-start(bf16[256,512]{1,0:T(8,128)(2,1)S(1)} %get-tuple-element.43._), channel_id=1, source_target_pairs={{0,2},{1,3},{2,4},{3,5},{4,6},{5,7},{6,0},{7,1},{8,10},{9,11},{10,... | collective-permute-start | bytes 786440 | tf_op jit(solution)/shard_map/ppermute | solution.py:478
  62.8 12.6 %collective-permute-start.12 = (bf16[256,512]{1,0:T(8,128)(2,1)S(1)}, bf16[256,512]{1,0:T(8,128)(2,1)S(1)}, u32[]{:S(2)}, u32[]{:S(2)}) collective-permute-start(bf16[256,512]{1,0:T(8,128)(2,1)S(1)} %get-tuple-element.44), channel_id=1, source_target_pairs={{0,6},{1,7},{2,0},{3,1},{4,2},{5,3},{6,4},{7,5},{8,14},{9,15},{10,... | collective-permute-start | bytes 786440 | tf_op jit(solution)/shard_map/ppermute | solution.py:478
  64.5 1.0 %copy-start.2 = (bf16[512,512]{1,0:T(8,128)(2,1)S(1)}, bf16[512,512]{1,0:T(8,128)(2,1)}, u32[]{:S(2)}) copy-start(bf16[512,512]{1,0:T(8,128)(2,1)} %get-tuple-element.35.near_keep) | copy-start | bytes 1572868
  65.5 1.0 %copy-start.3 = (bf16[512,512]{1,0:T(8,128)(2,1)S(1)}, bf16[512,512]{1,0:T(8,128)(2,1)}, u32[]{:S(2)}) copy-start(bf16[512,512]{1,0:T(8,128)(2,1)} %get-tuple-element.37.far_keep) | copy-start | bytes 1572868
  67.4 9.4 %collective-permute-start.14 = (bf16[256,512]{1,0:T(8,128)(2,1)}, bf16[256,512]{1,0:T(8,128)(2,1)S(1)}, u32[]{:S(2)}, u32[]{:S(2)}) collective-permute-start(bf16[256,512]{1,0:T(8,128)(2,1)} %get-tuple-element.48), channel_id=1, source_target_pairs={{0,2},{1,3},{2,4},{3,5},{4,6},{5,7},{6,0},{7,1},{8,10},{9,11},{10,... | collective-permute-start | bytes 786440 | tf_op jit(solution)/shard_map/ppermute | solution.py:478
  67.8 20.4 %copy-start.1 = (bf16[512,512]{1,0:T(8,128)(2,1)S(1)}, bf16[512,512]{1,0:T(8,128)(2,1)}, u32[]{:S(2)}) copy-start(bf16[512,512]{1,0:T(8,128)(2,1)} %get-tuple-element.33.keep) | copy-start | bytes 1572868
  67.8 9.0 %collective-permute-start.15 = (bf16[256,512]{1,0:T(8,128)(2,1)S(1)}, bf16[256,512]{1,0:T(8,128)(2,1)S(1)}, u32[]{:S(2)}, u32[]{:S(2)}) collective-permute-start(bf16[256,512]{1,0:T(8,128)(2,1)S(1)} %get-tuple-element.49), channel_id=1, source_target_pairs={{0,6},{1,7},{2,0},{3,1},{4,2},{5,3},{6,4},{7,5},{8,14},{9,15},{10,... | collective-permute-start | bytes 786440 | tf_op jit(solution)/shard_map/ppermute | solution.py:478
  75.3 1.6 %collective-permute-start.13 = (bf16[4,16,512]{2,1,0:T(8,128)(2,1)}, bf16[4,16,512]{2,1,0:T(8,128)(2,1)S(1)}, u32[]{:S(2)}, u32[]{:S(2)}) collective-permute-start(bf16[4,16,512]{2,1,0:T(8,128)(2,1)} %get-tuple-element.47), channel_id=1, source_target_pairs={{0,1},{1,0},{2,3},{3,2},{4,5},{5,4},{6,7},{7,6},{8,9},{9,8},{10,11... | collective-permute-start | bytes 196616 | tf_op jit(solution)/shard_map/ppermute | solution.py:483
  76.8 0.8 copy-start.5
  77.8 10.4 %collective-permute-start.16 = (bf16[272,512]{1,0:T(8,128)(2,1)S(1)}, bf16[272,512]{1,0:T(8,128)(2,1)S(1)}, u32[]{:S(2)}, u32[]{:S(2)}) collective-permute-start(bf16[272,512]{1,0:T(8,128)(2,1)S(1)} %get-tuple-element.50), channel_id=1, source_target_pairs={{0,2},{1,3},{2,4},{3,5},{4,6},{5,7},{6,0},{7,1},{8,10},{9,11},{10,... | collective-permute-start | bytes 835592 | tf_op jit(solution)/shard_map/ppermute | solution.py:478
  79.1 9.0 %collective-permute-start.17 = (bf16[272,512]{1,0:T(8,128)(2,1)S(1)}, bf16[272,512]{1,0:T(8,128)(2,1)S(1)}, u32[]{:S(2)}, u32[]{:S(2)}) collective-permute-start(bf16[272,512]{1,0:T(8,128)(2,1)S(1)} %get-tuple-element.51), channel_id=1, source_target_pairs={{0,6},{1,7},{2,0},{3,1},{4,2},{5,3},{6,4},{7,5},{8,14},{9,15},{10,... | collective-permute-start | bytes 835592 | tf_op jit(solution)/shard_map/ppermute | solution.py:478
  81.1 6.5 %collective-permute-start.18 = (bf16[16,512]{1,0:T(8,128)(2,1)S(1)}, bf16[16,512]{1,0:T(8,128)(2,1)S(1)}, u32[]{:S(2)}, u32[]{:S(2)}) collective-permute-start(bf16[16,512]{1,0:T(8,128)(2,1)S(1)} %get-tuple-element.53), channel_id=1, source_target_pairs={{0,4},{1,5},{2,6},{3,7},{4,0},{5,1},{6,2},{7,3},{8,12},{9,13},{10,... | collective-permute-start | bytes 49160 | tf_op jit(solution)/shard_map/ppermute | solution.py:478

commit v4 on v3

--- a/solution.py
+++ b/solution.py
@@ -20,7 +20,6 @@
 KC = 1024
 ROWS = 256
 QPAD = 16
-CONTEXT_LIMIT = 58
 
 epsilon = 1e-05
 rope_base = 500000.0
@@ -96,7 +95,7 @@
 
 def projection_kernel(
     len_ref, x_hbm, question_hbm, gain_ref, wq_hbm, wk_hbm, wv_hbm, ct_hbm, st_hbm, cb_ref, sb_ref,
-    q_ref, kv_ref, queries_ref, own_ref, ct_ref, st_ref, table_sems,
+    q_ref, kv_ref, queries_ref, ct_ref, st_ref, table_sems,
     x_ref, question_ref, wq_ref, wk_ref, wv_ref, scaled_ref, acc_ref, sq_ref, sems, question_sem,
 ):
     blk_at = lax.axis_index("blk")
@@ -175,11 +174,12 @@
     queries, key, value = heads_of(slice(0, BLK), cosine, sine)
     for h in range(HEADS):
         q_ref[h] = queries[h].astype(bf16)
-    kv_ref[:, :HD] = key.astype(bf16)
-    kv_ref[:, HD:] = value.astype(bf16)
+    kv_ref[:BLK, :HD] = key.astype(bf16)
+    kv_ref[:BLK, HD:] = value.astype(bf16)
     queries, key, value = heads_of(slice(BLK, BLK + QROWS), own_cosine, own_sine)
-    own_ref[:, :HD] = key.astype(bf16)
-    own_ref[:, HD:] = value.astype(bf16)
+    own = jnp.concatenate([key, value], axis=1)
+    own = jnp.concatenate([own, jnp.zeros((QPAD - QROWS, 2 * HD), f32)], axis=0)
+    kv_ref[BLK:] = own.astype(bf16)
     queries = jnp.concatenate(queries, axis=1).astype(bf16)
     for b in range(N_BLK):
         queries_ref[b] = queries
@@ -189,12 +189,11 @@
     return pl.pallas_call(
         projection_kernel,
         in_specs=[smem, anywhere, anywhere, vmem] + [anywhere] * 5 + [vmem] * 2,
-        out_specs=[vmem] * 4,
+        out_specs=[vmem] * 3,
         out_shape=[
             jax.ShapeDtypeStruct((HEADS, BLK, HD), bf16),
-            jax.ShapeDtypeStruct((BLK, 2 * HD), bf16),
+            jax.ShapeDtypeStruct((BLK + QPAD, 2 * HD), bf16),
             jax.ShapeDtypeStruct((N_BLK, QROWS, HEADS * HD), bf16),
-            jax.ShapeDtypeStruct((QROWS, 2 * HD), bf16),
         ],
         scratch_shapes=[
             pltpu.VMEM((BLK, HD), f32),
@@ -217,22 +216,22 @@
     )(block_len, context, question, gain, wq, wk, wv, *tables)
 
 
-def question_attention_kernel(len_ref, queries_ref, kv_ref, own_ref, out_ref, token_ref):
+def question_attention_kernel(len_ref, queries_ref, kv_ref, out_ref, token_ref):
     token_ref[...] = jnp.zeros_like(token_ref)
     blk_at = lax.axis_index("blk")
     live = lax.broadcasted_iota(jnp.int32, (QN, BLK), 1) < len_ref[blk_at]
     question_id = lax.broadcasted_iota(jnp.int32, (QN, HD), 0)
     lane = lax.broadcasted_iota(jnp.int32, (QN, HD), 1)
     seen = (lane < QROWS) & (lane + blk_at * QROWS <= question_id)
-    own = jnp.concatenate([own_ref[...].astype(f32), jnp.zeros((HD - QROWS, 2 * HD), f32)], 0)
-    own = own.astype(bf16)
-    values = with_ones(kv_ref[:, HD:])
+    own = jnp.concatenate([kv_ref[BLK:], jnp.zeros((HD - QPAD, 2 * HD), bf16)], 0)
+    keys = kv_ref[:BLK, :HD]
+    values = with_ones(kv_ref[:BLK, HD:])
     own_values = with_ones(own[:, HD:])
     tile = jnp.zeros((QN, HD), f32)
     for h in range(HEADS):
         cols = slice(h * HD, (h + 1) * HD)
         q = queries_ref[:, :, cols].reshape(QN, HD)
-        scores = jnp.where(live, dot_t(q, kv_ref[:, :HD]), masked_score)
+        scores = jnp.where(live, dot_t(q, keys), masked_score)
         own_scores = jnp.where(seen, dot_t(q, own[:, :HD]), masked_score)
         highest = jnp.maximum(
             jnp.max(scores, axis=-1, keepdims=True), jnp.max(own_scores, axis=-1, keepdims=True)
@@ -246,19 +245,19 @@
     out_ref[:, :, HEADS * HD :] = tile.reshape(N_BLK, QROWS, HD)
 
 
-def question_attention(block_len, queries, kv, own):
+def question_attention(block_len, queries, kv):
     return pl.pallas_call(
         question_attention_kernel,
         out_shape=[
             jax.ShapeDtypeStruct((N_BLK, QROWS, (HEADS + 1) * HD), f32),
             jax.ShapeDtypeStruct((8, HD), f32),
         ],
-        in_specs=[smem] + [vmem] * 3,
+        in_specs=[smem] + [vmem] * 2,
         out_specs=[vmem] * 2,
         compiler_params=params(),
         cost_estimate=cost(HEADS * QN * 640 * HD * 8, 2**20, HEADS * QN * 640),
         name="question_attention",
-    )(block_len, queries, kv, own)
+    )(block_len, queries, kv)
 
 
 def merged(qlen_ref, parts_ref):
@@ -286,14 +285,15 @@
     first = blk_at == 0
     row = lax.broadcasted_iota(jnp.int32, (ROWS, ROWS), 0)
     causal = lax.broadcasted_iota(jnp.int32, (ROWS, ROWS), 1) <= row
-    anchor_values = with_ones(akv_ref[:, HD:])
-    values = with_ones(kv_ref[:, HD:])
+    anchor_keys = akv_ref[:BLK, :HD]
+    anchor_values = with_ones(akv_ref[:BLK, HD:])
+    values = with_ones(kv_ref[:BLK, HD:])
     for r in range(BLK // ROWS):
         rows, before = slice(r * ROWS, (r + 1) * ROWS), slice(0, r * ROWS)
         valid = lax.broadcasted_iota(jnp.int32, (ROWS, HD), 0) + r * ROWS < len_ref[blk_at]
         for h in range(HEADS):
             q = q_ref[h, rows, :]
-            anchor = dot_t(q, akv_ref[:, :HD])
+            anchor = dot_t(q, anchor_keys)
             own = [jnp.where(causal, dot_t(q, kv_ref[rows, :HD]), masked_score)]
             if r:
                 own.append(dot_t(q, kv_ref[before, :HD]))
@@ -327,7 +327,7 @@
             pltpu.VMEM((HEADS * HD, D), bf16),
             pltpu.SemaphoreType.DMA,
         ],
-        compiler_params=params(CONTEXT_LIMIT),
+        compiler_params=params(47),
         cost_estimate=cost(HEADS * BLK * BLK * HD * 8 * 20, 4 * 2**20, HEADS * BLK * BLK),
         name="context_attention",
     )(block_len, q, kv, anchor, w_out, after)
@@ -354,7 +354,7 @@
         out_specs=[vmem] * 2,
         out_shape=[jax.ShapeDtypeStruct((NY, QPAD, FEAT), bf16)] * 2,
         scratch_shapes=[pltpu.VMEM((HEADS * HD, D), bf16), pltpu.SemaphoreType.DMA],
-        compiler_params=params(CONTEXT_LIMIT),
+        compiler_params=params(56),
         cost_estimate=cost(400 * 256 * HEADS * HD * FEAT * NY, 4 * 2**20),
         name="question_output",
     )(question_len, parts, w_out, after)
@@ -488,7 +488,7 @@
     tables = [jnp.asarray(t) for t in angle_tables(np.arange(BLK))]
     tables += [jnp.asarray(t) for t in angle_tables(np.arange(N_BLK + 1) * BLK)]
 
-    q, kv, queries, own_kv = projections(
+    q, kv, queries = projections(
         block_len, context, question, norm_gain.reshape(1, D), w_query, w_key, w_value, tables
     )
     held = jnp.where(blk_at == 0, kv, jnp.zeros_like(kv))
@@ -499,7 +499,7 @@
     within = {(0, 0): (0, 1), (0, 3): (0, 4), (0, 5): (0, 6)}, {(0, 0): (0, 7), (0, 3): (0, 2)}
     second = lax.ppermute(held, "blk", to_blocks({**within[0], (2, 0): (2, 3)}))
     third = lax.ppermute(held, "blk", to_blocks({**within[1], (2, 0): (2, 5)}))
-    parts, token = question_attention(block_len, queries, kv, own_kv)
+    parts, token = question_attention(block_len, queries, kv)
     held = sum_of(held, second, third, after=token)
     anchor = held
     for x, pairs in zip((1, 3), within):

time: 90.5 us -> 89.8 us (level)
  local copies, waits for them, and re-layouts: 5.62 us -> 2.84 us
  waiting for transfers between devices: 17.8 us -> 19.2 us
  Pallas kernels: 26.3 us -> 27.4 us
    unnamed x20 -> x10, local copies, waits for them, and re-layouts: 5.62 us -> 2.84 us
    ppermute x7, waiting for transfers between devices: 7.09 us -> 8.42 us  [shift_y(): return lax.ppermute(value, 'kv', pairs)]
  transfers between devices with their start and end apart: 21 -> 21, of which waited for: 5 -> 5; matrix products, arithmetic and copies ran while one was open for 1% -> 0% of each run, Pallas kernels for 18% -> 20%
where the time goes in v4:
time: 89.8 us; the launch traced here: 88.5 us
  starting transfers between devices  37.4 us (42%)
  Pallas kernels  27.4 us (31%)
  waiting for transfers between devices  19.2 us (21%)
  local copies, waits for them, and re-layouts  2.84 us (3%)
  between operations  1.52 us (2%)
    all_to_all x1, starting transfers between devices, body(): queries = lax.all_to_all(queries, 'blk', 0, 0)  11.6 us
    ppermute x7, starting transfers between devices, shift_y(): return lax.ppermute(value, 'kv', pairs)  11.3 us
    all_to_all x1, waiting for transfers between devices, body(): queries = lax.all_to_all(queries, 'blk', 0, 0)  10.3 us
    pallas_call x1, Pallas kernels, projections(): pl.pallas_call(projection_kernel, in_specs=[smem, anywhere, anywhere, vme...  9.01 us
    ppermute x7, waiting for transfers between devices, shift_y(): return lax.ppermute(value, 'kv', pairs)  8.42 us
    pallas_call x1, Pallas kernels, context_attention(): pl.pallas_call(context_kernel, in_specs=[smem] + [vmem] * 3 + [anywhere]...  7.84 us
    all_to_all x1, starting transfers between devices, body(): parts = lax.all_to_all(parts, 'blk', 0, 0)  5.21 us
    pallas_call x1, Pallas kernels, question_output(): pl.pallas_call(question_output_kernel, in_specs=[smem, vmem] + [anywhere]...  4.6 us
  transfers between devices with their start and end apart: 21, of which 5 were waited for; matrix products, arithmetic and copies ran while one was open for 0% of the time, Pallas kernels for 20%

profile of v4, /device:TPU:32, one launch (start us, length us, event | category | flops | bytes accessed | tf_op | source)
XLA Modules:
  0.0 88.5 jit_solution(11661984682912815962)
XLA Ops:
  0.6 9.0 %projections.1 = (bf16[4,512,128]{2,1,0:T(8,128)(2,1)}, bf16[528,256]{1,0:T(8,128)(2,1)}, bf16[32,8,512]{2,1,0:T(8,128)(2,1)}) custom-call(s32[32]{0:T(128)} %len_ref.5, bf16[512,4096]{1,0:T(8,128)(2,1)} %x_hbm.1, bf16[8,4096]{1,0:T(8,128)(2,1)} %question_hbm.1, f32[1,4096]{1,0:T(1,128)} %bitcast.1, bf16[4096,512]{1,0:T(8,128)(2,1)} %wq_hbm.1, ...), custom_call_target="tpu_custom_call" | custom-call | flops 3221225472 | bytes 12582912 | tf_op jit(solution)/shard_map/projections/pallas_call | solution.py:189
  9.7 0.8 collective-permute-start
  10.5 0.7 collective-permute-start.1
  11.2 0.7 collective-permute-start.2
  11.9 11.6 %all-to-all-start = ((bf16[32,8,512]{2,1,0:T(8,128)(2,1)}), bf16[32,8,512]{2,1,0:T(8,128)(2,1)S(1)}, u32[]{:S(2)}, u32[]{:S(2)}) async-start(bf16[32,8,512]{2,1,0:T(8,128)(2,1)} %get-tuple-element.29), calls=%async_computation | async-start | bytes 524288 | tf_op jit(solution)/shard_map/all_to_all | solution.py:498
  23.6 1.3 %collective-permute-start.3 = (bf16[528,256]{1,0:T(8,128)(2,1)S(1)}, bf16[528,256]{1,0:T(8,128)(2,1)S(1)}, u32[]{:S(2)}, u32[]{:S(2)}) collective-permute-start(bf16[528,256]{1,0:T(8,128)(2,1)S(1)} %add_add_fusion.1.refs_0_), channel_id=1, source_target_pairs={{0,8},{24,32},{40,48},{128,152},{1,9},{25,33},{41,49},{129,153},{2... | collective-permute-start | bytes 811016 | tf_op jit(solution)/shard_map/ppermute | solution.py:500
  24.9 0.7 collective-permute-start.4
  25.6 10.3 %all-to-all-done.queries_ref = bf16[32,8,512]{2,1,0:T(8,128)(2,1)S(1)} async-done(((bf16[32,8,512]{2,1,0:T(8,128)(2,1)}), bf16[32,8,512]{2,1,0:T(8,128)(2,1)S(1)}, u32[]{:S(2)}, u32[]{:S(2)}) %all-to-all-start) | async-done | bytes 262176 | tf_op jit(solution)/shard_map/all_to_all | solution.py:498
  35.9 1.0 %copy-done = bf16[528,256]{1,0:T(8,128)(2,1)S(1)} copy-done((bf16[528,256]{1,0:T(8,128)(2,1)S(1)}, bf16[528,256]{1,0:T(8,128)(2,1)}, u32[]{:S(2)}) %copy-start) | copy-done | bytes 270360
  36.8 3.0 %question_attention.1 = (f32[32,8,640]{2,1,0:T(8,128)}, f32[8,128]{1,0:T(8,128)S(1)}) custom-call(s32[32]{0:T(128)S(1)} %copy-done.3, bf16[32,8,512]{2,1,0:T(8,128)(2,1)S(1)} %all-to-all-done.queries_ref, bf16[528,256]{1,0:T(8,128)(2,1)S(1)} %copy-done), custom_call_target="tpu_custom_call" | custom-call | flops 671088640 | bytes 1048576 | tf_op jit(solution)/shard_map/question_attention/pallas_call | solution.py:249
  39.9 2.5 %collective-permute-start.5 = (bf16[528,256]{1,0:T(8,128)(2,1)S(1)}, bf16[528,256]{1,0:T(8,128)(2,1)S(1)}, u32[]{:S(2)}, u32[]{:S(2)}) collective-permute-start(bf16[528,256]{1,0:T(8,128)(2,1)S(1)} %sum_of.1), channel_id=1, source_target_pairs={{0,64},{8,72},{16,80},{24,88},{32,96},{40,104},{48,112},{56,120},{... | collective-permute-start | bytes 811016 | tf_op jit(solution)/shard_map/ppermute | solution.py:508
  42.5 1.3 %collective-permute-start.6 = (bf16[528,256]{1,0:T(8,128)(2,1)S(1)}, bf16[528,256]{1,0:T(8,128)(2,1)S(1)}, u32[]{:S(2)}, u32[]{:S(2)}) collective-permute-start(bf16[528,256]{1,0:T(8,128)(2,1)S(1)} %sum_of.1), channel_id=1, source_target_pairs={{0,192},{8,200},{16,208},{24,216},{32,224},{40,232},{48,240},{56,2... | collective-permute-start | bytes 811016 | tf_op jit(solution)/shard_map/ppermute | solution.py:508
  43.8 5.2 %all-to-all-start.1 = ((f32[32,8,640]{2,1,0:T(8,128)}), f32[32,8,640]{2,1,0:T(8,128)}, u32[]{:S(2)}, u32[]{:S(2)}) async-start(f32[32,8,640]{2,1,0:T(8,128)} %get-tuple-element.43), calls=%async_computation.1 | async-start | bytes 1310720 | tf_op jit(solution)/shard_map/all_to_all | solution.py:509
  49.1 1.0 %copy-done.4 = bf16[4,512,128]{2,1,0:T(8,128)(2,1)S(1)} copy-done((bf16[4,512,128]{2,1,0:T(8,128)(2,1)S(1)}, bf16[4,512,128]{2,1,0:T(8,128)(2,1)}, u32[]{:S(2)}) %copy-start.4) | copy-done | bytes 524312
  50.1 7.8 %context_attention.1 = (bf16[512,512]{1,0:T(8,128)(2,1)S(1)}, bf16[512,512]{1,0:T(8,128)(2,1)S(1)}, bf16[512,512]{1,0:T(8,128)(2,1)S(1)}, bf16[512,512]{1,0:T(8,...) custom-call(s32[32]{0:T(128)S(1)} %copy-done.3, ...), custom_call_target="tpu_custom_call" | custom-call | flops 21474836480 | bytes 4194304 | tf_op jit(solution)/shard_map/context_attention/pallas_call | solution.py:320
  58.1 0.5 collective-permute-start.8
  59.3 0.5 collective-permute-start.7
  60.0 0.8 across_sum.1
  60.8 1.6 %collective-permute-start.11 = (bf16[256,512]{1,0:T(8,128)(2,1)}, bf16[256,512]{1,0:T(8,128)(2,1)S(1)}, u32[]{:S(2)}, u32[]{:S(2)}) collective-permute-start(bf16[256,512]{1,0:T(8,128)(2,1)} %get-tuple-element.41._), channel_id=1, source_target_pairs={{0,2},{1,3},{2,4},{3,5},{4,6},{5,7},{6,0},{7,1},{8,10},{9,11},{10,... | collective-permute-start | bytes 786440 | tf_op jit(solution)/shard_map/ppermute | solution.py:478
  62.3 1.7 %collective-permute-start.12 = (bf16[256,512]{1,0:T(8,128)(2,1)S(1)}, bf16[256,512]{1,0:T(8,128)(2,1)S(1)}, u32[]{:S(2)}, u32[]{:S(2)}) collective-permute-start(bf16[256,512]{1,0:T(8,128)(2,1)S(1)} %get-tuple-element.42), channel_id=1, source_target_pairs={{0,6},{1,7},{2,0},{3,1},{4,2},{5,3},{6,4},{7,5},{8,14},{9,15},{10,... | collective-permute-start | bytes 786440 | tf_op jit(solution)/shard_map/ppermute | solution.py:478
  64.0 0.9 %others_sum.1 = (bf16[256,512]{1,0:T(8,128)(2,1)S(1)}, bf16[256,512]{1,0:T(8,128)(2,1)}, bf16[256,512]{1,0:T(8,128)(2,1)}, bf16[256,512]{1,0:T(8,128)(2,1)S(1)}) custom-call(bf16[512,512]{1,0:T(8,128)(2,1)S(1)} %get-tuple-element.33.near_keep, bf16[512,512]{1,0:T(8,128)(2,1)S(1)} %collective-permute-done.8.near_got, ...), custom_call_target="tpu_custom_call" | custom-call | tf_op jit(solution)/shard_map/others_sum/pallas_call | solution.py:395
  65.0 0.4 collective-permute-start.14
  65.3 2.9 %collective-permute-start.15 = (bf16[256,512]{1,0:T(8,128)(2,1)}, bf16[256,512]{1,0:T(8,128)(2,1)S(1)}, u32[]{:S(2)}, u32[]{:S(2)}) collective-permute-start(bf16[256,512]{1,0:T(8,128)(2,1)} %get-tuple-element.47), channel_id=1, source_target_pairs={{0,6},{1,7},{2,0},{3,1},{4,2},{5,3},{6,4},{7,5},{8,14},{9,15},{10,... | collective-permute-start | bytes 786440 | tf_op jit(solution)/shard_map/ppermute | solution.py:478
  68.2 0.3 all-to-all-done.1.parts_ref
  68.5 4.6 %question_output.1 = (bf16[4,16,512]{2,1,0:T(8,128)(2,1)}, bf16[4,16,512]{2,1,0:T(8,128)(2,1)}) custom-call(s32[1]{0:T(128)S(6)} %copy.15.qlen_ref, f32[32,8,640]{2,1,0:T(8,128)} %all-to-all-done.1.parts_ref, bf16[512,4096]{1,0:T(8,128)(2,1)} %w_hbm.3, bf16[256,512]{1,0:T(8,128)(2,1)} %get-tuple-element.41._), custom_call_target="tpu_custom_call" | custom-call | flops 107374182400 | bytes 4194304 | tf_op jit(solution)/shard_map/question_output/pallas_call | solution.py:351
  73.2 3.0 %collective-permute-done.14._.left_b = bf16[256,512]{1,0:T(8,128)(2,1)S(1)} collective-permute-done((bf16[256,512]{1,0:T(8,128)(2,1)}, bf16[256,512]{1,0:T(8,128)(2,1)S(1)}, u32[]{:S(2)}, u32[]{:S(2)}) %collective-permute-start.14) | collective-permute-done | bytes 262176 | tf_op jit(solution)/shard_map/ppermute | solution.py:478
  76.2 0.8 copy-done.2
  77.2 1.5 %collective-permute-start.16 = (bf16[272,512]{1,0:T(8,128)(2,1)S(1)}, bf16[272,512]{1,0:T(8,128)(2,1)S(1)}, u32[]{:S(2)}, u32[]{:S(2)}) collective-permute-start(bf16[272,512]{1,0:T(8,128)(2,1)S(1)} %get-tuple-element.48), channel_id=1, source_target_pairs={{0,2},{1,3},{2,4},{3,5},{4,6},{5,7},{6,0},{7,1},{8,10},{9,11},{10,... | collective-permute-start | bytes 835592 | tf_op jit(solution)/shard_map/ppermute | solution.py:478
  78.7 1.8 %collective-permute-start.17 = (bf16[272,512]{1,0:T(8,128)(2,1)S(1)}, bf16[272,512]{1,0:T(8,128)(2,1)S(1)}, u32[]{:S(2)}, u32[]{:S(2)}) collective-permute-start(bf16[272,512]{1,0:T(8,128)(2,1)S(1)} %get-tuple-element.49), channel_id=1, source_target_pairs={{0,6},{1,7},{2,0},{3,1},{4,2},{5,3},{6,4},{7,5},{8,14},{9,15},{10,... | collective-permute-start | bytes 835592 | tf_op jit(solution)/shard_map/ppermute | solution.py:478
  80.5 1.5 %collective-permute-start.18 = (bf16[16,512]{1,0:T(8,128)(2,1)S(1)}, bf16[16,512]{1,0:T(8,128)(2,1)S(1)}, u32[]{:S(2)}, u32[]{:S(2)}) collective-permute-start(bf16[16,512]{1,0:T(8,128)(2,1)S(1)} %get-tuple-element.51), channel_id=1, source_target_pairs={{0,4},{1,5},{2,6},{3,7},{4,0},{5,1},{6,2},{7,3},{8,12},{9,13},{10,... | collective-permute-start | bytes 49160 | tf_op jit(solution)/shard_map/ppermute | solution.py:478
  82.0 5.4 %collective-permute-done.18.q_across = bf16[16,512]{1,0:T(8,128)(2,1)S(1)} collective-permute-done((bf16[16,512]{1,0:T(8,128)(2,1)S(1)}, bf16[16,512]{1,0:T(8,128)(2,1)S(1)}, u32[]{:S(2)}, u32[]{:S(2)}) %collective-permute-start.18) | collective-permute-done | bytes 16416 | tf_op jit(solution)/shard_map/ppermute | solution.py:478
  87.4 1.1 %finish.1 = (bf16[512,512]{1,0:T(8,128)(2,1)}, bf16[8,512]{1,0:T(8,128)(2,1)}) custom-call(bf16[512,512]{1,0:T(8,128)(2,1)S(1)} %get-tuple-element.31.keep, bf16[512,512]{1,0:T(8,128)(2,1)S(1)} %collective-permute-done.7.got, bf16[272,512]{1,0:T(8,128)(2,1)S(1)} %collective-permute-done.16.left_a, bf16[256,512]{1,0:T(8,128)(2,1)S(1)} %collective-permute-done.14._.left_b, ...), custom_call_target="tpu_custom_call" | custom-call | flops 1048576 | bytes 2621440 | tf_op jit(solution)/shard_map/finish/pallas_call | solution.py:439
  (31 shorter events, 0.9 us)
Async XLA Ops:
  0.6 35.3 %copy-start.3 = (s32[32]{0:T(128)S(1)}, s32[32]{0:T(128)}, u32[]{:S(2)}) copy-start(s32[32]{0:T(128)} %len_ref.5) | copy-start | bytes 388
  9.7 39.4 %copy-start.1 = (bf16[528,256]{1,0:T(8,128)(2,1)S(1)}, bf16[528,256]{1,0:T(8,128)(2,1)}, u32[]{:S(2)}) copy-start(bf16[528,256]{1,0:T(8,128)(2,1)} %get-tuple-element.28.kv_ref) | copy-start | bytes 811012
  9.7 13.8 %collective-permute-start = (bf16[528,256]{1,0:T(8,128)(2,1)}, bf16[528,256]{1,0:T(8,128)(2,1)S(1)}, u32[]{:S(2)}, u32[]{:S(2)}) collective-permute-start(bf16[528,256]{1,0:T(8,128)(2,1)} %get-tuple-element.28.kv_ref), channel_id=1, source_target_pairs={{0,128},{1,129},{2,130},{3,131},{4,132},{5,133},{6,134},{7,135}} | collective-permute-start | bytes 811016 | tf_op jit(solution)/shard_map/ppermute | solution.py:495
  10.5 13.0 %collective-permute-start.1 = (bf16[528,256]{1,0:T(8,128)(2,1)}, bf16[528,256]{1,0:T(8,128)(2,1)S(1)}, u32[]{:S(2)}, u32[]{:S(2)}) collective-permute-start(bf16[528,256]{1,0:T(8,128)(2,1)} %get-tuple-element.28.kv_ref), channel_id=1, source_target_pairs={{0,24},{1,25},{2,26},{3,27},{4,28},{5,29},{6,30},{7,31}} | collective-permute-start | bytes 811016 | tf_op jit(solution)/shard_map/ppermute | solution.py:496
  11.2 12.3 %collective-permute-start.2 = (bf16[528,256]{1,0:T(8,128)(2,1)}, bf16[528,256]{1,0:T(8,128)(2,1)S(1)}, u32[]{:S(2)}, u32[]{:S(2)}) collective-permute-start(bf16[528,256]{1,0:T(8,128)(2,1)} %get-tuple-element.28.kv_ref), channel_id=1, source_target_pairs={{0,40},{1,41},{2,42},{3,43},{4,44},{5,45},{6,46},{7,47}} | collective-permute-start | bytes 811016 | tf_op jit(solution)/shard_map/ppermute | solution.py:497
  11.9 24.0 %all-to-all-start = ((bf16[32,8,512]{2,1,0:T(8,128)(2,1)}), bf16[32,8,512]{2,1,0:T(8,128)(2,1)S(1)}, u32[]{:S(2)}, u32[]{:S(2)}) async-start(bf16[32,8,512]{2,1,0:T(8,128)(2,1)} %get-tuple-element.29), calls=%async_computation | async-start | bytes 524288 | tf_op jit(solution)/shard_map/all_to_all | solution.py:498
  23.6 16.2 %collective-permute-start.3 = (bf16[528,256]{1,0:T(8,128)(2,1)S(1)}, bf16[528,256]{1,0:T(8,128)(2,1)S(1)}, u32[]{:S(2)}, u32[]{:S(2)}) collective-permute-start(bf16[528,256]{1,0:T(8,128)(2,1)S(1)} %add_add_fusion.1.refs_0_), channel_id=1, source_target_pairs={{0,8},{24,32},{40,48},{128,152},{1,9},{25,33},{41,49},{129,153},{2... | collective-permute-start | bytes 811016 | tf_op jit(solution)/shard_map/ppermute | solution.py:500
  24.9 14.9 %collective-permute-start.4 = (bf16[528,256]{1,0:T(8,128)(2,1)S(1)}, bf16[528,256]{1,0:T(8,128)(2,1)S(1)}, u32[]{:S(2)}, u32[]{:S(2)}) collective-permute-start(bf16[528,256]{1,0:T(8,128)(2,1)S(1)} %add_add_fusion.1.refs_0_), channel_id=1, source_target_pairs={{0,56},{24,16},{128,168},{1,57},{25,17},{129,169},{2,58},{26,18},{... | collective-permute-start | bytes 811016 | tf_op jit(solution)/shard_map/ppermute | solution.py:501
  35.9 1.0 %copy-start = (bf16[528,256]{1,0:T(8,128)(2,1)S(1)}, bf16[528,256]{1,0:T(8,128)(2,1)}, u32[]{:S(2)}) copy-start(bf16[528,256]{1,0:T(8,128)(2,1)} %get-tuple-element.28.kv_ref) | copy-start | bytes 811012
  39.9 9.1 %collective-permute-start.5 = (bf16[528,256]{1,0:T(8,128)(2,1)S(1)}, bf16[528,256]{1,0:T(8,128)(2,1)S(1)}, u32[]{:S(2)}, u32[]{:S(2)}) collective-permute-start(bf16[528,256]{1,0:T(8,128)(2,1)S(1)} %sum_of.1), channel_id=1, source_target_pairs={{0,64},{8,72},{16,80},{24,88},{32,96},{40,104},{48,112},{56,120},{... | collective-permute-start | bytes 811016 | tf_op jit(solution)/shard_map/ppermute | solution.py:508
  42.5 6.5 %collective-permute-start.6 = (bf16[528,256]{1,0:T(8,128)(2,1)S(1)}, bf16[528,256]{1,0:T(8,128)(2,1)S(1)}, u32[]{:S(2)}, u32[]{:S(2)}) collective-permute-start(bf16[528,256]{1,0:T(8,128)(2,1)S(1)} %sum_of.1), channel_id=1, source_target_pairs={{0,192},{8,200},{16,208},{24,216},{32,224},{40,232},{48,240},{56,2... | collective-permute-start | bytes 811016 | tf_op jit(solution)/shard_map/ppermute | solution.py:508
  43.8 24.7 %all-to-all-start.1 = ((f32[32,8,640]{2,1,0:T(8,128)}), f32[32,8,640]{2,1,0:T(8,128)}, u32[]{:S(2)}, u32[]{:S(2)}) async-start(f32[32,8,640]{2,1,0:T(8,128)} %get-tuple-element.43), calls=%async_computation.1 | async-start | bytes 1310720 | tf_op jit(solution)/shard_map/all_to_all | solution.py:509
  49.1 1.0 %copy-start.4 = (bf16[4,512,128]{2,1,0:T(8,128)(2,1)S(1)}, bf16[4,512,128]{2,1,0:T(8,128)(2,1)}, u32[]{:S(2)}) copy-start(bf16[4,512,128]{2,1,0:T(8,128)(2,1)} %get-tuple-element.27.q_ref) | copy-start | bytes 1572868
  58.0 2.0 %collective-permute-start.10 = (bf16[512,512]{1,0:T(8,128)(2,1)S(1)}, bf16[512,512]{1,0:T(8,128)(2,1)S(1)}, u32[]{:S(2)}, u32[]{:S(2)}) collective-permute-start(bf16[512,512]{1,0:T(8,128)(2,1)S(1)} %get-tuple-element.40), channel_id=1, source_target_pairs={{0,1},{1,0},{2,3},{3,2},{4,5},{5,4},{6,7},{7,6},{8,9},{9,8},{10,11... | collective-permute-start | bytes 1572872 | tf_op jit(solution)/shard_map/ppermute | solution.py:483
  58.1 5.9 %collective-permute-start.8 = (bf16[512,512]{1,0:T(8,128)(2,1)S(1)}, bf16[512,512]{1,0:T(8,128)(2,1)S(1)}, u32[]{:S(2)}, u32[]{:S(2)}) collective-permute-start(bf16[512,512]{1,0:T(8,128)(2,1)S(1)} %get-tuple-element.34), channel_id=1, source_target_pairs={{0,1},{1,0},{2,3},{3,2},{4,5},{5,4},{6,7},{7,6},{8,9},{9,8},{10,11... | collective-permute-start | bytes 1572872 | tf_op jit(solution)/shard_map/ppermute | solution.py:483
  58.6 5.4 %collective-permute-start.9 = (bf16[512,512]{1,0:T(8,128)(2,1)S(1)}, bf16[512,512]{1,0:T(8,128)(2,1)S(1)}, u32[]{:S(2)}, u32[]{:S(2)}) collective-permute-start(bf16[512,512]{1,0:T(8,128)(2,1)S(1)} %get-tuple-element.36), channel_id=1, source_target_pairs={{0,1},{1,0},{2,3},{3,2},{4,5},{5,4},{6,7},{7,6},{8,9},{9,8},{10,11... | collective-permute-start | bytes 1572872 | tf_op jit(solution)/shard_map/ppermute | solution.py:483
  59.3 22.7 %collective-permute-start.7 = (bf16[512,512]{1,0:T(8,128)(2,1)S(1)}, bf16[512,512]{1,0:T(8,128)(2,1)S(1)}, u32[]{:S(2)}, u32[]{:S(2)}) collective-permute-start(bf16[512,512]{1,0:T(8,128)(2,1)S(1)} %get-tuple-element.32), channel_id=1, source_target_pairs={{0,1},{1,0},{2,3},{3,2},{4,5},{5,4},{6,7},{7,6},{8,9},{9,8},{10,11... | collective-permute-start | bytes 1572872 | tf_op jit(solution)/shard_map/ppermute | solution.py:483
  60.8 12.3 %collective-permute-start.11 = (bf16[256,512]{1,0:T(8,128)(2,1)}, bf16[256,512]{1,0:T(8,128)(2,1)S(1)}, u32[]{:S(2)}, u32[]{:S(2)}) collective-permute-start(bf16[256,512]{1,0:T(8,128)(2,1)} %get-tuple-element.41._), channel_id=1, source_target_pairs={{0,2},{1,3},{2,4},{3,5},{4,6},{5,7},{6,0},{7,1},{8,10},{9,11},{10,... | collective-permute-start | bytes 786440 | tf_op jit(solution)/shard_map/ppermute | solution.py:478
  62.3 10.9 %collective-permute-start.12 = (bf16[256,512]{1,0:T(8,128)(2,1)S(1)}, bf16[256,512]{1,0:T(8,128)(2,1)S(1)}, u32[]{:S(2)}, u32[]{:S(2)}) collective-permute-start(bf16[256,512]{1,0:T(8,128)(2,1)S(1)} %get-tuple-element.42), channel_id=1, source_target_pairs={{0,6},{1,7},{2,0},{3,1},{4,2},{5,3},{6,4},{7,5},{8,14},{9,15},{10,... | collective-permute-start | bytes 786440 | tf_op jit(solution)/shard_map/ppermute | solution.py:478
  65.0 11.3 %collective-permute-start.14 = (bf16[256,512]{1,0:T(8,128)(2,1)}, bf16[256,512]{1,0:T(8,128)(2,1)S(1)}, u32[]{:S(2)}, u32[]{:S(2)}) collective-permute-start(bf16[256,512]{1,0:T(8,128)(2,1)} %get-tuple-element.46), channel_id=1, source_target_pairs={{0,2},{1,3},{2,4},{3,5},{4,6},{5,7},{6,0},{7,1},{8,10},{9,11},{10,... | collective-permute-start | bytes 786440 | tf_op jit(solution)/shard_map/ppermute | solution.py:478
  65.3 10.9 %collective-permute-start.15 = (bf16[256,512]{1,0:T(8,128)(2,1)}, bf16[256,512]{1,0:T(8,128)(2,1)S(1)}, u32[]{:S(2)}, u32[]{:S(2)}) collective-permute-start(bf16[256,512]{1,0:T(8,128)(2,1)} %get-tuple-element.47), channel_id=1, source_target_pairs={{0,6},{1,7},{2,0},{3,1},{4,2},{5,3},{6,4},{7,5},{8,14},{9,15},{10,... | collective-permute-start | bytes 786440 | tf_op jit(solution)/shard_map/ppermute | solution.py:478
  73.1 3.1 %collective-permute-start.13 = (bf16[4,16,512]{2,1,0:T(8,128)(2,1)}, bf16[4,16,512]{2,1,0:T(8,128)(2,1)S(1)}, u32[]{:S(2)}, u32[]{:S(2)}) collective-permute-start(bf16[4,16,512]{2,1,0:T(8,128)(2,1)} %get-tuple-element.45), channel_id=1, source_target_pairs={{0,1},{1,0},{2,3},{3,2},{4,5},{5,4},{6,7},{7,6},{8,9},{9,8},{10,11... | collective-permute-start | bytes 196616 | tf_op jit(solution)/shard_map/ppermute | solution.py:483
  76.2 0.8 copy-start.2
  77.2 10.2 %collective-permute-start.16 = (bf16[272,512]{1,0:T(8,128)(2,1)S(1)}, bf16[272,512]{1,0:T(8,128)(2,1)S(1)}, u32[]{:S(2)}, u32[]{:S(2)}) collective-permute-start(bf16[272,512]{1,0:T(8,128)(2,1)S(1)} %get-tuple-element.48), channel_id=1, source_target_pairs={{0,2},{1,3},{2,4},{3,5},{4,6},{5,7},{6,0},{7,1},{8,10},{9,11},{10,... | collective-permute-start | bytes 835592 | tf_op jit(solution)/shard_map/ppermute | solution.py:478
  78.7 8.8 %collective-permute-start.17 = (bf16[272,512]{1,0:T(8,128)(2,1)S(1)}, bf16[272,512]{1,0:T(8,128)(2,1)S(1)}, u32[]{:S(2)}, u32[]{:S(2)}) collective-permute-start(bf16[272,512]{1,0:T(8,128)(2,1)S(1)} %get-tuple-element.49), channel_id=1, source_target_pairs={{0,6},{1,7},{2,0},{3,1},{4,2},{5,3},{6,4},{7,5},{8,14},{9,15},{10,... | collective-permute-start | bytes 835592 | tf_op jit(solution)/shard_map/ppermute | solution.py:478
  80.5 6.9 %collective-permute-start.18 = (bf16[16,512]{1,0:T(8,128)(2,1)S(1)}, bf16[16,512]{1,0:T(8,128)(2,1)S(1)}, u32[]{:S(2)}, u32[]{:S(2)}) collective-permute-start(bf16[16,512]{1,0:T(8,128)(2,1)S(1)} %get-tuple-element.51), channel_id=1, source_target_pairs={{0,4},{1,5},{2,6},{3,7},{4,0},{5,1},{6,2},{7,3},{8,12},{9,13},{10,... | collective-permute-start | bytes 49160 | tf_op jit(solution)/shard_map/ppermute | solution.py:478

commit v5 on v4

--- a/solution.py
+++ b/solution.py
@@ -274,14 +274,23 @@
     return jnp.concatenate([rows, jnp.zeros((QPAD - QROWS, HEADS * HD), f32)], 0).astype(bf16)
 
 
+def chip_columns(to_y):
+    width = NC * FEAT
+    return pl.ds(pl.multiple_of(lax.rem(to_y, NY) * width, width), width)
+
+
 def context_kernel(
     len_ref, q_ref, kv_ref, akv_ref, w_hbm, _, *refs
 ):
-    keep_refs, send_refs, (att_ref, w_ref, sem) = refs[:NY], refs[NY : 2 * NY], refs[2 * NY :]
+    keep_refs, send_refs, (att_ref, w_ref, sems) = refs[:NY], refs[NY : 2 * NY], refs[2 * NY :]
     blk_at, kv_at = lax.axis_index("blk"), lax.axis_index("kv")
     y_at, c_at = kv_at // NC, lax.rem(kv_at, NC)
-    copy = pltpu.make_async_copy(w_hbm, w_ref, sem)
-    copy.start()
+    shares = []
+    for i, d in enumerate((2, 1, 3, 0)):
+        columns = chip_columns(y_at + d)
+        copy = pltpu.make_async_copy(w_hbm.at[:, columns], w_ref.at[i], sems.at[i])
+        copy.start()
+        shares.append((d, copy))
     first = blk_at == 0
     row = lax.broadcasted_iota(jnp.int32, (ROWS, ROWS), 0)
     causal = lax.broadcasted_iota(jnp.int32, (ROWS, ROWS), 1) <= row
@@ -308,12 +317,11 @@
                 mixture = mixture + dot(jnp.exp2(scores - highest).astype(bf16), values[at])
             result = mixture[:, :HD] / mixture[:, HD:]
             att_ref[rows, h * HD : (h + 1) * HD] = jnp.where(valid, result, 0.0).astype(bf16)
-    copy.wait()
-    for d in range(NY):
-        to_y = lax.rem(y_at + d, NY)
+    for i, (d, copy) in enumerate(shares):
+        copy.wait()
         for ref, to_c in ((send_refs[d], 1 - c_at), (keep_refs[d], c_at)):
-            columns = pl.ds(pl.multiple_of((to_y * NC + to_c) * FEAT, FEAT), FEAT)
-            ref[...] = dot(att_ref[...], w_ref[:, columns]).astype(bf16)
+            columns = pl.ds(pl.multiple_of(to_c * FEAT, FEAT), FEAT)
+            ref[...] = dot(att_ref[...], w_ref[i, :, columns]).astype(bf16)
 
 
 def context_attention(block_len, q, kv, anchor, w_out, after):
@@ -324,8 +332,8 @@
         out_shape=[jax.ShapeDtypeStruct((BLK, FEAT), bf16)] * (2 * NY),
         scratch_shapes=[
             pltpu.VMEM((BLK, HEADS * HD), bf16),
-            pltpu.VMEM((HEADS * HD, D), bf16),
-            pltpu.SemaphoreType.DMA,
+            pltpu.VMEM((NY, HEADS * HD, NC * FEAT), bf16),
+            pltpu.SemaphoreType.DMA((NY,)),
         ],
         compiler_params=params(47),
         cost_estimate=cost(HEADS * BLK * BLK * HD * 8 * 20, 4 * 2**20, HEADS * BLK * BLK),

time: 89.8 us -> 89.4 us (level)
  transfers between devices with their start and end apart: 21 -> 21, of which waited for: 5 -> 5; matrix products, arithmetic and copies ran while one was open for 0% -> 0% of each run, Pallas kernels for 20% -> 19%
where the time goes in v5:
time: 89.4 us; the launch traced here: 88.3 us
  starting transfers between devices  37.4 us (42%)
  Pallas kernels  27 us (30%)
  waiting for transfers between devices  19.4 us (22%)
  local copies, waits for them, and re-layouts  2.84 us (3%)
  between operations  1.52 us (2%)
    all_to_all x1, starting transfers between devices, body(): queries = lax.all_to_all(queries, 'blk', 0, 0)  11.6 us
    ppermute x7, starting transfers between devices, shift_y(): return lax.ppermute(value, 'kv', pairs)  11.3 us
    all_to_all x1, waiting for transfers between devices, body(): queries = lax.all_to_all(queries, 'blk', 0, 0)  10.3 us
    pallas_call x1, Pallas kernels, projections(): pl.pallas_call(projection_kernel, in_specs=[smem, anywhere, anywhere, vme...  9.01 us
    ppermute x7, waiting for transfers between devices, shift_y(): return lax.ppermute(value, 'kv', pairs)  8.19 us
    pallas_call x1, Pallas kernels, context_attention(): pl.pallas_call(context_kernel, in_specs=[smem] + [vmem] * 3 + [anywhere]...  7.43 us
    all_to_all x1, starting transfers between devices, body(): parts = lax.all_to_all(parts, 'blk', 0, 0)  5.21 us
    pallas_call x1, Pallas kernels, question_output(): pl.pallas_call(question_output_kernel, in_specs=[smem, vmem] + [anywhere]...  4.6 us
  transfers between devices with their start and end apart: 21, of which 5 were waited for; matrix products, arithmetic and copies ran while one was open for 0% of the time, Pallas kernels for 19%

profile of v5, /device:TPU:32, one launch (start us, length us, event | category | flops | bytes accessed | tf_op | source)
XLA Modules:
  0.0 88.3 jit_solution(18149525070203896630)
XLA Ops:
  0.6 9.0 %projections.1 = (bf16[4,512,128]{2,1,0:T(8,128)(2,1)}, bf16[528,256]{1,0:T(8,128)(2,1)}, bf16[32,8,512]{2,1,0:T(8,128)(2,1)}) custom-call(s32[32]{0:T(128)} %len_ref.5, bf16[512,4096]{1,0:T(8,128)(2,1)} %x_hbm.1, bf16[8,4096]{1,0:T(8,128)(2,1)} %question_hbm.1, f32[1,4096]{1,0:T(1,128)} %bitcast.1, bf16[4096,512]{1,0:T(8,128)(2,1)} %wq_hbm.1, ...), custom_call_target="tpu_custom_call" | custom-call | flops 3221225472 | bytes 12582912 | tf_op jit(solution)/shard_map/projections/pallas_call | solution.py:189
  9.7 0.8 collective-permute-start
  10.5 0.7 collective-permute-start.1
  11.2 0.7 collective-permute-start.2
  11.9 11.6 %all-to-all-start = ((bf16[32,8,512]{2,1,0:T(8,128)(2,1)}), bf16[32,8,512]{2,1,0:T(8,128)(2,1)S(1)}, u32[]{:S(2)}, u32[]{:S(2)}) async-start(bf16[32,8,512]{2,1,0:T(8,128)(2,1)} %get-tuple-element.29), calls=%async_computation | async-start | bytes 524288 | tf_op jit(solution)/shard_map/all_to_all | solution.py:506
  23.6 1.3 %collective-permute-start.3 = (bf16[528,256]{1,0:T(8,128)(2,1)S(1)}, bf16[528,256]{1,0:T(8,128)(2,1)S(1)}, u32[]{:S(2)}, u32[]{:S(2)}) collective-permute-start(bf16[528,256]{1,0:T(8,128)(2,1)S(1)} %add_add_fusion.1.refs_0_), channel_id=1, source_target_pairs={{0,8},{24,32},{40,48},{128,152},{1,9},{25,33},{41,49},{129,153},{2... | collective-permute-start | bytes 811016 | tf_op jit(solution)/shard_map/ppermute | solution.py:508
  24.9 0.7 collective-permute-start.4
  25.6 10.3 %all-to-all-done.queries_ref = bf16[32,8,512]{2,1,0:T(8,128)(2,1)S(1)} async-done(((bf16[32,8,512]{2,1,0:T(8,128)(2,1)}), bf16[32,8,512]{2,1,0:T(8,128)(2,1)S(1)}, u32[]{:S(2)}, u32[]{:S(2)}) %all-to-all-start) | async-done | bytes 262176 | tf_op jit(solution)/shard_map/all_to_all | solution.py:506
  35.9 1.0 %copy-done = bf16[528,256]{1,0:T(8,128)(2,1)S(1)} copy-done((bf16[528,256]{1,0:T(8,128)(2,1)S(1)}, bf16[528,256]{1,0:T(8,128)(2,1)}, u32[]{:S(2)}) %copy-start) | copy-done | bytes 270360
  36.8 3.0 %question_attention.1 = (f32[32,8,640]{2,1,0:T(8,128)}, f32[8,128]{1,0:T(8,128)S(1)}) custom-call(s32[32]{0:T(128)S(1)} %copy-done.3, bf16[32,8,512]{2,1,0:T(8,128)(2,1)S(1)} %all-to-all-done.queries_ref, bf16[528,256]{1,0:T(8,128)(2,1)S(1)} %copy-done), custom_call_target="tpu_custom_call" | custom-call | flops 671088640 | bytes 1048576 | tf_op jit(solution)/shard_map/question_attention/pallas_call | solution.py:249
  39.9 2.5 %collective-permute-start.5 = (bf16[528,256]{1,0:T(8,128)(2,1)S(1)}, bf16[528,256]{1,0:T(8,128)(2,1)S(1)}, u32[]{:S(2)}, u32[]{:S(2)}) collective-permute-start(bf16[528,256]{1,0:T(8,128)(2,1)S(1)} %sum_of.1), channel_id=1, source_target_pairs={{0,64},{8,72},{16,80},{24,88},{32,96},{40,104},{48,112},{56,120},{... | collective-permute-start | bytes 811016 | tf_op jit(solution)/shard_map/ppermute | solution.py:516
  42.5 1.3 %collective-permute-start.6 = (bf16[528,256]{1,0:T(8,128)(2,1)S(1)}, bf16[528,256]{1,0:T(8,128)(2,1)S(1)}, u32[]{:S(2)}, u32[]{:S(2)}) collective-permute-start(bf16[528,256]{1,0:T(8,128)(2,1)S(1)} %sum_of.1), channel_id=1, source_target_pairs={{0,192},{8,200},{16,208},{24,216},{32,224},{40,232},{48,240},{56,2... | collective-permute-start | bytes 811016 | tf_op jit(solution)/shard_map/ppermute | solution.py:516
  43.8 5.2 %all-to-all-start.1 = ((f32[32,8,640]{2,1,0:T(8,128)}), f32[32,8,640]{2,1,0:T(8,128)}, u32[]{:S(2)}, u32[]{:S(2)}) async-start(f32[32,8,640]{2,1,0:T(8,128)} %get-tuple-element.43), calls=%async_computation.1 | async-start | bytes 1310720 | tf_op jit(solution)/shard_map/all_to_all | solution.py:517
  49.1 1.0 %copy-done.4 = bf16[4,512,128]{2,1,0:T(8,128)(2,1)S(1)} copy-done((bf16[4,512,128]{2,1,0:T(8,128)(2,1)S(1)}, bf16[4,512,128]{2,1,0:T(8,128)(2,1)}, u32[]{:S(2)}) %copy-start.4) | copy-done | bytes 524312
  50.1 7.4 %context_attention.1 = (bf16[512,512]{1,0:T(8,128)(2,1)S(1)}, bf16[512,512]{1,0:T(8,128)(2,1)S(1)}, bf16[512,512]{1,0:T(8,128)(2,1)S(1)}, bf16[512,512]{1,0:T(8,...) custom-call(s32[32]{0:T(128)S(1)} %copy-done.3, ...), custom_call_target="tpu_custom_call" | custom-call | flops 21474836480 | bytes 4194304 | tf_op jit(solution)/shard_map/context_attention/pallas_call | solution.py:328
  57.7 0.5 collective-permute-start.8
  58.9 0.5 collective-permute-start.7
  59.6 0.8 across_sum.1
  60.3 1.6 %collective-permute-start.11 = (bf16[256,512]{1,0:T(8,128)(2,1)}, bf16[256,512]{1,0:T(8,128)(2,1)S(1)}, u32[]{:S(2)}, u32[]{:S(2)}) collective-permute-start(bf16[256,512]{1,0:T(8,128)(2,1)} %get-tuple-element.41._), channel_id=1, source_target_pairs={{0,2},{1,3},{2,4},{3,5},{4,6},{5,7},{6,0},{7,1},{8,10},{9,11},{10,... | collective-permute-start | bytes 786440 | tf_op jit(solution)/shard_map/ppermute | solution.py:486
  61.9 1.7 %collective-permute-start.12 = (bf16[256,512]{1,0:T(8,128)(2,1)S(1)}, bf16[256,512]{1,0:T(8,128)(2,1)S(1)}, u32[]{:S(2)}, u32[]{:S(2)}) collective-permute-start(bf16[256,512]{1,0:T(8,128)(2,1)S(1)} %get-tuple-element.42), channel_id=1, source_target_pairs={{0,6},{1,7},{2,0},{3,1},{4,2},{5,3},{6,4},{7,5},{8,14},{9,15},{10,... | collective-permute-start | bytes 786440 | tf_op jit(solution)/shard_map/ppermute | solution.py:486
  63.6 0.9 %others_sum.1 = (bf16[256,512]{1,0:T(8,128)(2,1)S(1)}, bf16[256,512]{1,0:T(8,128)(2,1)}, bf16[256,512]{1,0:T(8,128)(2,1)}, bf16[256,512]{1,0:T(8,128)(2,1)S(1)}) custom-call(bf16[512,512]{1,0:T(8,128)(2,1)S(1)} %get-tuple-element.33.near_keep, bf16[512,512]{1,0:T(8,128)(2,1)S(1)} %collective-permute-done.8.near_got, ...), custom_call_target="tpu_custom_call" | custom-call | tf_op jit(solution)/shard_map/others_sum/pallas_call | solution.py:403
  64.5 0.4 collective-permute-start.14
  64.9 2.9 %collective-permute-start.15 = (bf16[256,512]{1,0:T(8,128)(2,1)}, bf16[256,512]{1,0:T(8,128)(2,1)S(1)}, u32[]{:S(2)}, u32[]{:S(2)}) collective-permute-start(bf16[256,512]{1,0:T(8,128)(2,1)} %get-tuple-element.47), channel_id=1, source_target_pairs={{0,6},{1,7},{2,0},{3,1},{4,2},{5,3},{6,4},{7,5},{8,14},{9,15},{10,... | collective-permute-start | bytes 786440 | tf_op jit(solution)/shard_map/ppermute | solution.py:486
  67.8 0.7 all-to-all-done.1.parts_ref
  68.5 4.6 %question_output.1 = (bf16[4,16,512]{2,1,0:T(8,128)(2,1)}, bf16[4,16,512]{2,1,0:T(8,128)(2,1)}) custom-call(s32[1]{0:T(128)S(6)} %copy.15.qlen_ref, f32[32,8,640]{2,1,0:T(8,128)} %all-to-all-done.1.parts_ref, bf16[512,4096]{1,0:T(8,128)(2,1)} %w_hbm.3, bf16[256,512]{1,0:T(8,128)(2,1)} %get-tuple-element.41._), custom_call_target="tpu_custom_call" | custom-call | flops 107374182400 | bytes 4194304 | tf_op jit(solution)/shard_map/question_output/pallas_call | solution.py:359
  73.2 2.6 %collective-permute-done.14._.left_b = bf16[256,512]{1,0:T(8,128)(2,1)S(1)} collective-permute-done((bf16[256,512]{1,0:T(8,128)(2,1)}, bf16[256,512]{1,0:T(8,128)(2,1)S(1)}, u32[]{:S(2)}, u32[]{:S(2)}) %collective-permute-start.14) | collective-permute-done | bytes 262176 | tf_op jit(solution)/shard_map/ppermute | solution.py:486
  75.8 0.8 copy-done.2
  76.8 1.5 %collective-permute-start.16 = (bf16[272,512]{1,0:T(8,128)(2,1)S(1)}, bf16[272,512]{1,0:T(8,128)(2,1)S(1)}, u32[]{:S(2)}, u32[]{:S(2)}) collective-permute-start(bf16[272,512]{1,0:T(8,128)(2,1)S(1)} %get-tuple-element.48), channel_id=1, source_target_pairs={{0,2},{1,3},{2,4},{3,5},{4,6},{5,7},{6,0},{7,1},{8,10},{9,11},{10,... | collective-permute-start | bytes 835592 | tf_op jit(solution)/shard_map/ppermute | solution.py:486
  78.3 1.8 %collective-permute-start.17 = (bf16[272,512]{1,0:T(8,128)(2,1)S(1)}, bf16[272,512]{1,0:T(8,128)(2,1)S(1)}, u32[]{:S(2)}, u32[]{:S(2)}) collective-permute-start(bf16[272,512]{1,0:T(8,128)(2,1)S(1)} %get-tuple-element.49), channel_id=1, source_target_pairs={{0,6},{1,7},{2,0},{3,1},{4,2},{5,3},{6,4},{7,5},{8,14},{9,15},{10,... | collective-permute-start | bytes 835592 | tf_op jit(solution)/shard_map/ppermute | solution.py:486
  80.1 1.5 %collective-permute-start.18 = (bf16[16,512]{1,0:T(8,128)(2,1)S(1)}, bf16[16,512]{1,0:T(8,128)(2,1)S(1)}, u32[]{:S(2)}, u32[]{:S(2)}) collective-permute-start(bf16[16,512]{1,0:T(8,128)(2,1)S(1)} %get-tuple-element.51), channel_id=1, source_target_pairs={{0,4},{1,5},{2,6},{3,7},{4,0},{5,1},{6,2},{7,3},{8,12},{9,13},{10,... | collective-permute-start | bytes 49160 | tf_op jit(solution)/shard_map/ppermute | solution.py:486
  81.6 5.6 %collective-permute-done.18.q_across = bf16[16,512]{1,0:T(8,128)(2,1)S(1)} collective-permute-done((bf16[16,512]{1,0:T(8,128)(2,1)S(1)}, bf16[16,512]{1,0:T(8,128)(2,1)S(1)}, u32[]{:S(2)}, u32[]{:S(2)}) %collective-permute-start.18) | collective-permute-done | bytes 16416 | tf_op jit(solution)/shard_map/ppermute | solution.py:486
  87.2 1.1 %finish.1 = (bf16[512,512]{1,0:T(8,128)(2,1)}, bf16[8,512]{1,0:T(8,128)(2,1)}) custom-call(bf16[512,512]{1,0:T(8,128)(2,1)S(1)} %get-tuple-element.31.keep, bf16[512,512]{1,0:T(8,128)(2,1)S(1)} %collective-permute-done.7.got, bf16[272,512]{1,0:T(8,128)(2,1)S(1)} %collective-permute-done.16.left_a, bf16[256,512]{1,0:T(8,128)(2,1)S(1)} %collective-permute-done.14._.left_b, ...), custom_call_target="tpu_custom_call" | custom-call | flops 1048576 | bytes 2621440 | tf_op jit(solution)/shard_map/finish/pallas_call | solution.py:447
  (31 shorter events, 0.9 us)
Async XLA Ops:
  0.6 35.3 %copy-start.3 = (s32[32]{0:T(128)S(1)}, s32[32]{0:T(128)}, u32[]{:S(2)}) copy-start(s32[32]{0:T(128)} %len_ref.5) | copy-start | bytes 388
  9.7 39.4 %copy-start.1 = (bf16[528,256]{1,0:T(8,128)(2,1)S(1)}, bf16[528,256]{1,0:T(8,128)(2,1)}, u32[]{:S(2)}) copy-start(bf16[528,256]{1,0:T(8,128)(2,1)} %get-tuple-element.28.kv_ref) | copy-start | bytes 811012
  9.7 13.8 %collective-permute-start = (bf16[528,256]{1,0:T(8,128)(2,1)}, bf16[528,256]{1,0:T(8,128)(2,1)S(1)}, u32[]{:S(2)}, u32[]{:S(2)}) collective-permute-start(bf16[528,256]{1,0:T(8,128)(2,1)} %get-tuple-element.28.kv_ref), channel_id=1, source_target_pairs={{0,128},{1,129},{2,130},{3,131},{4,132},{5,133},{6,134},{7,135}} | collective-permute-start | bytes 811016 | tf_op jit(solution)/shard_map/ppermute | solution.py:503
  10.5 13.0 %collective-permute-start.1 = (bf16[528,256]{1,0:T(8,128)(2,1)}, bf16[528,256]{1,0:T(8,128)(2,1)S(1)}, u32[]{:S(2)}, u32[]{:S(2)}) collective-permute-start(bf16[528,256]{1,0:T(8,128)(2,1)} %get-tuple-element.28.kv_ref), channel_id=1, source_target_pairs={{0,24},{1,25},{2,26},{3,27},{4,28},{5,29},{6,30},{7,31}} | collective-permute-start | bytes 811016 | tf_op jit(solution)/shard_map/ppermute | solution.py:504
  11.2 12.3 %collective-permute-start.2 = (bf16[528,256]{1,0:T(8,128)(2,1)}, bf16[528,256]{1,0:T(8,128)(2,1)S(1)}, u32[]{:S(2)}, u32[]{:S(2)}) collective-permute-start(bf16[528,256]{1,0:T(8,128)(2,1)} %get-tuple-element.28.kv_ref), channel_id=1, source_target_pairs={{0,40},{1,41},{2,42},{3,43},{4,44},{5,45},{6,46},{7,47}} | collective-permute-start | bytes 811016 | tf_op jit(solution)/shard_map/ppermute | solution.py:505
  11.9 24.0 %all-to-all-start = ((bf16[32,8,512]{2,1,0:T(8,128)(2,1)}), bf16[32,8,512]{2,1,0:T(8,128)(2,1)S(1)}, u32[]{:S(2)}, u32[]{:S(2)}) async-start(bf16[32,8,512]{2,1,0:T(8,128)(2,1)} %get-tuple-element.29), calls=%async_computation | async-start | bytes 524288 | tf_op jit(solution)/shard_map/all_to_all | solution.py:506
  23.6 16.2 %collective-permute-start.3 = (bf16[528,256]{1,0:T(8,128)(2,1)S(1)}, bf16[528,256]{1,0:T(8,128)(2,1)S(1)}, u32[]{:S(2)}, u32[]{:S(2)}) collective-permute-start(bf16[528,256]{1,0:T(8,128)(2,1)S(1)} %add_add_fusion.1.refs_0_), channel_id=1, source_target_pairs={{0,8},{24,32},{40,48},{128,152},{1,9},{25,33},{41,49},{129,153},{2... | collective-permute-start | bytes 811016 | tf_op jit(solution)/shard_map/ppermute | solution.py:508
  24.9 14.9 %collective-permute-start.4 = (bf16[528,256]{1,0:T(8,128)(2,1)S(1)}, bf16[528,256]{1,0:T(8,128)(2,1)S(1)}, u32[]{:S(2)}, u32[]{:S(2)}) collective-permute-start(bf16[528,256]{1,0:T(8,128)(2,1)S(1)} %add_add_fusion.1.refs_0_), channel_id=1, source_target_pairs={{0,56},{24,16},{128,168},{1,57},{25,17},{129,169},{2,58},{26,18},{... | collective-permute-start | bytes 811016 | tf_op jit(solution)/shard_map/ppermute | solution.py:509
  35.9 1.0 %copy-start = (bf16[528,256]{1,0:T(8,128)(2,1)S(1)}, bf16[528,256]{1,0:T(8,128)(2,1)}, u32[]{:S(2)}) copy-start(bf16[528,256]{1,0:T(8,128)(2,1)} %get-tuple-element.28.kv_ref) | copy-start | bytes 811012
  39.9 9.1 %collective-permute-start.5 = (bf16[528,256]{1,0:T(8,128)(2,1)S(1)}, bf16[528,256]{1,0:T(8,128)(2,1)S(1)}, u32[]{:S(2)}, u32[]{:S(2)}) collective-permute-start(bf16[528,256]{1,0:T(8,128)(2,1)S(1)} %sum_of.1), channel_id=1, source_target_pairs={{0,64},{8,72},{16,80},{24,88},{32,96},{40,104},{48,112},{56,120},{... | collective-permute-start | bytes 811016 | tf_op jit(solution)/shard_map/ppermute | solution.py:516
  42.5 6.5 %collective-permute-start.6 = (bf16[528,256]{1,0:T(8,128)(2,1)S(1)}, bf16[528,256]{1,0:T(8,128)(2,1)S(1)}, u32[]{:S(2)}, u32[]{:S(2)}) collective-permute-start(bf16[528,256]{1,0:T(8,128)(2,1)S(1)} %sum_of.1), channel_id=1, source_target_pairs={{0,192},{8,200},{16,208},{24,216},{32,224},{40,232},{48,240},{56,2... | collective-permute-start | bytes 811016 | tf_op jit(solution)/shard_map/ppermute | solution.py:516
  43.8 24.7 %all-to-all-start.1 = ((f32[32,8,640]{2,1,0:T(8,128)}), f32[32,8,640]{2,1,0:T(8,128)}, u32[]{:S(2)}, u32[]{:S(2)}) async-start(f32[32,8,640]{2,1,0:T(8,128)} %get-tuple-element.43), calls=%async_computation.1 | async-start | bytes 1310720 | tf_op jit(solution)/shard_map/all_to_all | solution.py:517
  49.1 1.0 %copy-start.4 = (bf16[4,512,128]{2,1,0:T(8,128)(2,1)S(1)}, bf16[4,512,128]{2,1,0:T(8,128)(2,1)}, u32[]{:S(2)}) copy-start(bf16[4,512,128]{2,1,0:T(8,128)(2,1)} %get-tuple-element.27.q_ref) | copy-start | bytes 1572868
  57.6 2.0 %collective-permute-start.10 = (bf16[512,512]{1,0:T(8,128)(2,1)S(1)}, bf16[512,512]{1,0:T(8,128)(2,1)S(1)}, u32[]{:S(2)}, u32[]{:S(2)}) collective-permute-start(bf16[512,512]{1,0:T(8,128)(2,1)S(1)} %get-tuple-element.40), channel_id=1, source_target_pairs={{0,1},{1,0},{2,3},{3,2},{4,5},{5,4},{6,7},{7,6},{8,9},{9,8},{10,11... | collective-permute-start | bytes 1572872 | tf_op jit(solution)/shard_map/ppermute | solution.py:491
  57.7 5.9 %collective-permute-start.8 = (bf16[512,512]{1,0:T(8,128)(2,1)S(1)}, bf16[512,512]{1,0:T(8,128)(2,1)S(1)}, u32[]{:S(2)}, u32[]{:S(2)}) collective-permute-start(bf16[512,512]{1,0:T(8,128)(2,1)S(1)} %get-tuple-element.34), channel_id=1, source_target_pairs={{0,1},{1,0},{2,3},{3,2},{4,5},{5,4},{6,7},{7,6},{8,9},{9,8},{10,11... | collective-permute-start | bytes 1572872 | tf_op jit(solution)/shard_map/ppermute | solution.py:491
  58.2 5.4 %collective-permute-start.9 = (bf16[512,512]{1,0:T(8,128)(2,1)S(1)}, bf16[512,512]{1,0:T(8,128)(2,1)S(1)}, u32[]{:S(2)}, u32[]{:S(2)}) collective-permute-start(bf16[512,512]{1,0:T(8,128)(2,1)S(1)} %get-tuple-element.36), channel_id=1, source_target_pairs={{0,1},{1,0},{2,3},{3,2},{4,5},{5,4},{6,7},{7,6},{8,9},{9,8},{10,11... | collective-permute-start | bytes 1572872 | tf_op jit(solution)/shard_map/ppermute | solution.py:491
  58.9 22.7 %collective-permute-start.7 = (bf16[512,512]{1,0:T(8,128)(2,1)S(1)}, bf16[512,512]{1,0:T(8,128)(2,1)S(1)}, u32[]{:S(2)}, u32[]{:S(2)}) collective-permute-start(bf16[512,512]{1,0:T(8,128)(2,1)S(1)} %get-tuple-element.32), channel_id=1, source_target_pairs={{0,1},{1,0},{2,3},{3,2},{4,5},{5,4},{6,7},{7,6},{8,9},{9,8},{10,11... | collective-permute-start | bytes 1572872 | tf_op jit(solution)/shard_map/ppermute | solution.py:491
  60.3 12.7 %collective-permute-start.11 = (bf16[256,512]{1,0:T(8,128)(2,1)}, bf16[256,512]{1,0:T(8,128)(2,1)S(1)}, u32[]{:S(2)}, u32[]{:S(2)}) collective-permute-start(bf16[256,512]{1,0:T(8,128)(2,1)} %get-tuple-element.41._), channel_id=1, source_target_pairs={{0,2},{1,3},{2,4},{3,5},{4,6},{5,7},{6,0},{7,1},{8,10},{9,11},{10,... | collective-permute-start | bytes 786440 | tf_op jit(solution)/shard_map/ppermute | solution.py:486
  61.9 11.3 %collective-permute-start.12 = (bf16[256,512]{1,0:T(8,128)(2,1)S(1)}, bf16[256,512]{1,0:T(8,128)(2,1)S(1)}, u32[]{:S(2)}, u32[]{:S(2)}) collective-permute-start(bf16[256,512]{1,0:T(8,128)(2,1)S(1)} %get-tuple-element.42), channel_id=1, source_target_pairs={{0,6},{1,7},{2,0},{3,1},{4,2},{5,3},{6,4},{7,5},{8,14},{9,15},{10,... | collective-permute-start | bytes 786440 | tf_op jit(solution)/shard_map/ppermute | solution.py:486
  64.5 11.3 %collective-permute-start.14 = (bf16[256,512]{1,0:T(8,128)(2,1)}, bf16[256,512]{1,0:T(8,128)(2,1)S(1)}, u32[]{:S(2)}, u32[]{:S(2)}) collective-permute-start(bf16[256,512]{1,0:T(8,128)(2,1)} %get-tuple-element.46), channel_id=1, source_target_pairs={{0,2},{1,3},{2,4},{3,5},{4,6},{5,7},{6,0},{7,1},{8,10},{9,11},{10,... | collective-permute-start | bytes 786440 | tf_op jit(solution)/shard_map/ppermute | solution.py:486
  64.9 10.9 %collective-permute-start.15 = (bf16[256,512]{1,0:T(8,128)(2,1)}, bf16[256,512]{1,0:T(8,128)(2,1)S(1)}, u32[]{:S(2)}, u32[]{:S(2)}) collective-permute-start(bf16[256,512]{1,0:T(8,128)(2,1)} %get-tuple-element.47), channel_id=1, source_target_pairs={{0,6},{1,7},{2,0},{3,1},{4,2},{5,3},{6,4},{7,5},{8,14},{9,15},{10,... | collective-permute-start | bytes 786440 | tf_op jit(solution)/shard_map/ppermute | solution.py:486
  73.1 2.7 %collective-permute-start.13 = (bf16[4,16,512]{2,1,0:T(8,128)(2,1)}, bf16[4,16,512]{2,1,0:T(8,128)(2,1)S(1)}, u32[]{:S(2)}, u32[]{:S(2)}) collective-permute-start(bf16[4,16,512]{2,1,0:T(8,128)(2,1)} %get-tuple-element.45), channel_id=1, source_target_pairs={{0,1},{1,0},{2,3},{3,2},{4,5},{5,4},{6,7},{7,6},{8,9},{9,8},{10,11... | collective-permute-start | bytes 196616 | tf_op jit(solution)/shard_map/ppermute | solution.py:491
  75.8 0.8 copy-start.2
  76.8 10.4 %collective-permute-start.16 = (bf16[272,512]{1,0:T(8,128)(2,1)S(1)}, bf16[272,512]{1,0:T(8,128)(2,1)S(1)}, u32[]{:S(2)}, u32[]{:S(2)}) collective-permute-start(bf16[272,512]{1,0:T(8,128)(2,1)S(1)} %get-tuple-element.48), channel_id=1, source_target_pairs={{0,2},{1,3},{2,4},{3,5},{4,6},{5,7},{6,0},{7,1},{8,10},{9,11},{10,... | collective-permute-start | bytes 835592 | tf_op jit(solution)/shard_map/ppermute | solution.py:486
  78.3 8.9 %collective-permute-start.17 = (bf16[272,512]{1,0:T(8,128)(2,1)S(1)}, bf16[272,512]{1,0:T(8,128)(2,1)S(1)}, u32[]{:S(2)}, u32[]{:S(2)}) collective-permute-start(bf16[272,512]{1,0:T(8,128)(2,1)S(1)} %get-tuple-element.49), channel_id=1, source_target_pairs={{0,6},{1,7},{2,0},{3,1},{4,2},{5,3},{6,4},{7,5},{8,14},{9,15},{10,... | collective-permute-start | bytes 835592 | tf_op jit(solution)/shard_map/ppermute | solution.py:486
  80.1 7.1 %collective-permute-start.18 = (bf16[16,512]{1,0:T(8,128)(2,1)S(1)}, bf16[16,512]{1,0:T(8,128)(2,1)S(1)}, u32[]{:S(2)}, u32[]{:S(2)}) collective-permute-start(bf16[16,512]{1,0:T(8,128)(2,1)S(1)} %get-tuple-element.51), channel_id=1, source_target_pairs={{0,4},{1,5},{2,6},{3,7},{4,0},{5,1},{6,2},{7,3},{8,12},{9,13},{10,... | collective-permute-start | bytes 49160 | tf_op jit(solution)/shard_map/ppermute | solution.py:486

commit v6 on v5

--- a/solution.py
+++ b/solution.py
@@ -280,9 +280,10 @@
 
 
 def context_kernel(
-    len_ref, q_ref, kv_ref, akv_ref, w_hbm, _, *refs
+    len_ref, q_ref, kv_ref, held_ref, left_ref, right_ref, w_hbm, _, *refs
 ):
-    keep_refs, send_refs, (att_ref, w_ref, sems) = refs[:NY], refs[NY : 2 * NY], refs[2 * NY :]
+    keep_refs, send_refs, (att_ref, akv_ref, w_ref, sems) = refs[:NY], refs[NY : 2 * NY], refs[2 * NY :]
+    akv_ref[...] = held_ref[...] + left_ref[...] + right_ref[...]
     blk_at, kv_at = lax.axis_index("blk"), lax.axis_index("kv")
     y_at, c_at = kv_at // NC, lax.rem(kv_at, NC)
     shares = []
@@ -324,21 +325,22 @@
             ref[...] = dot(att_ref[...], w_ref[i, :, columns]).astype(bf16)
 
 
-def context_attention(block_len, q, kv, anchor, w_out, after):
+def context_attention(block_len, q, kv, anchors, w_out, after):
     return pl.pallas_call(
         context_kernel,
-        in_specs=[smem] + [vmem] * 3 + [anywhere] * 2,
+        in_specs=[smem] + [vmem] * 5 + [anywhere] * 2,
         out_specs=[vmem] * (2 * NY),
         out_shape=[jax.ShapeDtypeStruct((BLK, FEAT), bf16)] * (2 * NY),
         scratch_shapes=[
             pltpu.VMEM((BLK, HEADS * HD), bf16),
+            pltpu.VMEM((BLK + QPAD, 2 * HD), bf16),
             pltpu.VMEM((NY, HEADS * HD, NC * FEAT), bf16),
             pltpu.SemaphoreType.DMA((NY,)),
         ],
         compiler_params=params(47),
         cost_estimate=cost(HEADS * BLK * BLK * HD * 8 * 20, 4 * 2**20, HEADS * BLK * BLK),
         name="context_attention",
-    )(block_len, q, kv, anchor, w_out, after)
+    )(block_len, q, kv, *anchors, w_out, after)
 
 
 def question_output_kernel(qlen_ref, parts_ref, w_hbm, _, keep_ref, send_ref, w_ref, sem):
@@ -509,14 +511,14 @@
     third = lax.ppermute(held, "blk", to_blocks({**within[1], (2, 0): (2, 5)}))
     parts, token = question_attention(block_len, queries, kv)
     held = sum_of(held, second, third, after=token)
-    anchor = held
+    anchors = [held]
     for x, pairs in zip((1, 3), within):
         pairs = {(2, a): (2, b) for (_, a), (_, b) in pairs.items()}
         across = {(0, z): (x, z) for z in range(NZ)}
-        anchor = anchor + lax.ppermute(held, "blk", to_blocks({**across, **pairs}))
+        anchors.append(lax.ppermute(held, "blk", to_blocks({**across, **pairs})))
     parts = lax.all_to_all(parts, "blk", 0, 0)
 
-    products = context_attention(block_len, q, kv, anchor, w_out, token)
+    products = context_attention(block_len, q, kv, anchors, w_out, token)
     keep, send = products[:NY], products[NY:]
     first, second = across_sum(keep[2], swap_cores(send[2]))
     near_a, near_b, far_a, far_b = others_sum(

time: 89.4 us -> 89.1 us (level)
  local copies, waits for them, and re-layouts: 2.84 us -> 1.81 us
    unnamed x10, local copies, waits for them, and re-layouts: 2.84 us -> 1.81 us
    all_to_all x1, waiting for transfers between devices: 0.7 us -> 1.73 us  [body(): parts = lax.all_to_all(parts, 'blk', 0, 0)]
where the time goes in v6:
time: 89.1 us; the launch traced here: 88.2 us
  starting transfers between devices  37.7 us (42%)
  Pallas kernels  27.1 us (30%)
  waiting for transfers between devices  20.1 us (23%)
  local copies, waits for them, and re-layouts  1.81 us (2%)
  between operations  1.52 us (2%)
    all_to_all x1, starting transfers between devices, body(): queries = lax.all_to_all(queries, 'blk', 0, 0)  11.6 us
    ppermute x7, starting transfers between devices, shift_y(): return lax.ppermute(value, 'kv', pairs)  11.6 us
    all_to_all x1, waiting for transfers between devices, body(): queries = lax.all_to_all(queries, 'blk', 0, 0)  10.3 us
    pallas_call x1, Pallas kernels, projections(): pl.pallas_call(projection_kernel, in_specs=[smem, anywhere, anywhere, vme...  9.01 us
    ppermute x7, waiting for transfers between devices, shift_y(): return lax.ppermute(value, 'kv', pairs)  7.87 us
    pallas_call x1, Pallas kernels, context_attention(): pl.pallas_call(context_kernel, in_specs=[smem] + [vmem] * 5 + [anywhere]...  7.49 us
    all_to_all x1, starting transfers between devices, body(): parts = lax.all_to_all(parts, 'blk', 0, 0)  5.21 us
    pallas_call x1, Pallas kernels, question_output(): pl.pallas_call(question_output_kernel, in_specs=[smem, vmem] + [anywhere]...  4.6 us
  transfers between devices with their start and end apart: 21, of which 5 were waited for; matrix products, arithmetic and copies ran while one was open for 0% of the time, Pallas kernels for 19%

profile of v6, /device:TPU:32, one launch (start us, length us, event | category | flops | bytes accessed | tf_op | source)
XLA Modules:
  0.0 88.2 jit_solution(10530991081490810494)
XLA Ops:
  0.6 9.0 %projections.1 = (bf16[4,512,128]{2,1,0:T(8,128)(2,1)}, bf16[528,256]{1,0:T(8,128)(2,1)}, bf16[32,8,512]{2,1,0:T(8,128)(2,1)}) custom-call(s32[32]{0:T(128)} %len_ref.5, bf16[512,4096]{1,0:T(8,128)(2,1)} %x_hbm.1, bf16[8,4096]{1,0:T(8,128)(2,1)} %question_hbm.1, f32[1,4096]{1,0:T(1,128)} %bitcast.1, bf16[4096,512]{1,0:T(8,128)(2,1)} %wq_hbm.1, ...), custom_call_target="tpu_custom_call" | custom-call | flops 3221225472 | bytes 12582912 | tf_op jit(solution)/shard_map/projections/pallas_call | solution.py:189
  9.7 0.8 collective-permute-start
  10.5 0.7 collective-permute-start.1
  11.2 0.7 collective-permute-start.2
  11.9 11.6 %all-to-all-start = ((bf16[32,8,512]{2,1,0:T(8,128)(2,1)}), bf16[32,8,512]{2,1,0:T(8,128)(2,1)S(1)}, u32[]{:S(2)}, u32[]{:S(2)}) async-start(bf16[32,8,512]{2,1,0:T(8,128)(2,1)} %get-tuple-element.29), calls=%async_computation | async-start | bytes 524288 | tf_op jit(solution)/shard_map/all_to_all | solution.py:508
  23.6 1.3 %collective-permute-start.3 = (bf16[528,256]{1,0:T(8,128)(2,1)S(1)}, bf16[528,256]{1,0:T(8,128)(2,1)S(1)}, u32[]{:S(2)}, u32[]{:S(2)}) collective-permute-start(bf16[528,256]{1,0:T(8,128)(2,1)S(1)} %add_add_fusion.refs_0_), channel_id=1, source_target_pairs={{0,8},{24,32},{40,48},{128,152},{1,9},{25,33},{41,49},{129,153},{2... | collective-permute-start | bytes 811016 | tf_op jit(solution)/shard_map/ppermute | solution.py:510
  24.9 0.7 collective-permute-start.4
  25.6 10.3 %all-to-all-done.queries_ref = bf16[32,8,512]{2,1,0:T(8,128)(2,1)S(1)} async-done(((bf16[32,8,512]{2,1,0:T(8,128)(2,1)}), bf16[32,8,512]{2,1,0:T(8,128)(2,1)S(1)}, u32[]{:S(2)}, u32[]{:S(2)}) %all-to-all-start) | async-done | bytes 262176 | tf_op jit(solution)/shard_map/all_to_all | solution.py:508
  35.9 1.0 %copy-done = bf16[528,256]{1,0:T(8,128)(2,1)S(1)} copy-done((bf16[528,256]{1,0:T(8,128)(2,1)S(1)}, bf16[528,256]{1,0:T(8,128)(2,1)}, u32[]{:S(2)}) %copy-start) | copy-done | bytes 270360
  36.8 3.0 %question_attention.1 = (f32[32,8,640]{2,1,0:T(8,128)}, f32[8,128]{1,0:T(8,128)S(1)}) custom-call(s32[32]{0:T(128)S(1)} %copy-done.3, bf16[32,8,512]{2,1,0:T(8,128)(2,1)S(1)} %all-to-all-done.queries_ref, bf16[528,256]{1,0:T(8,128)(2,1)S(1)} %copy-done), custom_call_target="tpu_custom_call" | custom-call | flops 671088640 | bytes 1048576 | tf_op jit(solution)/shard_map/question_attention/pallas_call | solution.py:249
  39.9 2.5 %collective-permute-start.5 = (bf16[528,256]{1,0:T(8,128)(2,1)S(1)}, bf16[528,256]{1,0:T(8,128)(2,1)S(1)}, u32[]{:S(2)}, u32[]{:S(2)}) collective-permute-start(bf16[528,256]{1,0:T(8,128)(2,1)S(1)} %sum_of.1.held_ref), channel_id=1, source_target_pairs={{0,64},{8,72},{16,80},{24,88},{32,96},{40,104},{48,112},{56,120},{... | collective-permute-start | bytes 811016 | tf_op jit(solution)/shard_map/ppermute | solution.py:518
  42.5 1.3 %collective-permute-start.6 = (bf16[528,256]{1,0:T(8,128)(2,1)S(1)}, bf16[528,256]{1,0:T(8,128)(2,1)S(1)}, u32[]{:S(2)}, u32[]{:S(2)}) collective-permute-start(bf16[528,256]{1,0:T(8,128)(2,1)S(1)} %sum_of.1.held_ref), channel_id=1, source_target_pairs={{0,192},{8,200},{16,208},{24,216},{32,224},{40,232},{48,240},{56,2... | collective-permute-start | bytes 811016 | tf_op jit(solution)/shard_map/ppermute | solution.py:518
  43.8 5.2 %all-to-all-start.1 = ((f32[32,8,640]{2,1,0:T(8,128)}), f32[32,8,640]{2,1,0:T(8,128)}, u32[]{:S(2)}, u32[]{:S(2)}) async-start(f32[32,8,640]{2,1,0:T(8,128)} %get-tuple-element.43), calls=%async_computation.1 | async-start | bytes 1310720 | tf_op jit(solution)/shard_map/all_to_all | solution.py:519
  49.1 7.5 %context_attention.1 = (bf16[512,512]{1,0:T(8,128)(2,1)S(1)}, bf16[512,512]{1,0:T(8,128)(2,1)S(1)}, bf16[512,512]{1,0:T(8,128)(2,1)S(1)}, bf16[512,512]{1,0:T(8,...) custom-call(s32[32]{0:T(128)S(1)} %copy-done.3, ...), custom_call_target="tpu_custom_call" | custom-call | flops 21474836480 | bytes 4194304 | tf_op jit(solution)/shard_map/context_attention/pallas_call | solution.py:329
  56.7 0.5 collective-permute-start.8
  57.9 0.5 collective-permute-start.7
  58.4 0.1 collective-permute-done.10.got_ref
  58.5 0.8 across_sum.1
  59.3 1.6 %collective-permute-start.11 = (bf16[256,512]{1,0:T(8,128)(2,1)}, bf16[256,512]{1,0:T(8,128)(2,1)S(1)}, u32[]{:S(2)}, u32[]{:S(2)}) collective-permute-start(bf16[256,512]{1,0:T(8,128)(2,1)} %get-tuple-element.41._), channel_id=1, source_target_pairs={{0,2},{1,3},{2,4},{3,5},{4,6},{5,7},{6,0},{7,1},{8,10},{9,11},{10,... | collective-permute-start | bytes 786440 | tf_op jit(solution)/shard_map/ppermute | solution.py:488
  60.9 1.7 %collective-permute-start.12 = (bf16[256,512]{1,0:T(8,128)(2,1)S(1)}, bf16[256,512]{1,0:T(8,128)(2,1)S(1)}, u32[]{:S(2)}, u32[]{:S(2)}) collective-permute-start(bf16[256,512]{1,0:T(8,128)(2,1)S(1)} %get-tuple-element.42), channel_id=1, source_target_pairs={{0,6},{1,7},{2,0},{3,1},{4,2},{5,3},{6,4},{7,5},{8,14},{9,15},{10,... | collective-permute-start | bytes 786440 | tf_op jit(solution)/shard_map/ppermute | solution.py:488
  62.6 0.9 %others_sum.1 = (bf16[256,512]{1,0:T(8,128)(2,1)S(1)}, bf16[256,512]{1,0:T(8,128)(2,1)}, bf16[256,512]{1,0:T(8,128)(2,1)}, bf16[256,512]{1,0:T(8,128)(2,1)S(1)}) custom-call(bf16[512,512]{1,0:T(8,128)(2,1)S(1)} %get-tuple-element.33.near_keep, bf16[512,512]{1,0:T(8,128)(2,1)S(1)} %collective-permute-done.8.near_got, ...), custom_call_target="tpu_custom_call" | custom-call | tf_op jit(solution)/shard_map/others_sum/pallas_call | solution.py:405
  63.5 0.4 collective-permute-start.14
  63.9 2.9 %collective-permute-start.15 = (bf16[256,512]{1,0:T(8,128)(2,1)}, bf16[256,512]{1,0:T(8,128)(2,1)S(1)}, u32[]{:S(2)}, u32[]{:S(2)}) collective-permute-start(bf16[256,512]{1,0:T(8,128)(2,1)} %get-tuple-element.47), channel_id=1, source_target_pairs={{0,6},{1,7},{2,0},{3,1},{4,2},{5,3},{6,4},{7,5},{8,14},{9,15},{10,... | collective-permute-start | bytes 786440 | tf_op jit(solution)/shard_map/ppermute | solution.py:488
  66.8 1.7 %all-to-all-done.1.parts_ref = f32[32,8,640]{2,1,0:T(8,128)} async-done(((f32[32,8,640]{2,1,0:T(8,128)}), f32[32,8,640]{2,1,0:T(8,128)}, u32[]{:S(2)}, u32[]{:S(2)}) %all-to-all-start.1) | async-done | bytes 655392 | tf_op jit(solution)/shard_map/all_to_all | solution.py:519
  68.5 4.6 %question_output.1 = (bf16[4,16,512]{2,1,0:T(8,128)(2,1)}, bf16[4,16,512]{2,1,0:T(8,128)(2,1)}) custom-call(s32[1]{0:T(128)S(6)} %copy.15.qlen_ref, f32[32,8,640]{2,1,0:T(8,128)} %all-to-all-done.1.parts_ref, bf16[512,4096]{1,0:T(8,128)(2,1)} %w_hbm.3, bf16[256,512]{1,0:T(8,128)(2,1)} %get-tuple-element.41._), custom_call_target="tpu_custom_call" | custom-call | flops 107374182400 | bytes 4194304 | tf_op jit(solution)/shard_map/question_output/pallas_call | solution.py:361
  73.2 1.6 %collective-permute-done.14._.left_b = bf16[256,512]{1,0:T(8,128)(2,1)S(1)} collective-permute-done((bf16[256,512]{1,0:T(8,128)(2,1)}, bf16[256,512]{1,0:T(8,128)(2,1)S(1)}, u32[]{:S(2)}, u32[]{:S(2)}) %collective-permute-start.14) | collective-permute-done | bytes 262176 | tf_op jit(solution)/shard_map/ppermute | solution.py:488
  74.8 0.8 copy-done.2
  75.8 1.5 %collective-permute-start.16 = (bf16[272,512]{1,0:T(8,128)(2,1)S(1)}, bf16[272,512]{1,0:T(8,128)(2,1)S(1)}, u32[]{:S(2)}, u32[]{:S(2)}) collective-permute-start(bf16[272,512]{1,0:T(8,128)(2,1)S(1)} %get-tuple-element.48), channel_id=1, source_target_pairs={{0,2},{1,3},{2,4},{3,5},{4,6},{5,7},{6,0},{7,1},{8,10},{9,11},{10,... | collective-permute-start | bytes 835592 | tf_op jit(solution)/shard_map/ppermute | solution.py:488
  77.2 1.8 %collective-permute-start.17 = (bf16[272,512]{1,0:T(8,128)(2,1)S(1)}, bf16[272,512]{1,0:T(8,128)(2,1)S(1)}, u32[]{:S(2)}, u32[]{:S(2)}) collective-permute-start(bf16[272,512]{1,0:T(8,128)(2,1)S(1)} %get-tuple-element.49), channel_id=1, source_target_pairs={{0,6},{1,7},{2,0},{3,1},{4,2},{5,3},{6,4},{7,5},{8,14},{9,15},{10,... | collective-permute-start | bytes 835592 | tf_op jit(solution)/shard_map/ppermute | solution.py:488
  79.1 1.8 %collective-permute-start.18 = (bf16[16,512]{1,0:T(8,128)(2,1)S(1)}, bf16[16,512]{1,0:T(8,128)(2,1)S(1)}, u32[]{:S(2)}, u32[]{:S(2)}) collective-permute-start(bf16[16,512]{1,0:T(8,128)(2,1)S(1)} %get-tuple-element.51), channel_id=1, source_target_pairs={{0,4},{1,5},{2,6},{3,7},{4,0},{5,1},{6,2},{7,3},{8,12},{9,13},{10,... | collective-permute-start | bytes 49160 | tf_op jit(solution)/shard_map/ppermute | solution.py:488
  80.9 6.3 %collective-permute-done.18.q_across = bf16[16,512]{1,0:T(8,128)(2,1)S(1)} collective-permute-done((bf16[16,512]{1,0:T(8,128)(2,1)S(1)}, bf16[16,512]{1,0:T(8,128)(2,1)S(1)}, u32[]{:S(2)}, u32[]{:S(2)}) %collective-permute-start.18) | collective-permute-done | bytes 16416 | tf_op jit(solution)/shard_map/ppermute | solution.py:488
  87.2 1.1 %finish.1 = (bf16[512,512]{1,0:T(8,128)(2,1)}, bf16[8,512]{1,0:T(8,128)(2,1)}) custom-call(bf16[512,512]{1,0:T(8,128)(2,1)S(1)} %get-tuple-element.31.keep, bf16[512,512]{1,0:T(8,128)(2,1)S(1)} %collective-permute-done.7.got, bf16[272,512]{1,0:T(8,128)(2,1)S(1)} %collective-permute-done.16.left_a, bf16[256,512]{1,0:T(8,128)(2,1)S(1)} %collective-permute-done.14._.left_b, ...), custom_call_target="tpu_custom_call" | custom-call | flops 1048576 | bytes 2621440 | tf_op jit(solution)/shard_map/finish/pallas_call | solution.py:449
  (30 shorter events, 0.7 us)
Async XLA Ops:
  0.6 35.3 %copy-start.3 = (s32[32]{0:T(128)S(1)}, s32[32]{0:T(128)}, u32[]{:S(2)}) copy-start(s32[32]{0:T(128)} %len_ref.5) | copy-start | bytes 388
  9.7 39.4 %copy-start.1 = (bf16[528,256]{1,0:T(8,128)(2,1)S(1)}, bf16[528,256]{1,0:T(8,128)(2,1)}, u32[]{:S(2)}) copy-start(bf16[528,256]{1,0:T(8,128)(2,1)} %get-tuple-element.28.kv_ref) | copy-start | bytes 811012
  9.7 39.4 %copy-start.4 = (bf16[4,512,128]{2,1,0:T(8,128)(2,1)S(1)}, bf16[4,512,128]{2,1,0:T(8,128)(2,1)}, u32[]{:S(2)}) copy-start(bf16[4,512,128]{2,1,0:T(8,128)(2,1)} %get-tuple-element.27.q_ref) | copy-start | bytes 1572868
  9.7 13.8 %collective-permute-start = (bf16[528,256]{1,0:T(8,128)(2,1)}, bf16[528,256]{1,0:T(8,128)(2,1)S(1)}, u32[]{:S(2)}, u32[]{:S(2)}) collective-permute-start(bf16[528,256]{1,0:T(8,128)(2,1)} %get-tuple-element.28.kv_ref), channel_id=1, source_target_pairs={{0,128},{1,129},{2,130},{3,131},{4,132},{5,133},{6,134},{7,135}} | collective-permute-start | bytes 811016 | tf_op jit(solution)/shard_map/ppermute | solution.py:505
  10.5 13.0 %collective-permute-start.1 = (bf16[528,256]{1,0:T(8,128)(2,1)}, bf16[528,256]{1,0:T(8,128)(2,1)S(1)}, u32[]{:S(2)}, u32[]{:S(2)}) collective-permute-start(bf16[528,256]{1,0:T(8,128)(2,1)} %get-tuple-element.28.kv_ref), channel_id=1, source_target_pairs={{0,24},{1,25},{2,26},{3,27},{4,28},{5,29},{6,30},{7,31}} | collective-permute-start | bytes 811016 | tf_op jit(solution)/shard_map/ppermute | solution.py:506
  11.2 12.3 %collective-permute-start.2 = (bf16[528,256]{1,0:T(8,128)(2,1)}, bf16[528,256]{1,0:T(8,128)(2,1)S(1)}, u32[]{:S(2)}, u32[]{:S(2)}) collective-permute-start(bf16[528,256]{1,0:T(8,128)(2,1)} %get-tuple-element.28.kv_ref), channel_id=1, source_target_pairs={{0,40},{1,41},{2,42},{3,43},{4,44},{5,45},{6,46},{7,47}} | collective-permute-start | bytes 811016 | tf_op jit(solution)/shard_map/ppermute | solution.py:507
  11.9 24.0 %all-to-all-start = ((bf16[32,8,512]{2,1,0:T(8,128)(2,1)}), bf16[32,8,512]{2,1,0:T(8,128)(2,1)S(1)}, u32[]{:S(2)}, u32[]{:S(2)}) async-start(bf16[32,8,512]{2,1,0:T(8,128)(2,1)} %get-tuple-element.29), calls=%async_computation | async-start | bytes 524288 | tf_op jit(solution)/shard_map/all_to_all | solution.py:508
  23.6 16.2 %collective-permute-start.3 = (bf16[528,256]{1,0:T(8,128)(2,1)S(1)}, bf16[528,256]{1,0:T(8,128)(2,1)S(1)}, u32[]{:S(2)}, u32[]{:S(2)}) collective-permute-start(bf16[528,256]{1,0:T(8,128)(2,1)S(1)} %add_add_fusion.refs_0_), channel_id=1, source_target_pairs={{0,8},{24,32},{40,48},{128,152},{1,9},{25,33},{41,49},{129,153},{2... | collective-permute-start | bytes 811016 | tf_op jit(solution)/shard_map/ppermute | solution.py:510
  24.9 14.9 %collective-permute-start.4 = (bf16[528,256]{1,0:T(8,128)(2,1)S(1)}, bf16[528,256]{1,0:T(8,128)(2,1)S(1)}, u32[]{:S(2)}, u32[]{:S(2)}) collective-permute-start(bf16[528,256]{1,0:T(8,128)(2,1)S(1)} %add_add_fusion.refs_0_), channel_id=1, source_target_pairs={{0,56},{24,16},{128,168},{1,57},{25,17},{129,169},{2,58},{26,18},{... | collective-permute-start | bytes 811016 | tf_op jit(solution)/shard_map/ppermute | solution.py:511
  35.9 1.0 %copy-start = (bf16[528,256]{1,0:T(8,128)(2,1)S(1)}, bf16[528,256]{1,0:T(8,128)(2,1)}, u32[]{:S(2)}) copy-start(bf16[528,256]{1,0:T(8,128)(2,1)} %get-tuple-element.28.kv_ref) | copy-start | bytes 811012
  39.9 9.1 %collective-permute-start.5 = (bf16[528,256]{1,0:T(8,128)(2,1)S(1)}, bf16[528,256]{1,0:T(8,128)(2,1)S(1)}, u32[]{:S(2)}, u32[]{:S(2)}) collective-permute-start(bf16[528,256]{1,0:T(8,128)(2,1)S(1)} %sum_of.1.held_ref), channel_id=1, source_target_pairs={{0,64},{8,72},{16,80},{24,88},{32,96},{40,104},{48,112},{56,120},{... | collective-permute-start | bytes 811016 | tf_op jit(solution)/shard_map/ppermute | solution.py:518
  42.5 6.5 %collective-permute-start.6 = (bf16[528,256]{1,0:T(8,128)(2,1)S(1)}, bf16[528,256]{1,0:T(8,128)(2,1)S(1)}, u32[]{:S(2)}, u32[]{:S(2)}) collective-permute-start(bf16[528,256]{1,0:T(8,128)(2,1)S(1)} %sum_of.1.held_ref), channel_id=1, source_target_pairs={{0,192},{8,200},{16,208},{24,216},{32,224},{40,232},{48,240},{56,2... | collective-permute-start | bytes 811016 | tf_op jit(solution)/shard_map/ppermute | solution.py:518
  43.8 24.7 %all-to-all-start.1 = ((f32[32,8,640]{2,1,0:T(8,128)}), f32[32,8,640]{2,1,0:T(8,128)}, u32[]{:S(2)}, u32[]{:S(2)}) async-start(f32[32,8,640]{2,1,0:T(8,128)} %get-tuple-element.43), calls=%async_computation.1 | async-start | bytes 1310720 | tf_op jit(solution)/shard_map/all_to_all | solution.py:519
  56.6 2.0 %collective-permute-start.10 = (bf16[512,512]{1,0:T(8,128)(2,1)S(1)}, bf16[512,512]{1,0:T(8,128)(2,1)S(1)}, u32[]{:S(2)}, u32[]{:S(2)}) collective-permute-start(bf16[512,512]{1,0:T(8,128)(2,1)S(1)} %get-tuple-element.40), channel_id=1, source_target_pairs={{0,1},{1,0},{2,3},{3,2},{4,5},{5,4},{6,7},{7,6},{8,9},{9,8},{10,11... | collective-permute-start | bytes 1572872 | tf_op jit(solution)/shard_map/ppermute | solution.py:493
  56.7 5.9 %collective-permute-start.8 = (bf16[512,512]{1,0:T(8,128)(2,1)S(1)}, bf16[512,512]{1,0:T(8,128)(2,1)S(1)}, u32[]{:S(2)}, u32[]{:S(2)}) collective-permute-start(bf16[512,512]{1,0:T(8,128)(2,1)S(1)} %get-tuple-element.34), channel_id=1, source_target_pairs={{0,1},{1,0},{2,3},{3,2},{4,5},{5,4},{6,7},{7,6},{8,9},{9,8},{10,11... | collective-permute-start | bytes 1572872 | tf_op jit(solution)/shard_map/ppermute | solution.py:493
  57.1 5.4 %collective-permute-start.9 = (bf16[512,512]{1,0:T(8,128)(2,1)S(1)}, bf16[512,512]{1,0:T(8,128)(2,1)S(1)}, u32[]{:S(2)}, u32[]{:S(2)}) collective-permute-start(bf16[512,512]{1,0:T(8,128)(2,1)S(1)} %get-tuple-element.36), channel_id=1, source_target_pairs={{0,1},{1,0},{2,3},{3,2},{4,5},{5,4},{6,7},{7,6},{8,9},{9,8},{10,11... | collective-permute-start | bytes 1572872 | tf_op jit(solution)/shard_map/ppermute | solution.py:493
  57.9 23.0 %collective-permute-start.7 = (bf16[512,512]{1,0:T(8,128)(2,1)S(1)}, bf16[512,512]{1,0:T(8,128)(2,1)S(1)}, u32[]{:S(2)}, u32[]{:S(2)}) collective-permute-start(bf16[512,512]{1,0:T(8,128)(2,1)S(1)} %get-tuple-element.32), channel_id=1, source_target_pairs={{0,1},{1,0},{2,3},{3,2},{4,5},{5,4},{6,7},{7,6},{8,9},{9,8},{10,11... | collective-permute-start | bytes 1572872 | tf_op jit(solution)/shard_map/ppermute | solution.py:493
  59.3 13.8 %collective-permute-start.11 = (bf16[256,512]{1,0:T(8,128)(2,1)}, bf16[256,512]{1,0:T(8,128)(2,1)S(1)}, u32[]{:S(2)}, u32[]{:S(2)}) collective-permute-start(bf16[256,512]{1,0:T(8,128)(2,1)} %get-tuple-element.41._), channel_id=1, source_target_pairs={{0,2},{1,3},{2,4},{3,5},{4,6},{5,7},{6,0},{7,1},{8,10},{9,11},{10,... | collective-permute-start | bytes 786440 | tf_op jit(solution)/shard_map/ppermute | solution.py:488
  60.9 12.3 %collective-permute-start.12 = (bf16[256,512]{1,0:T(8,128)(2,1)S(1)}, bf16[256,512]{1,0:T(8,128)(2,1)S(1)}, u32[]{:S(2)}, u32[]{:S(2)}) collective-permute-start(bf16[256,512]{1,0:T(8,128)(2,1)S(1)} %get-tuple-element.42), channel_id=1, source_target_pairs={{0,6},{1,7},{2,0},{3,1},{4,2},{5,3},{6,4},{7,5},{8,14},{9,15},{10,... | collective-permute-start | bytes 786440 | tf_op jit(solution)/shard_map/ppermute | solution.py:488
  63.5 11.3 %collective-permute-start.14 = (bf16[256,512]{1,0:T(8,128)(2,1)}, bf16[256,512]{1,0:T(8,128)(2,1)S(1)}, u32[]{:S(2)}, u32[]{:S(2)}) collective-permute-start(bf16[256,512]{1,0:T(8,128)(2,1)} %get-tuple-element.46), channel_id=1, source_target_pairs={{0,2},{1,3},{2,4},{3,5},{4,6},{5,7},{6,0},{7,1},{8,10},{9,11},{10,... | collective-permute-start | bytes 786440 | tf_op jit(solution)/shard_map/ppermute | solution.py:488
  63.9 10.9 %collective-permute-start.15 = (bf16[256,512]{1,0:T(8,128)(2,1)}, bf16[256,512]{1,0:T(8,128)(2,1)S(1)}, u32[]{:S(2)}, u32[]{:S(2)}) collective-permute-start(bf16[256,512]{1,0:T(8,128)(2,1)} %get-tuple-element.47), channel_id=1, source_target_pairs={{0,6},{1,7},{2,0},{3,1},{4,2},{5,3},{6,4},{7,5},{8,14},{9,15},{10,... | collective-permute-start | bytes 786440 | tf_op jit(solution)/shard_map/ppermute | solution.py:488
  73.1 1.7 %collective-permute-start.13 = (bf16[4,16,512]{2,1,0:T(8,128)(2,1)}, bf16[4,16,512]{2,1,0:T(8,128)(2,1)S(1)}, u32[]{:S(2)}, u32[]{:S(2)}) collective-permute-start(bf16[4,16,512]{2,1,0:T(8,128)(2,1)} %get-tuple-element.45), channel_id=1, source_target_pairs={{0,1},{1,0},{2,3},{3,2},{4,5},{5,4},{6,7},{7,6},{8,9},{9,8},{10,11... | collective-permute-start | bytes 196616 | tf_op jit(solution)/shard_map/ppermute | solution.py:493
  74.8 0.8 copy-start.2
  75.8 11.4 %collective-permute-start.16 = (bf16[272,512]{1,0:T(8,128)(2,1)S(1)}, bf16[272,512]{1,0:T(8,128)(2,1)S(1)}, u32[]{:S(2)}, u32[]{:S(2)}) collective-permute-start(bf16[272,512]{1,0:T(8,128)(2,1)S(1)} %get-tuple-element.48), channel_id=1, source_target_pairs={{0,2},{1,3},{2,4},{3,5},{4,6},{5,7},{6,0},{7,1},{8,10},{9,11},{10,... | collective-permute-start | bytes 835592 | tf_op jit(solution)/shard_map/ppermute | solution.py:488
  77.2 9.9 %collective-permute-start.17 = (bf16[272,512]{1,0:T(8,128)(2,1)S(1)}, bf16[272,512]{1,0:T(8,128)(2,1)S(1)}, u32[]{:S(2)}, u32[]{:S(2)}) collective-permute-start(bf16[272,512]{1,0:T(8,128)(2,1)S(1)} %get-tuple-element.49), channel_id=1, source_target_pairs={{0,6},{1,7},{2,0},{3,1},{4,2},{5,3},{6,4},{7,5},{8,14},{9,15},{10,... | collective-permute-start | bytes 835592 | tf_op jit(solution)/shard_map/ppermute | solution.py:488
  79.1 8.1 %collective-permute-start.18 = (bf16[16,512]{1,0:T(8,128)(2,1)S(1)}, bf16[16,512]{1,0:T(8,128)(2,1)S(1)}, u32[]{:S(2)}, u32[]{:S(2)}) collective-permute-start(bf16[16,512]{1,0:T(8,128)(2,1)S(1)} %get-tuple-element.51), channel_id=1, source_target_pairs={{0,4},{1,5},{2,6},{3,7},{4,0},{5,1},{6,2},{7,3},{8,12},{9,13},{10,... | collective-permute-start | bytes 49160 | tf_op jit(solution)/shard_map/ppermute | solution.py:488
